TPU v7x, 128 devices: a whole 4x4x4 slice. The times are simulated.
128 devices in a mesh: section: 2 (over x_lo), shard: 4 (over x_hi, core), replica: 16 (over z, y).
Axes of the slice: x: 4 (x_hi: 2, x_lo: 2; x = x_hi * 2 + x_lo), y: 4, z: 4, core: 2. Of those that a mesh axis runs over, the one named last changes fastest.
Arguments:
- tokens: bfloat16 [2, 4, 1024, 1088], P(None, 'shard', 'replica'), may hold values from -6 to 6
- cotangent: bfloat16 [2, 4, 1024, 1088], P(None, 'shard', 'replica'), may hold values from -6 to 6
- doc_ids: int32 [2, 4, 1024], P(None, 'shard', 'replica'), may hold values from 0 to 2, as said below
- gains: float32 [2, 2, 1088], P('section'), may hold values from 0.5 to 1.5
- biases: float32 [2, 6, 1088], P('section'), may hold values from -1.8 to 1.8
- up_bias: float32 [2, 4352], P('section'), may hold values from -1.8 to 1.8
- w_qkv: bfloat16 [2, 1088, 3264], P('section', 'shard'), may hold values from -0.1875 to 0.1875
- w_out: bfloat16 [2, 1088, 1088], P('section', 'shard'), may hold values from -1.5 to 1.5
- w_up: bfloat16 [2, 1088, 4352], P('section', 'shard'), may hold values from -0.1875 to 0.1875
- w_down: bfloat16 [2, 4352, 1088], P('section', 'shard'), may hold values from -0.09375 to 0.09375
Outputs:
- layer_out: bfloat16 [2, 2, 4, 1024, 1088], P('section', None, 'shard', 'replica')
- input_grad: bfloat16 [2, 2, 4, 1024, 1088], P('section', None, 'shard', 'replica')
- gains_grad: float32 [2, 2, 1088], P('section')
- biases_grad: float32 [2, 6, 1088], P('section')
- up_bias_grad: float32 [2, 4352], P('section')
- w_qkv_grad: float32 [2, 1088, 3264], P('section', 'shard')
- w_out_grad: float32 [2, 1088, 1088], P('section', 'shard')
- w_up_grad: float32 [2, 1088, 4352], P('section', 'shard')
- w_down_grad: float32 [2, 4352, 1088], P('section', 'shard')
Inputs may be any that keep to these rules, and one draw needn't show every extreme that they name: `doc_ids`: within each sequence the numbers never fall; 0 covers the first 1 to 32 positions, 2 the last 1 to 32 positions, 1 all the others.
All inputs are finite; a program needn't handle non-finite values.
Results may differ from a plain program's by a relative error of at most 0.028.
Values may be sent and summed in bfloat16 or wider, within the bound.
A program may use at most 192 MiB of HBM per device.

v0:
```python
from functools import partial

import jax
import jax.numpy as jnp
from jax import lax
from jax.sharding import PartitionSpec as P

H = 17
HD = 64


epsilon = 1e-05
masked_score = -1e30


def as_sent(value):
    return jax.tree.map(lambda a: a.astype(jnp.bfloat16) if a.dtype == jnp.float32 else a, value)


def passed_along(block, axis, distance):
    devices = range(lax.axis_size(axis))
    route = [(i - distance, i) for i in devices if i - distance in devices]
    return lax.ppermute(block, axis, route)


def layer_norm(values, gain_row, shift_row):
    centre = values - jnp.mean(values, axis=-1, keepdims=True)
    inverse = lax.rsqrt(jnp.mean(centre * centre, axis=-1, keepdims=True) + epsilon)
    normed = centre * inverse
    return (normed * gain_row + shift_row, normed, inverse)


def norm_back(grad_normed_out, normed, inverse, gain_row):
    scaled = grad_normed_out * gain_row
    middle = jnp.mean(scaled, axis=-1, keepdims=True)
    slope = jnp.mean(scaled * normed, axis=-1, keepdims=True)
    return inverse * (scaled - middle - normed * slope)


def split_heads(matrix):
    return matrix.reshape(matrix.shape[0], H, HD)


def score_block(query_rows, key_rows, allowed):
    raw_scores = jnp.einsum(
        "qhd,khd->hqk",
        split_heads(query_rows),
        split_heads(key_rows),
        preferred_element_type=jnp.float32,
    )
    return jnp.where(allowed[None], raw_scores * HD ** (-0.5), masked_score)


def times_transposed(left, right):
    return lax.dot_general(
        left, right, (((1,), (1,)), ((), ())), preferred_element_type=jnp.float32
    )


def outer_sum(left, right):
    return lax.dot_general(
        left, right, (((0,), (0,)), ((), ())), preferred_element_type=jnp.float32
    )


def select_tree(flag, when_true, when_false):
    return jax.tree.map(partial(jnp.where, flag), when_true, when_false)


def layer_forward(inputs, allowed, gain_rows, bias_rows, up_shift, weights):
    w_qkv, w_out, w_up, w_down = weights
    row_count, model_width = inputs.shape
    normed_in, normed_first, inverse_first = layer_norm(inputs, gain_rows[0], bias_rows[0])
    act_first = normed_in.astype(jnp.bfloat16)
    mixed_out = jnp.dot(act_first, w_qkv, preferred_element_type=jnp.float32)
    query_local = (mixed_out[:, :model_width] + bias_rows[1]).astype(jnp.bfloat16)
    key_local = mixed_out[:, model_width : 2 * model_width].astype(jnp.bfloat16)
    value_local = (mixed_out[:, 2 * model_width :] + bias_rows[2]).astype(jnp.bfloat16)
    key_all, value_all = (
        lax.all_gather(key_local, "replica", axis=0, tiled=True),
        lax.all_gather(value_local, "replica", axis=0, tiled=True),
    )
    scores = score_block(query_local, key_all, allowed)
    largest = jnp.max(scores, axis=-1, keepdims=True)
    exponent = jnp.exp(scores - largest)
    summed = jnp.sum(exponent, axis=-1, keepdims=True)
    attention = (exponent / summed).astype(jnp.bfloat16)
    log_total = largest + jnp.log(summed)
    head_out = jnp.einsum(
        "hqk,khd->qhd", attention, split_heads(value_all), preferred_element_type=jnp.float32
    )
    attended = head_out.reshape(row_count, model_width).astype(jnp.bfloat16)
    residual = inputs + jnp.dot(attended, w_out, preferred_element_type=jnp.float32) + bias_rows[3]
    normed_mid, normed_second, inverse_second = layer_norm(residual, gain_rows[1], bias_rows[4])
    act_second = normed_mid.astype(jnp.bfloat16)
    hidden_pre = jnp.dot(act_second, w_up, preferred_element_type=jnp.float32) + up_shift
    hidden = jax.nn.gelu(hidden_pre, approximate=True).astype(jnp.bfloat16)
    result = residual + jnp.dot(hidden, w_down, preferred_element_type=jnp.float32) + bias_rows[5]
    kept = {
        "normed_first": normed_first,
        "inverse_first": inverse_first,
        "act_first": act_first,
        "query_local": query_local,
        "key_local": key_local,
        "value_local": value_local,
        "key_all": key_all,
        "value_all": value_all,
        "log_total": log_total,
        "attended": attended,
        "normed_second": normed_second,
        "inverse_second": inverse_second,
        "act_second": act_second,
        "hidden_pre": hidden_pre,
        "hidden": hidden,
    }
    return (result, kept)


def layer_backward(grad_out, kept, allowed, gain_rows, weights):
    w_qkv, w_out, w_up, w_down = weights
    row_count, model_width = grad_out.shape
    grad_down = grad_out.astype(jnp.bfloat16)
    grad_hidden = times_transposed(grad_down, w_down)
    gelu_value, gelu_pull = jax.vjp(partial(jax.nn.gelu, approximate=True), kept["hidden_pre"])
    grad_pre = gelu_pull(grad_hidden)[0].astype(jnp.bfloat16)
    grad_second = times_transposed(grad_pre, w_up)
    grad_resid = grad_out + norm_back(
        grad_second, kept["normed_second"], kept["inverse_second"], gain_rows[1]
    )
    grad_branch = grad_resid.astype(jnp.bfloat16)
    grad_heads = times_transposed(grad_branch, w_out).astype(jnp.bfloat16)
    key_all, value_all = (
        lax.all_gather(as_sent(kept["key_local"]), "replica", axis=0, tiled=True),
        lax.all_gather(as_sent(kept["value_local"]), "replica", axis=0, tiled=True),
    )
    scores = score_block(kept["query_local"], key_all, allowed)
    soft = jnp.exp(scores - kept["log_total"])
    grad_soft = jnp.einsum(
        "qhd,khd->hqk",
        split_heads(grad_heads),
        split_heads(value_all),
        preferred_element_type=jnp.float32,
    )
    along = jnp.sum(soft * grad_soft, axis=-1, keepdims=True)
    grad_scores = (soft * (grad_soft - along)).astype(jnp.bfloat16)
    scale_factor = HD ** (-0.5)
    grad_query = jnp.einsum(
        "hqk,khd->qhd", grad_scores, split_heads(key_all), preferred_element_type=jnp.float32
    )
    grad_query = grad_query.reshape(row_count, model_width) * scale_factor
    key_term = jnp.einsum(
        "hqk,qhd->khd",
        grad_scores,
        split_heads(kept["query_local"]),
        preferred_element_type=jnp.float32,
    )
    key_term = key_term.reshape(-1, model_width) * scale_factor
    value_term = jnp.einsum(
        "hqk,qhd->khd",
        soft.astype(jnp.bfloat16),
        split_heads(grad_heads),
        preferred_element_type=jnp.float32,
    )
    value_term = value_term.reshape(-1, model_width)
    grad_key, grad_value = (
        lax.psum_scatter(
            key_term.astype(jnp.bfloat16), "replica", scatter_dimension=0, tiled=True
        ).astype(jnp.float32),
        lax.psum_scatter(
            value_term.astype(jnp.bfloat16), "replica", scatter_dimension=0, tiled=True
        ).astype(jnp.float32),
    )
    grad_mixed = jnp.concatenate([grad_query, grad_key, grad_value], axis=1).astype(jnp.bfloat16)
    grad_first = times_transposed(grad_mixed, w_qkv)
    grad_in = grad_resid + norm_back(
        grad_first, kept["normed_first"], kept["inverse_first"], gain_rows[0]
    )
    record = {
        "grad_down": grad_down,
        "grad_pre": grad_pre,
        "grad_branch": grad_branch,
        "grad_mixed": grad_mixed,
        "grad_first": grad_first,
        "grad_second": grad_second,
    }
    return (grad_in, record)


def stacked(members, entry_name):
    return jnp.concatenate([member[entry_name] for member in members], axis=0)


def weight_terms(caches, records):
    return (
        outer_sum(stacked(caches, "act_first"), stacked(records, "grad_mixed")),
        outer_sum(stacked(caches, "attended"), stacked(records, "grad_branch")),
        outer_sum(stacked(caches, "act_second"), stacked(records, "grad_pre")),
        outer_sum(stacked(caches, "hidden"), stacked(records, "grad_down")),
    )


def small_terms(caches, records, model_width):
    grad_first = stacked(records, "grad_first")
    grad_second = stacked(records, "grad_second")
    grad_mixed = stacked(records, "grad_mixed").astype(jnp.float32)
    gain_grad = jnp.stack(
        [
            jnp.sum(grad_first * stacked(caches, "normed_first"), axis=0),
            jnp.sum(grad_second * stacked(caches, "normed_second"), axis=0),
        ]
    )
    bias_grad = jnp.stack(
        [
            jnp.sum(grad_first, axis=0),
            jnp.sum(grad_mixed[:, :model_width], axis=0),
            jnp.sum(grad_mixed[:, 2 * model_width :], axis=0),
            jnp.sum(stacked(records, "grad_branch").astype(jnp.float32), axis=0),
            jnp.sum(grad_second, axis=0),
            jnp.sum(stacked(records, "grad_down").astype(jnp.float32), axis=0),
        ]
    )
    up_grad = jnp.sum(stacked(records, "grad_pre").astype(jnp.float32), axis=0)
    return (gain_grad, bias_grad, up_grad)


def shards(tokens, cotangent, doc_ids, gains, biases, up_bias, w_qkv, w_out, w_up, w_down):
    micro = tokens.shape[0]
    row_count = tokens.shape[2]
    model_width = tokens.shape[3]
    replicas = lax.axis_size("replica")
    is_first = lax.axis_index("section") == 0
    gathered = (
        lax.all_gather(w_qkv, "shard", axis=1, tiled=True),
        lax.all_gather(w_out, "shard", axis=1, tiled=True),
        lax.all_gather(w_up, "shard", axis=1, tiled=True),
        lax.all_gather(w_down, "shard", axis=1, tiled=True),
    )
    weights = tuple((member[0] for member in gathered))
    gain_rows = gains[0]
    bias_rows = biases[0]
    up_shift = up_bias[0]
    key_docs = lax.all_gather(doc_ids, "replica", axis=2, tiled=True)
    query_pos = lax.axis_index("replica") * row_count + jnp.arange(row_count, dtype=jnp.int32)
    key_pos = jnp.arange(row_count * replicas, dtype=jnp.int32)
    causal = key_pos[None, :] <= query_pos[:, None]
    masks = [
        causal & (doc_ids[micro_index, 0][:, None] == key_docs[micro_index, 0][None, :])
        for micro_index in range(micro)
    ]
    inbox = jnp.zeros((row_count, model_width), jnp.bfloat16)
    outputs = []
    forward_kept = []
    for step_index in range(micro + 1):
        ahead = min(step_index, micro - 1)
        behind = max(step_index - 1, 0)
        inputs = jnp.where(is_first, tokens[ahead, 0], inbox).astype(jnp.float32)
        allowed = jnp.where(is_first, masks[ahead], masks[behind])
        result, kept = layer_forward(inputs, allowed, gain_rows, bias_rows, up_shift, weights)
        sent = result.astype(jnp.bfloat16)
        if step_index < micro:
            inbox = passed_along(sent, "section", 1)
        outputs.append(sent)
        forward_kept.append(kept)
    caches = [
        select_tree(is_first, forward_kept[micro_index], forward_kept[micro_index + 1])
        for micro_index in range(micro)
    ]
    inbox = jnp.zeros((row_count, model_width), jnp.bfloat16)
    grads_sent = []
    backward_kept = []
    for step_index in range(micro + 1):
        ahead = min(step_index, micro - 1)
        behind = max(step_index - 1, 0)
        grad_out = jnp.where(is_first, inbox, cotangent[ahead, 0]).astype(jnp.float32)
        kept = select_tree(is_first, caches[behind], caches[ahead])
        allowed = jnp.where(is_first, masks[behind], masks[ahead])
        grad_in, record = layer_backward(grad_out, kept, allowed, gain_rows, weights)
        sent = grad_in.astype(jnp.bfloat16)
        if step_index < micro:
            inbox = passed_along(sent, "section", -1)
        grads_sent.append(sent)
        backward_kept.append(record)
    records = [
        select_tree(is_first, backward_kept[micro_index + 1], backward_kept[micro_index])
        for micro_index in range(micro)
    ]
    shard_grads = jax.tree.map(
        lambda part: part.astype(jnp.float32),
        lax.psum_scatter(
            as_sent(weight_terms(caches, records)), "shard", scatter_dimension=0, tiled=True
        ),
    )
    summed = (
        lax.psum(shard_grads[0].astype(jnp.bfloat16), "replica").astype(jnp.float32),
        lax.psum(shard_grads[1].astype(jnp.bfloat16), "replica").astype(jnp.float32),
        lax.psum(shard_grads[2].astype(jnp.bfloat16), "replica").astype(jnp.float32),
        lax.psum(shard_grads[3].astype(jnp.bfloat16), "replica").astype(jnp.float32),
    )
    small = lax.psum(small_terms(caches, records, model_width), ("shard", "replica"))
    layer_out = jnp.stack(
        [
            jnp.where(is_first, outputs[micro_index], outputs[micro_index + 1])
            for micro_index in range(micro)
        ]
    )
    input_grad = jnp.stack(
        [
            jnp.where(is_first, grads_sent[micro_index + 1], grads_sent[micro_index])
            for micro_index in range(micro)
        ]
    )
    return (
        layer_out[None, :, None],
        input_grad[None, :, None],
        small[0][None],
        small[1][None],
        small[2][None],
        summed[0][None],
        summed[1][None],
        summed[2][None],
        summed[3][None],
    )


def solution(mesh):
    placed = (
        P(None, "shard", "replica", None),
        P(None, "shard", "replica", None),
        P(None, "shard", "replica"),
        P("section", None, None),
        P("section", None, None),
        P("section", None),
        P("section", "shard", None),
        P("section", "shard", None),
        P("section", "shard", None),
        P("section", "shard", None),
    )
    return jax.shard_map(
        shards,
        mesh=mesh,
        in_specs=placed,
        out_specs=(
            P("section", None, "shard", "replica", None),
            P("section", None, "shard", "replica", None),
            P("section", None, None),
            P("section", None, None),
            P("section", None),
            P("section", "shard", None),
            P("section", "shard", None),
            P("section", "shard", None),
            P("section", "shard", None),
        ),
        check_vma=False,
    )
```

profile of v0, /device:TPU:0, one launch (start us, length us, event | category | flops | bytes accessed | tf_op | source)
XLA Modules:
  0.0 2002.5 jit_solution(6015183817905108311)
XLA Ops:
  12.5 55.5 %all-gather.17.cloned.1.call-done = bf16[1,1088,3264]{2,1,0:T(8,128)(2,1)} async-done(((bf16[1,272,3264]{2,1,0:T(8,128)(2,1)}), bf16[1,1088,3264]{2,1,0:T(8,128)(2,1)}) %all-gather.17.cloned.1.call-update) | async-done | bytes 7102480 | tf_op jit(solution)/shard_map/all_gather | solution.py:233
  76.1 24.5 %all_gather.53 = s32[2,1,1024]{0,1,2:T(1,128)S(1)} all-gather(s32[2,1,64]{0,1,2:T(1,128)S(1)} %copy.117), channel_id=1, replica_groups=mesh['section'=2,'shard'=4,'replica'=16] {'replica'}, dimensions={2}, use_global_device_ids=true | all-gather | bytes 8704 | tf_op jit(solution)/shard_map/all_gather | solution.py:242
  100.6 38.3 %slice_reduce_fusion.2 = (s32[1024]{0:T(1024)S(1)}, s32[1024]{0:T(1024)S(1)}) fusion(s32[2,1,1024]{0,1,2:T(1,128)S(1)} %all_gather.53), kind=kLoop, calls=%fused_computation.214 | loop fusion | bytes 16384 | tf_op jit(solution)/shard_map/slice | solution.py:247
  143.1 23.8 %all-gather.19.cloned.1.call-done = bf16[1024,1088]{1,0:T(8,128)(2,1)} async-done(((bf16[64,1088]{1,0:T(8,128)(2,1)}), bf16[1024,1088]{1,0:T(8,128)(2,1)}) %all-gather.19.cloned.1.call-update) | async-done | bytes 2228240 | tf_op jit(solution)/shard_map/all_gather | solution.py:81
  199.2 66.8 %all-gather.25.cloned.1.call-done = bf16[1,1088,4352]{2,1,0:T(8,128)(2,1)} async-done(((bf16[1,272,4352]{2,1,0:T(8,128)(2,1)}), bf16[1,1088,4352]{2,1,0:T(8,128)(2,1)}) %all-gather.25.cloned.1.call-update) | async-done | bytes 9469968 | tf_op jit(solution)/shard_map/all_gather | solution.py:235
  272.4 66.2 %all-gather.27.cloned.1.call-done = bf16[1,4352,1088]{2,1,0:T(8,128)(2,1)} async-done(((bf16[1,1088,1088]{2,1,0:T(8,128)(2,1)}), bf16[1,4352,1088]{2,1,0:T(8,128)(2,1)}) %all-gather.27.cloned.1.call-update) | async-done | bytes 9469968 | tf_op jit(solution)/shard_map/all_gather | solution.py:236
  356.7 44.9 %all-gather.31.cloned.1.call-done = bf16[1024,1088]{1,0:T(8,128)(2,1)} async-done(((bf16[64,1088]{1,0:T(8,128)(2,1)}), bf16[1024,1088]{1,0:T(8,128)(2,1)}) %all-gather.31.cloned.1.call-update) | async-done | bytes 2228240 | tf_op jit(solution)/shard_map/all_gather | solution.py:80
  408.9 39.9 %all-gather.29.cloned.1.call-done = bf16[1024,1088]{1,0:T(8,128)(2,1)} async-done(((bf16[64,1088]{1,0:T(8,128)(2,1)}), bf16[1024,1088]{1,0:T(8,128)(2,1)}) %all-gather.29.cloned.1.call-update) | async-done | bytes 2228240 | tf_op jit(solution)/shard_map/all_gather | solution.py:81
  495.9 25.7 %all-gather.35.cloned.1.call-done = bf16[1024,1088]{1,0:T(8,128)(2,1)} async-done(((bf16[64,1088]{1,0:T(8,128)(2,1)}), bf16[1024,1088]{1,0:T(8,128)(2,1)}) %all-gather.35.cloned.1.call-update) | async-done | bytes 2228240 | tf_op jit(solution)/shard_map/all_gather | solution.py:80
  531.8 36.9 %all-gather.33.cloned.1.call-done = bf16[1024,1088]{1,0:T(8,128)(2,1)} async-done(((bf16[64,1088]{1,0:T(8,128)(2,1)}), bf16[1024,1088]{1,0:T(8,128)(2,1)}) %all-gather.33.cloned.1.call-update) | async-done | bytes 2228240 | tf_op jit(solution)/shard_map/all_gather | solution.py:81
  583.1 32.8 %all-gather.37.cloned.1.call-done = bf16[1024,1088]{1,0:T(8,128)(2,1)} async-done(((bf16[64,1088]{1,0:T(8,128)(2,1)}), bf16[1024,1088]{1,0:T(8,128)(2,1)}) %all-gather.37.cloned.1.call-update) | async-done | bytes 2228240 | tf_op jit(solution)/shard_map/all_gather | solution.py:133
  620.2 42.8 %all-gather.39.cloned.1.call-done = bf16[1024,1088]{1,0:T(8,128)(2,1)} async-done(((bf16[64,1088]{1,0:T(8,128)(2,1)}), bf16[1024,1088]{1,0:T(8,128)(2,1)}) %all-gather.39.cloned.1.call-update) | async-done | bytes 2228240 | tf_op jit(solution)/shard_map/all_gather | solution.py:134
  714.5 73.8 %reduce-scatter.31.cloned.1.call-done = bf16[64,1088]{1,0:T(8,128)(2,1)} async-done(((bf16[1024,1088]{1,0:T(8,128)(2,1)}), bf16[64,1088]{1,0:T(8,128)(2,1)}) %reduce-scatter.31.cloned.1.call-update) | async-done | bytes 139280
  790.1 76.1 %reduce-scatter.33.cloned.1.call-done = bf16[64,1088]{1,0:T(8,128)(2,1)} async-done(((bf16[1024,1088]{1,0:T(8,128)(2,1)}), bf16[64,1088]{1,0:T(8,128)(2,1)}) %reduce-scatter.33.cloned.1.call-update) | async-done | bytes 139280
  878.9 34.3 %all-gather.43.cloned.1.call-done = bf16[1024,1088]{1,0:T(8,128)(2,1)} async-done(((bf16[64,1088]{1,0:T(8,128)(2,1)}), bf16[1024,1088]{1,0:T(8,128)(2,1)}) %all-gather.43.cloned.1.call-update) | async-done | bytes 2228240 | tf_op jit(solution)/shard_map/all_gather | solution.py:134
  969.5 68.8 %reduce-scatter.35.cloned.1.call-done = bf16[64,1088]{1,0:T(8,128)(2,1)} async-done(((bf16[1024,1088]{1,0:T(8,128)(2,1)}), bf16[64,1088]{1,0:T(8,128)(2,1)}) %reduce-scatter.35.cloned.1.call-update) | async-done | bytes 139280
  1039.5 77.0 %reduce-scatter.37.cloned.1.call-done = bf16[64,1088]{1,0:T(8,128)(2,1)} async-done(((bf16[1024,1088]{1,0:T(8,128)(2,1)}), bf16[64,1088]{1,0:T(8,128)(2,1)}) %reduce-scatter.37.cloned.1.call-update) | async-done | bytes 139280
  1128.9 34.5 %all-gather.47.cloned.1.call-done = bf16[1024,1088]{1,0:T(8,128)(2,1)} async-done(((bf16[64,1088]{1,0:T(8,128)(2,1)}), bf16[1024,1088]{1,0:T(8,128)(2,1)}) %all-gather.47.cloned.1.call-update) | async-done | bytes 2228240 | tf_op jit(solution)/shard_map/all_gather | solution.py:134
  1212.2 58.3 %reduce-scatter.39.cloned.1.call-done = bf16[64,1088]{1,0:T(8,128)(2,1)} async-done(((bf16[1024,1088]{1,0:T(8,128)(2,1)}), bf16[64,1088]{1,0:T(8,128)(2,1)}) %reduce-scatter.39.cloned.1.call-update) | async-done | bytes 139280
  1271.6 77.0 %reduce-scatter.41.cloned.1.call-done = bf16[64,1088]{1,0:T(8,128)(2,1)} async-done(((bf16[1024,1088]{1,0:T(8,128)(2,1)}), bf16[64,1088]{1,0:T(8,128)(2,1)}) %reduce-scatter.41.cloned.1.call-update) | async-done | bytes 139280
  1391.9 73.9 %reduce-scatter.23.cloned.1.call-done = bf16[272,3264]{1,0:T(8,128)(2,1)} async-done(((bf16[1088,3264]{1,0:T(8,128)(2,1)}), bf16[272,3264]{1,0:T(8,128)(2,1)}) %reduce-scatter.23.cloned.1.call-update) | async-done | bytes 1775632 | tf_op jit(solution)/shard_map/reduce_scatter | solution.py:289
  1465.8 91.4 %reduce-scatter.29.cloned.1.call-done = bf16[1088,1088]{1,0:T(8,128)(2,1)} async-done(((bf16[4352,1088]{1,0:T(8,128)(2,1)}), bf16[1088,1088]{1,0:T(8,128)(2,1)}) %reduce-scatter.29.cloned.1.call-update) | async-done | bytes 2367504 | tf_op jit(solution)/shard_map/reduce_scatter | solution.py:289
  1557.2 87.6 %reduce-scatter.27.cloned.1.call-done = bf16[272,4352]{1,0:T(8,128)(2,1)} async-done(((bf16[1088,4352]{1,0:T(8,128)(2,1)}), bf16[272,4352]{1,0:T(8,128)(2,1)}) %reduce-scatter.27.cloned.1.call-update) | async-done | bytes 2367504 | tf_op jit(solution)/shard_map/reduce_scatter | solution.py:289
  1655.4 329.1 %all-reduce = (f32[1,2,1088]{2,1,0:T(2,128)}, f32[1,6,1088]{2,0,1:T(1,128)}, f32[1,4352]{1,0:T(1,128)}) all-reduce(f32[1,2,1088]{2,1,0:T(2,128)S(1)} %maximum_bitcast_fusion.2, f32[1,6,1088]{2,0,1:T(1,128)S(1)} %broadcast_in_dim.126, ...), channel_id=1, replica_groups=mesh['section'=2,'shard'=4,'replica'=16] {'shard','replica'}, use_global_device_ids=true, to_apply=%region_41.42 | all-reduce | flops 13056 | bytes 104448 | tf_op jit(solution)/shard_map/psum | solution.py:299
  (697 shorter events, 404.6 us)
Async XLA Ops:
  7.9 132.1 %all-gather.21.cloned.1.call-start = ((), (), s32[]{:S(2)}) async-start(), calls=%async_computation.12 | async-start | bytes 2506752 | tf_op jit(solution)/shard_map/all_gather | solution.py:80
  74.1 122.5 %all-gather.23.cloned.1.call-start = ((), (), s32[]{:S(2)}) async-start(), calls=%async_computation.13 | async-start | bytes 3133440 | tf_op jit(solution)/shard_map/all_gather | solution.py:234
  74.7 191.4 %all-gather.25.cloned.1.call-start = ((), (), s32[]{:S(2)}) async-start(), calls=%async_computation.14 | async-start | bytes 11837440 | tf_op jit(solution)/shard_map/all_gather | solution.py:235
  75.3 263.4 %all-gather.27.cloned.1.call-start = ((), (), s32[]{:S(2)}) async-start(), calls=%async_computation.15 | async-start | bytes 12533760 | tf_op jit(solution)/shard_map/all_gather | solution.py:236
  75.9 325.7 %all-gather.31.cloned.1.call-start = ((), (), s32[]{:S(2)}) async-start(), calls=%async_computation.17 | async-start | bytes 2506752 | tf_op jit(solution)/shard_map/all_gather | solution.py:80
  354.2 94.6 %all-gather.29.cloned.1.call-start = ((), (), s32[]{:S(2)}) async-start(), calls=%async_computation.16 | async-start | bytes 2506752 | tf_op jit(solution)/shard_map/all_gather | solution.py:81
  356.0 165.6 %all-gather.35.cloned.1.call-start = ((), (), s32[]{:S(2)}) async-start(), calls=%async_computation.19 | async-start | bytes 2506752 | tf_op jit(solution)/shard_map/all_gather | solution.py:80
  476.3 139.7 %all-gather.37.cloned.1.call-start = ((), (), s32[]{:S(2)}) async-start(), calls=%async_computation.20 | async-start | bytes 2506752 | tf_op jit(solution)/shard_map/all_gather | solution.py:133
  477.0 186.0 %all-gather.39.cloned.1.call-start = ((), (), s32[]{:S(2)}) async-start(), calls=%async_computation.21 | async-start | bytes 2506752 | tf_op jit(solution)/shard_map/all_gather | solution.py:134
  477.6 232.7 %all-gather.41.cloned.1.call-start = ((), (), s32[]{:S(2)}) async-start(), calls=%async_computation.22 | async-start | bytes 2506752 | tf_op jit(solution)/shard_map/all_gather | solution.py:133
  495.5 292.8 %reduce-scatter.31.cloned.1.call-start = ((), (), s32[]{:S(2)}) async-start(), calls=%async_computation.30 | async-start | bytes 2506752
  680.1 186.1 %reduce-scatter.33.cloned.1.call-start = ((), (), s32[]{:S(2)}) async-start(), calls=%async_computation.31 | async-start | bytes 2506752
  690.4 222.8 %all-gather.43.cloned.1.call-start = ((), (), s32[]{:S(2)}) async-start(), calls=%async_computation.23 | async-start | bytes 2506752 | tf_op jit(solution)/shard_map/all_gather | solution.py:134
  690.9 271.2 %all-gather.45.cloned.1.call-start = ((), (), s32[]{:S(2)}) async-start(), calls=%async_computation.24 | async-start | bytes 2506752 | tf_op jit(solution)/shard_map/all_gather | solution.py:133
  692.2 346.2 %reduce-scatter.35.cloned.1.call-start = ((), (), s32[]{:S(2)}) async-start(), calls=%async_computation.32 | async-start | bytes 2506752
  950.0 166.4 %reduce-scatter.37.cloned.1.call-start = ((), (), s32[]{:S(2)}) async-start(), calls=%async_computation.33 | async-start | bytes 2506752
  960.3 203.1 %all-gather.47.cloned.1.call-start = ((), (), s32[]{:S(2)}) async-start(), calls=%async_computation.25 | async-start | bytes 2506752 | tf_op jit(solution)/shard_map/all_gather | solution.py:134
  960.9 309.6 %reduce-scatter.39.cloned.1.call-start = ((), (), s32[]{:S(2)}) async-start(), calls=%async_computation.34 | async-start | bytes 2506752
  1196.1 152.6 %reduce-scatter.41.cloned.1.call-start = ((), (), s32[]{:S(2)}) async-start(), calls=%async_computation.35 | async-start | bytes 2506752
  1205.4 186.5 %reduce-scatter.25.cloned.1.call-start = ((), (), s32[]{:S(2)}) async-start(), calls=%async_computation.27 | async-start | bytes 3133440 | tf_op jit(solution)/shard_map/reduce_scatter | solution.py:289
  1208.9 257.0 %reduce-scatter.23.cloned.1.call-start = ((), (), s32[]{:S(2)}) async-start(), calls=%async_computation.26 | async-start | bytes 9052160 | tf_op jit(solution)/shard_map/reduce_scatter | solution.py:289
  1364.4 192.8 %reduce-scatter.29.cloned.1.call-start = ((), (), s32[]{:S(2)}) async-start(), calls=%async_computation.29 | async-start | bytes 12533760 | tf_op jit(solution)/shard_map/reduce_scatter | solution.py:289
  1373.2 271.6 %reduce-scatter.27.cloned.1.call-start = ((), (), s32[]{:S(2)}) async-start(), calls=%async_computation.28 | async-start | bytes 11837440 | tf_op jit(solution)/shard_map/reduce_scatter | solution.py:289
  1381.8 603.4 %all-reduce.4.cloned.1.call-start = ((), (), s32[]{:S(2)}) async-start(), calls=%async_computation.36 | async-start | bytes 14622720 | tf_op jit(solution)/shard_map/psum | solution.py:294
  (233 other events, 7015.4 us)
Sparse Core Ops, SparseCore 0:
  9.7 58.2 all-gather.16
  73.4 45.6 all-gather.20
  121.8 45.0 all-gather.18
  198.1 67.8 all-gather.24
  267.6 71.0 all-gather.26
  354.3 47.2 all-gather.30
  403.7 45.0 all-gather.28
  475.8 45.7 all-gather.34
  523.6 45.0 all-gather.32
  570.8 45.0 all-gather.36
  617.9 45.0 all-gather.38
  665.2 45.0 all-gather.40
  714.0 74.2 reduce-scatter.30
  792.0 74.1 reduce-scatter.32
  868.2 44.9 all-gather.42
  915.2 45.0 all-gather.44
  964.0 74.2 reduce-scatter.34
  1042.2 74.1 reduce-scatter.36
  1196.2 74.2 reduce-scatter.38
  1274.4 74.2 reduce-scatter.40
  1394.6 71.1 reduce-scatter.22
  1468.5 88.6 reduce-scatter.28
  1559.8 84.9 reduce-scatter.26
  1648.6 132.8 all-reduce.3
  (3 shorter events, 112.9 us)
where the time goes:
time: 2020 us; the launch traced here: 2000 us
  waiting for transfers between devices  1240 us (61%)
  blocking collectives  354 us (18%)
  matrix products  193 us (10%)
  local copies, waits for them, and re-layouts  147 us (7%)
  other arithmetic  42.5 us (2%)
    unnamed x33, waiting for transfers between devices  436 us
    psum x1, blocking collectives, shards(): lax.psum(small_terms(caches, records, model_width), ('shard', 'replica'))  329 us
    reduce_scatter x4, waiting for transfers between devices, shards(): lax.psum_scatter(as_sent(weight_terms(caches, records)), 'shard', scatter...  263 us
    all_gather x3, waiting for transfers between devices, layer_backward(): lax.all_gather(as_sent(kept['value_local']), 'replica', axis=0, tiled=True)  112 us
    all_gather x3, waiting for transfers between devices, layer_forward(): lax.all_gather(value_local, 'replica', axis=0, tiled=True)  101 us
    all_gather x3, waiting for transfers between devices, layer_forward(): lax.all_gather(key_local, 'replica', axis=0, tiled=True)  70.6 us
    all_gather x1, waiting for transfers between devices, shards(): lax.all_gather(w_up, 'shard', axis=1, tiled=True)  66.8 us
    all_gather x1, waiting for transfers between devices, shards(): lax.all_gather(w_down, 'shard', axis=1, tiled=True)  66.2 us
  transfers between devices with their start and end apart: 31, of which 26 were waited for; matrix products, arithmetic and copies ran while one was open for 15% of the time, Pallas kernels for 0%

commit v1 on v0

v1 whole, which is shorter than its diff:
```python
import functools

import jax
import jax.numpy as jnp
from jax import lax
from jax.experimental import pallas as pl
from jax.experimental.pallas import tpu as pltpu
from jax.sharding import PartitionSpec as P

MESH = pl.DeviceIdType.MESH
H = 17
HD = 64
TQ = 64
SEQ = 1024
NR = 16
D = 1088
FF = 4352
SCALE = HD ** (-0.5)
epsilon = 1e-05
masked_score = -1e30
BQ = 256
PIECE = 896
RED_ROWS = 288
HALF = 144


def layer_norm(values, gain_row, shift_row):
    centre = values - jnp.mean(values, axis=-1, keepdims=True)
    inverse = lax.rsqrt(jnp.mean(centre * centre, axis=-1, keepdims=True) + epsilon)
    normed = centre * inverse
    return (normed * gain_row + shift_row, normed, inverse)


def norm_back(grad_normed_out, normed, inverse, gain_row):
    scaled = grad_normed_out * gain_row
    middle = jnp.mean(scaled, axis=-1, keepdims=True)
    slope = jnp.mean(scaled * normed, axis=-1, keepdims=True)
    return inverse * (scaled - middle - normed * slope)


def times(left, right):
    return jnp.dot(left, right, preferred_element_type=jnp.float32)


def times_transposed(left, right):
    return lax.dot_general(
        left, right, (((1,), (1,)), ((), ())), preferred_element_type=jnp.float32
    )


def outer_sum(left, right):
    return lax.dot_general(
        left, right, (((0,), (0,)), ((), ())), preferred_element_type=jnp.float32
    )


def y_peer(me, d):
    return (me // 4) * 4 + lax.rem(lax.rem(me, 4) + d, 4)


def z_peer(me, d):
    return lax.rem(me + 4 * d, NR)


def any_peer(me, d):
    return lax.rem(me // 4 + d // 4, 4) * 4 + lax.rem(lax.rem(me, 4) + d % 4, 4)


def remote(src, dst, send, recv, where):
    return pltpu.make_async_remote_copy(
        src_ref=src,
        dst_ref=dst,
        send_sem=send,
        recv_sem=recv,
        device_id=where,
        device_id_type=MESH,
    )


def greet(places):
    barrier = pltpu.get_barrier_semaphore()
    for where in places:
        pl.semaphore_signal(barrier, inc=1, device_id=where, device_id_type=MESH)
    pl.semaphore_wait(barrier, len(places))


def swap_kernel(x, o, send, recv, local):
    me = lax.axis_index("replica")
    greet([{"replica": any_peer(me, d)} for d in range(1, NR)])
    copies = []
    for d in range(1, NR):
        to = any_peer(me, d)
        copy = remote(x.at[to], o.at[me], send.at[d], recv.at[d], {"replica": to})
        copy.start()
        copies.append(copy)
    own = pltpu.make_async_copy(x.at[me], o.at[me], local)
    own.start()
    own.wait()
    for copy in copies:
        copy.wait()


def swap(x, collective_id):
    return pl.pallas_call(
        swap_kernel,
        out_shape=jax.ShapeDtypeStruct(x.shape, x.dtype),
        in_specs=[pl.BlockSpec(memory_space=pl.ANY)],
        out_specs=pl.BlockSpec(memory_space=pl.ANY),
        scratch_shapes=[
            pltpu.SemaphoreType.DMA((NR,)),
            pltpu.SemaphoreType.DMA((NR,)),
            pltpu.SemaphoreType.DMA,
        ],
        compiler_params=pltpu.CompilerParams(collective_id=collective_id, has_side_effects=True),
        name="swap",
    )(x)


W_SHAPES = ((272, 3264), (272, 1088), (272, 4352), (1088, 1088))
W_CUTS = (1664, 512, 2176, 512)


def weights_kernel(*refs):
    ins, outs = refs[:4], refs[4:8]
    (own_s, own_r, local, xp_s, xp_r, xd_s, xd_r, a1_s, a1_r, b1_s, b1_r, a2_s, a2_r, b2_s, b2_r, f_s, f_r) = refs[8:]
    j = lax.axis_index("shard")
    me = lax.axis_index("replica")
    z, y = me // 4, lax.rem(me, 4)
    xj = lax.rem(j + 2, 4)
    cj = j + 1 - 2 * lax.rem(j, 2)
    x_place, c_place = {"shard": xj}, {"shard": cj}
    y_places = [{"replica": y_peer(me, d)} for d in (1, 2, 3)]
    z_places = [{"replica": z_peer(me, d)} for d in (1, 2, 3)]
    greet([x_place, c_place] + y_places + z_places)

    def rows(start, count):
        return pl.ds(pl.multiple_of(start, 16), count)

    waits = []
    x_pieces, x_directs = [], []
    for a, (r, n) in enumerate(W_SHAPES):
        u = r // 17
        piece = remote(ins[a].at[rows(me * u, u)], outs[a].at[rows(j * r + me * u, u)], xp_s.at[a], xp_r.at[a], x_place)
        piece.start()
        x_pieces.append(piece)
    for a, (r, n) in enumerate(W_SHAPES):
        u = r // 17
        direct = remote(ins[a].at[rows(16 * u, u)], outs[a].at[rows(j * r + 16 * u, u)], xd_s.at[a], xd_r.at[a], x_place)
        direct.start()
        x_directs.append(direct)
    for a, (r, n) in enumerate(W_SHAPES):
        copy = remote(ins[a], outs[a].at[rows(j * r, r)], own_s.at[a], own_r.at[a], c_place)
        copy.start()
        waits.append(copy)
        copy = pltpu.make_async_copy(ins[a], outs[a].at[rows(j * r, r)], local.at[a])
        copy.start()
        waits.append(copy)
    firsts = []
    for a, (r, n) in enumerate(W_SHAPES):
        u, cut = r // 17, W_CUTS[a]
        x_pieces[a].wait()
        here = rows(xj * r + me * u, u)
        part_a = outs[a].at[here, pl.ds(0, cut)]
        part_b = outs[a].at[here, pl.ds(cut, n - cut)]
        group = []
        for i in range(3):
            group.append(remote(part_a, part_a, a1_s.at[a, i], a1_r.at[a, i], y_places[i]))
            group.append(remote(part_b, part_b, b1_s.at[a, i], b1_r.at[a, i], z_places[i]))
        for copy in group:
            copy.start()
        firsts.append(group)
    seconds = []
    for a, (r, n) in enumerate(W_SHAPES):
        u, cut = r // 17, W_CUTS[a]
        for copy in firsts[a]:
            copy.wait()
        part_a = outs[a].at[rows(xj * r + z * (4 * u), 4 * u), pl.ds(0, cut)]
        group = []
        for i in range(3):
            group.append(remote(part_a, part_a, a2_s.at[a, i], a2_r.at[a, i], z_places[i]))
            for k in range(4):
                part_b = outs[a].at[rows(xj * r + (4 * k + y) * u, u), pl.ds(cut, n - cut)]
                group.append(remote(part_b, part_b, b2_s.at[a, i, k], b2_r.at[a, i, k], y_places[i]))
        for copy in group:
            copy.start()
        seconds.append(group)
    for a, (r, n) in enumerate(W_SHAPES):
        for copy in seconds[a]:
            copy.wait()
        x_directs[a].wait()
        whole = outs[a].at[rows(xj * r, r)]
        copy = remote(whole, whole, f_s.at[a], f_r.at[a], c_place)
        copy.start()
        waits.append(copy)
    for copy in waits:
        copy.wait()


def gather_weights(weights):
    dma = pltpu.SemaphoreType.DMA
    return pl.pallas_call(
        weights_kernel,
        out_shape=[jax.ShapeDtypeStruct((4 * r, n), jnp.bfloat16) for r, n in W_SHAPES],
        in_specs=[pl.BlockSpec(memory_space=pl.ANY)] * 4,
        out_specs=[pl.BlockSpec(memory_space=pl.ANY)] * 4,
        scratch_shapes=[dma((4,))] * 7 + [dma((4, 3))] * 6 + [dma((4, 3, 4))] * 2 + [dma((4,))] * 2,
        compiler_params=pltpu.CompilerParams(collective_id=1, has_side_effects=True),
        name="gather_weights",
    )(*weights)


def total_kernel(
    g, out, own_a, own_b, buf_a, buf_b, sum_a, sum_b, got_a, got_b,
    loc, r1a_s, r1a_r, r1b_s, r1b_r, r2a_s, r2a_r, r2b_s, r2b_r, g1a_s, g1a_r, g1b_s, g1b_r, g2a_s, g2a_r, g2b_s, g2b_r, fin,
):
    me = lax.axis_index("replica")
    z, y = me // 4, lax.rem(me, 4)
    y_ids = [y_peer(me, d) for d in (1, 2, 3)]
    z_ids = [z_peer(me, d) for d in (1, 2, 3)]
    y_places = [{"replica": p} for p in y_ids]
    z_places = [{"replica": p} for p in z_ids]
    greet(y_places + z_places)
    rows_a, rows_b = pl.ds(0, HALF), pl.ds(HALF, HALF)

    def columns(piece, count=1):
        return pl.ds(pl.multiple_of(piece * PIECE, 128), count * PIECE)

    def start(copies):
        for copy in copies:
            copy.start()

    def finish(copies):
        for copy in copies:
            copy.wait()

    locals_ = [
        pltpu.make_async_copy(g.at[rows_a, columns(4 * k + y)], own_a.at[k], loc.at[k])
        for k in range(4)
    ] + [pltpu.make_async_copy(g.at[rows_b, columns(4 * z, 4)], own_b, loc.at[4])]
    start(locals_)
    one_a, one_b = [], []
    for i in range(3):
        ty, tz = lax.rem(y + 1 + i, 4), lax.rem(z + 1 + i, 4)
        one_b.append(remote(g.at[rows_b, columns(4 * tz, 4)], buf_b.at[i], r1b_s.at[i], r1b_r.at[i], z_places[i]))
        for k in range(4):
            one_a.append(remote(g.at[rows_a, columns(4 * k + ty)], buf_a.at[i, k], r1a_s.at[i, k], r1a_r.at[i, k], y_places[i]))
    start(one_a)
    start(one_b)
    finish(locals_)
    finish(one_a)
    f32 = jnp.float32
    for k in range(4):
        total = own_a[k].astype(f32) + buf_a[0, k].astype(f32)
        total = total + buf_a[1, k].astype(f32) + buf_a[2, k].astype(f32)
        sum_a[k] = total.astype(jnp.bfloat16)
    two_a = []
    for i in range(3):
        tz = lax.rem(z + 1 + i, 4)
        two_a.append(remote(sum_a.at[tz], got_a.at[i], r2a_s.at[i], r2a_r.at[i], z_places[i]))
    start(two_a)
    finish(one_b)
    for k in range(4):
        part = pl.ds(k * PIECE, PIECE)
        total = own_b[:, part].astype(f32) + buf_b[0, :, part].astype(f32)
        total = total + buf_b[1, :, part].astype(f32) + buf_b[2, :, part].astype(f32)
        sum_b[k] = total.astype(jnp.bfloat16)
    two_b = []
    for i in range(3):
        ty = lax.rem(y + 1 + i, 4)
        two_b.append(remote(sum_b.at[ty], got_b.at[i], r2b_s.at[i], r2b_r.at[i], y_places[i]))
    start(two_b)
    here = columns(me)
    finish(two_a)
    total = sum_a[z].astype(f32) + got_a[0].astype(f32) + got_a[1].astype(f32) + got_a[2].astype(f32)
    own_a[0] = total.astype(jnp.bfloat16)
    back_a = [
        remote(own_a.at[0], out.at[rows_a, here], g1a_s.at[i], g1a_r.at[i], z_places[i]) for i in range(3)
    ]
    start(back_a)
    last_a = pltpu.make_async_copy(own_a.at[0], out.at[rows_a, here], fin.at[0])
    last_a.start()
    finish(two_b)
    total = sum_b[y].astype(f32) + got_b[0].astype(f32) + got_b[1].astype(f32) + got_b[2].astype(f32)
    own_a[1] = total.astype(jnp.bfloat16)
    back_b = [
        remote(own_a.at[1], out.at[rows_b, here], g1b_s.at[i], g1b_r.at[i], y_places[i]) for i in range(3)
    ]
    start(back_b)
    last_b = pltpu.make_async_copy(own_a.at[1], out.at[rows_b, here], fin.at[1])
    last_b.start()
    last_a.wait()
    finish(back_a)
    end_a, end_b = [], []
    for i in range(3):
        for k in range(4):
            part = out.at[rows_a, columns(4 * k + y)]
            end_a.append(remote(part, part, g2a_s.at[i, k], g2a_r.at[i, k], y_places[i]))
    start(end_a)
    last_b.wait()
    finish(back_b)
    for i in range(3):
        part = out.at[rows_b, columns(4 * z, 4)]
        end_b.append(remote(part, part, g2b_s.at[i], g2b_r.at[i], z_places[i]))
    start(end_b)
    finish(end_a)
    finish(end_b)


def total_over_replicas(g):
    dma = pltpu.SemaphoreType.DMA
    bf16 = jnp.bfloat16
    return pl.pallas_call(
        total_kernel,
        out_shape=jax.ShapeDtypeStruct(g.shape, g.dtype),
        in_specs=[pl.BlockSpec(memory_space=pl.ANY)],
        out_specs=pl.BlockSpec(memory_space=pl.ANY),
        scratch_shapes=[
            pltpu.VMEM((4, HALF, PIECE), bf16),
            pltpu.VMEM((HALF, 4 * PIECE), bf16),
            pltpu.VMEM((3, 4, HALF, PIECE), bf16),
            pltpu.VMEM((3, HALF, 4 * PIECE), bf16),
            pltpu.VMEM((4, HALF, PIECE), bf16),
            pltpu.VMEM((4, HALF, PIECE), bf16),
            pltpu.VMEM((3, HALF, PIECE), bf16),
            pltpu.VMEM((3, HALF, PIECE), bf16),
            dma((5,)),
            dma((3, 4)), dma((3, 4)), dma((3,)), dma((3,)),
            dma((3,)), dma((3,)), dma((3,)), dma((3,)),
            dma((3,)), dma((3,)), dma((3,)), dma((3,)),
            dma((3, 4)), dma((3, 4)), dma((3,)), dma((3,)),
            dma((2,)),
        ],
        compiler_params=pltpu.CompilerParams(
            collective_id=2, has_side_effects=True, vmem_limit_bytes=48 * 1024 * 1024
        ),
        name="total_over_replicas",
    )(g)


def lane_mask(shape, micro):
    lane = lax.broadcasted_iota(jnp.int32, shape, len(shape) - 1)
    return (lane >= HD) if micro else (lane < HD)


def allowed_block(n0, n2, first_query, queries, keys):
    i = lax.broadcasted_iota(jnp.int32, (queries, keys), 0) + first_query
    j = lax.broadcasted_iota(jnp.int32, (queries, keys), 1)
    row = lax.broadcasted_iota(jnp.int32, (queries, 1), 0) + first_query
    start = jnp.where(row >= n2, n2, jnp.where(row >= n0, n0, 0))
    return (j <= i) & (j >= start)


def scores_of(q, k, micro, allowed):
    zero = jnp.zeros((), jnp.bfloat16)
    q = jnp.where(lane_mask(q.shape, micro), q, zero)
    s = lax.dot_general(q, k, (((1,), (1,)), ((), ())), preferred_element_type=jnp.float32)
    return jnp.where(allowed, s * SCALE, masked_score)


def take(x, entry, start, count):
    return x[pl.ds(start, count), entry].reshape(count * TQ, 2 * HD)


def forward_kernel(bounds, x, q16, o, o16, lse, lse16):
    zero = jnp.zeros((), jnp.bfloat16)
    me = lax.axis_index("replica")

    def attend(q, k, v, micro, first_query):
        allowed = allowed_block(bounds[micro], bounds[2 + micro], first_query, q.shape[0], k.shape[0])
        s = scores_of(q, k, micro, allowed)
        largest = jnp.max(s, axis=-1, keepdims=True)
        e = jnp.exp(s - largest)
        summed = jnp.sum(e, axis=-1, keepdims=True)
        p = (e * (1.0 / summed)).astype(jnp.bfloat16)
        v = jnp.where(lane_mask(v.shape, micro), v, zero)
        return times(p, v), largest + jnp.log(summed)

    per = BQ // TQ
    for b in range(SEQ // BQ):
        count = (b + 1) * per
        q = take(x, 0, b * per, per)
        k = take(x, 1, 0, count)
        v = take(x, 2, 0, count)
        o0, l0 = attend(q, k, v, 0, b * BQ)
        o1, l1 = attend(q, k, v, 1, b * BQ)
        o[pl.ds(b * per, per)] = (o0 + o1).astype(jnp.bfloat16).reshape(per, TQ, 2 * HD)
        lse[pl.ds(b * BQ, BQ)] = jnp.where(lane_mask((BQ, 2 * HD), 0), l0, l1)
    q = q16[...]
    k = take(x, 3, 0, NR)
    v = take(x, 4, 0, NR)
    o0, l0 = attend(q, k, v, 0, me * TQ)
    o1, l1 = attend(q, k, v, 1, me * TQ)
    o16[...] = (o0 + o1).astype(jnp.bfloat16)
    lse16[...] = jnp.where(lane_mask((TQ, 2 * HD), 0), l0, l1)


def vmem_specs(count):
    return [pl.BlockSpec(memory_space=pltpu.VMEM)] * count


def attention_forward(bounds, x, q16):
    f32, bf16 = jnp.float32, jnp.bfloat16
    return pl.pallas_call(
        forward_kernel,
        out_shape=[
            jax.ShapeDtypeStruct((NR, TQ, 2 * HD), bf16),
            jax.ShapeDtypeStruct((TQ, 2 * HD), bf16),
            jax.ShapeDtypeStruct((SEQ, 2 * HD), f32),
            jax.ShapeDtypeStruct((TQ, 2 * HD), f32),
        ],
        in_specs=[pl.BlockSpec(memory_space=pltpu.SMEM)] + vmem_specs(2),
        out_specs=vmem_specs(4),
        compiler_params=pltpu.CompilerParams(vmem_limit_bytes=48 * 1024 * 1024),
        name="attention_forward",
    )(bounds, x, q16)


def backward_kernel(bounds, x, q16, lse, lse16, do, do16, dx, dq16, dk, dv):
    zero = jnp.zeros((), jnp.bfloat16)
    me = lax.axis_index("replica")
    bf16 = jnp.bfloat16

    def pull(q, k, v, grad, logs, micro, first_query):
        allowed = allowed_block(bounds[micro], bounds[2 + micro], first_query, q.shape[0], k.shape[0])
        s = scores_of(q, k, micro, allowed)
        soft = jnp.exp(s - logs[:, micro * HD : micro * HD + 1])
        grad = jnp.where(lane_mask(grad.shape, micro), grad, zero)
        dp = times_transposed(grad, v)
        along = jnp.sum(soft * dp, axis=-1, keepdims=True)
        ds = (soft * (dp - along)).astype(bf16)
        q = jnp.where(lane_mask(q.shape, micro), q, zero)
        k = jnp.where(lane_mask(k.shape, micro), k, zero)
        return times(ds, k), outer_sum(ds, q), outer_sum(soft.astype(bf16), grad)

    per = BQ // TQ
    for b in reversed(range(SEQ // BQ)):
        count = (b + 1) * per
        q = take(x, 0, b * per, per)
        k = take(x, 1, 0, count)
        v = take(x, 2, 0, count)
        grad = do[pl.ds(b * per, per)].reshape(BQ, 2 * HD)
        logs = lse[pl.ds(b * BQ, BQ)]
        q0, k0, v0 = pull(q, k, v, grad, logs, 0, b * BQ)
        q1, k1, v1 = pull(q, k, v, grad, logs, 1, b * BQ)
        dx[pl.ds(b * per, per), 0] = ((q0 + q1) * SCALE).astype(bf16).reshape(per, TQ, 2 * HD)
        keys = pl.ds(0, (b + 1) * BQ)
        if b == SEQ // BQ - 1:
            dk[keys] = k0 + k1
            dv[keys] = v0 + v1
        else:
            dk[keys] += k0 + k1
            dv[keys] += v0 + v1
    dx[:, 1] = (dk[...] * SCALE).astype(bf16).reshape(NR, TQ, 2 * HD)
    dx[:, 2] = dv[...].astype(bf16).reshape(NR, TQ, 2 * HD)
    q = q16[...]
    k = take(x, 3, 0, NR)
    v = take(x, 4, 0, NR)
    q0, k0, v0 = pull(q, k, v, do16[...], lse16[...], 0, me * TQ)
    q1, k1, v1 = pull(q, k, v, do16[...], lse16[...], 1, me * TQ)
    dq16[...] = ((q0 + q1) * SCALE).astype(bf16)
    dx[:, 3] = ((k0 + k1) * SCALE).astype(bf16).reshape(NR, TQ, 2 * HD)
    dx[:, 4] = (v0 + v1).astype(bf16).reshape(NR, TQ, 2 * HD)


def attention_backward(bounds, x, q16, lse, lse16, do, do16):
    f32, bf16 = jnp.float32, jnp.bfloat16
    return pl.pallas_call(
        backward_kernel,
        out_shape=[
            jax.ShapeDtypeStruct((NR, 5, TQ, 2 * HD), bf16),
            jax.ShapeDtypeStruct((TQ, 2 * HD), bf16),
        ],
        in_specs=[pl.BlockSpec(memory_space=pltpu.SMEM)] + vmem_specs(6),
        out_specs=vmem_specs(2),
        scratch_shapes=[pltpu.VMEM((SEQ, 2 * HD), f32), pltpu.VMEM((SEQ, 2 * HD), f32)],
        compiler_params=pltpu.CompilerParams(vmem_limit_bytes=48 * 1024 * 1024),
        name="attention_backward",
    )(bounds, x, q16, lse, lse16, do, do16)


def heads_first(matrix):
    n = matrix.shape[1] // HD
    return matrix.reshape(2, TQ, n, HD).transpose(2, 1, 0, 3).reshape(n, TQ, 2 * HD)


def heads_last(blocks):
    n = blocks.shape[0]
    return blocks.reshape(n, TQ, 2, HD).transpose(2, 1, 0, 3).reshape(2 * TQ, n * HD)


def layer_forward(inputs, bounds, gain_rows, bias_rows, up_shift, weights):
    w_qkv, w_out, w_up, w_down = weights
    bf16 = jnp.bfloat16
    normed_in, normed_first, inverse_first = layer_norm(inputs, gain_rows[0], bias_rows[0])
    act_first = normed_in.astype(bf16)
    mixed_out = times(act_first, w_qkv)
    shift = jnp.concatenate([bias_rows[1], jnp.zeros_like(bias_rows[1]), bias_rows[2]], axis=1)
    mixed = heads_first((mixed_out + shift).astype(bf16)).reshape(3, H, TQ, 2 * HD)
    q16 = mixed[0, H - 1]
    message = jnp.concatenate(
        [
            mixed[:, : H - 1].transpose(1, 0, 2, 3),
            jnp.broadcast_to(mixed[None, 1:, H - 1], (NR, 2, TQ, 2 * HD)),
        ],
        axis=1,
    )
    whole = swap(message.reshape(NR, 5 * TQ, 2 * HD), 3).reshape(NR, 5, TQ, 2 * HD)
    o, o16, lse, lse16 = attention_forward(bounds, whole, q16)
    o = swap(o, 4)
    attended = heads_last(jnp.concatenate([o, o16[None]], axis=0))
    residual = inputs + times(attended, w_out) + bias_rows[3]
    normed_mid, normed_second, inverse_second = layer_norm(residual, gain_rows[1], bias_rows[4])
    act_second = normed_mid.astype(bf16)
    hidden_pre = times(act_second, w_up) + up_shift
    hidden = jax.nn.gelu(hidden_pre, approximate=True).astype(bf16)
    result = residual + times(hidden, w_down) + bias_rows[5]
    kept = {
        "normed_first": normed_first,
        "inverse_first": inverse_first,
        "act_first": act_first,
        "whole": whole,
        "q16": q16,
        "lse": lse,
        "lse16": lse16,
        "attended": attended,
        "normed_second": normed_second,
        "inverse_second": inverse_second,
        "act_second": act_second,
        "hidden_pre": hidden_pre,
        "hidden": hidden,
    }
    return (result, kept)


def layer_backward(grad_out, kept, bounds, gain_rows, weights):
    w_qkv, w_out, w_up, w_down = weights
    bf16 = jnp.bfloat16
    grad_down = grad_out.astype(bf16)
    grad_hidden = times_transposed(grad_down, w_down)
    gelu_value, gelu_pull = jax.vjp(
        functools.partial(jax.nn.gelu, approximate=True), kept["hidden_pre"]
    )
    grad_pre = gelu_pull(grad_hidden)[0].astype(bf16)
    grad_second = times_transposed(grad_pre, w_up)
    grad_resid = grad_out + norm_back(
        grad_second, kept["normed_second"], kept["inverse_second"], gain_rows[1]
    )
    grad_branch = grad_resid.astype(bf16)
    grad_heads = heads_first(times_transposed(grad_branch, w_out).astype(bf16))
    do = swap(grad_heads[: H - 1], 4)
    dx, dq16 = attention_backward(
        bounds, kept["whole"], kept["q16"], kept["lse"], kept["lse16"], do, grad_heads[H - 1]
    )
    back = swap(dx.reshape(NR, 5 * TQ, 2 * HD), 3).reshape(NR, 5, TQ, 2 * HD)
    last = jnp.sum(back[:, 3:].astype(jnp.float32), axis=0).astype(bf16)
    last = jnp.concatenate([dq16[None], last], axis=0)
    parts = jnp.concatenate([back[:, :3].transpose(1, 0, 2, 3), last[:, None]], axis=1)
    grad_mixed = heads_last(parts.reshape(3 * H, TQ, 2 * HD))
    grad_first = times_transposed(grad_mixed, w_qkv)
    grad_in = grad_resid + norm_back(
        grad_first, kept["normed_first"], kept["inverse_first"], gain_rows[0]
    )
    record = {
        "grad_down": grad_down,
        "grad_pre": grad_pre,
        "grad_branch": grad_branch,
        "grad_mixed": grad_mixed,
        "grad_first": grad_first,
        "grad_second": grad_second,
    }
    return (grad_in, record)


X_ROUTE = [(j, j ^ 2) for j in range(4)]
C_ROUTE = [(j, j ^ 1) for j in range(4)]


def everyone(value):
    pair = jnp.stack([value, lax.ppermute(value, "shard", X_ROUTE)])
    other = lax.ppermute(pair, "shard", C_ROUTE)
    return jnp.concatenate([pair, other]).reshape(4 * value.shape[0], value.shape[1])


def own_columns(value):
    rows, width = value.shape
    cut = value.reshape(rows, 4, width // 4).transpose(1, 0, 2).reshape(2, 2, rows, width // 4)
    j = lax.axis_index("shard")
    upper, odd = j >= 2, lax.rem(j, 2) == 1
    mine = jnp.where(upper, cut[1], cut[0])
    theirs = lax.ppermute(jnp.where(upper, cut[0], cut[1]), "shard", X_ROUTE)
    both = jnp.stack([mine, theirs])
    keep = jnp.where(odd, both[:, 1], both[:, 0])
    give = jnp.where(odd, both[:, 0], both[:, 1])
    got = lax.ppermute(give, "shard", C_ROUTE)
    return jnp.concatenate([keep, got]).reshape(4 * rows, width // 4)


def small_row(kept, record):
    def column_sum(value):
        return jnp.sum(value.astype(jnp.float32), axis=0, keepdims=True)

    mixed = record["grad_mixed"]
    row = jnp.concatenate(
        [
            column_sum(record["grad_first"] * kept["normed_first"]),
            column_sum(record["grad_second"] * kept["normed_second"]),
            column_sum(record["grad_first"]),
            column_sum(mixed[:, :D]),
            column_sum(mixed[:, 2 * D :]),
            column_sum(record["grad_branch"]),
            column_sum(record["grad_second"]),
            column_sum(record["grad_down"]),
            column_sum(record["grad_pre"]),
        ],
        axis=1,
    )
    row = row + lax.ppermute(row, "shard", X_ROUTE)
    return row + lax.ppermute(row, "shard", C_ROUTE)


def shards(tokens, cotangent, doc_ids, gains, biases, up_bias, w_qkv, w_out, w_up, w_down):
    f32, bf16 = jnp.float32, jnp.bfloat16
    is_first = lax.axis_index("section") == 0
    weights = gather_weights((w_qkv[0], w_out[0], w_up[0], w_down[0]))
    docs = lax.all_gather(doc_ids[:, 0], "replica", axis=1, tiled=True)
    n0 = jnp.sum((docs == 0).astype(jnp.int32), axis=1)
    n2 = SEQ - jnp.sum((docs == 2).astype(jnp.int32), axis=1)
    bounds = jnp.concatenate([n0, n2])
    gain_rows = [gains[0, i : i + 1] for i in range(2)]
    bias_rows = [biases[0, i : i + 1] for i in range(6)]
    own_in = tokens.reshape(2 * TQ, D)
    own_cot = cotangent.reshape(2 * TQ, D)
    result, _ = layer_forward(own_in.astype(f32), bounds, gain_rows, bias_rows, up_bias, weights)
    inbox = lax.ppermute(result.astype(bf16), "section", [(0, 1)])
    inputs = jnp.where(is_first, own_in, inbox)
    result, kept = layer_forward(inputs.astype(f32), bounds, gain_rows, bias_rows, up_bias, weights)
    layer_out = result.astype(bf16)
    lefts = [own_columns(kept[k]) for k in ("act_first", "attended", "act_second", "hidden")]
    grad_in, _ = layer_backward(own_cot.astype(f32), kept, bounds, gain_rows, weights)
    inbox = lax.ppermute(grad_in.astype(bf16), "section", [(1, 0)])
    grad_out = jnp.where(is_first, inbox, own_cot)
    grad_in, record = layer_backward(grad_out.astype(f32), kept, bounds, gain_rows, weights)
    rights = [everyone(record[k]) for k in ("grad_mixed", "grad_branch", "grad_pre", "grad_down")]
    terms = [outer_sum(a, b).astype(bf16) for a, b in zip(lefts, rights)]
    down = terms[3].reshape(4, 272, D).transpose(1, 0, 2).reshape(272, 4 * D)
    block = jnp.concatenate([terms[0], terms[1], terms[2], down], axis=1)
    width = block.shape[1]
    row = small_row(kept, record).astype(bf16)
    block = jnp.concatenate([block, row, jnp.zeros((RED_ROWS - 273, width), bf16)], axis=0)
    block = jnp.pad(block, ((0, 0), (0, NR * PIECE - width)))
    summed = total_over_replicas(block)
    grads = summed[:272].astype(f32)
    small = summed[272].astype(f32)
    return (
        layer_out.reshape(1, 2, 1, TQ, D),
        grad_in.astype(bf16).reshape(1, 2, 1, TQ, D),
        small[: 2 * D].reshape(1, 2, D),
        small[2 * D : 8 * D].reshape(1, 6, D),
        small[8 * D : 8 * D + FF].reshape(1, FF),
        grads[None, :, : 3 * D],
        grads[None, :, 3 * D : 4 * D],
        grads[None, :, 4 * D : 8 * D],
        grads[:, 8 * D : 12 * D].reshape(272, 4, D).transpose(1, 0, 2).reshape(1, 1088, D),
    )


def solution(mesh):
    placed = (
        P(None, "shard", "replica", None),
        P(None, "shard", "replica", None),
        P(None, "shard", "replica"),
        P("section", None, None),
        P("section", None, None),
        P("section", None),
        P("section", "shard", None),
        P("section", "shard", None),
        P("section", "shard", None),
        P("section", "shard", None),
    )
    return jax.shard_map(
        shards,
        mesh=mesh,
        in_specs=placed,
        out_specs=(
            P("section", None, "shard", "replica", None),
            P("section", None, "shard", "replica", None),
            P("section", None, None),
            P("section", None, None),
            P("section", None),
            P("section", "shard", None),
            P("section", "shard", None),
            P("section", "shard", None),
            P("section", "shard", None),
        ),
        check_vma=False,
    )
```

time: 2020 us -> 869 us (0.43)
  waiting for transfers between devices: 1240 us -> 25.2 us
  Pallas kernels: 0 us -> 481 us
  blocking collectives: 354 us -> 24.7 us
  matrix products: 193 us -> 99.1 us
    all_gather x16 -> x0, waiting for transfers between devices: 532 us -> none  [the longest x3 112 us: layer_backward(): lax.all_gather(as_sent(kept['value_local']), 'replica', axis=0, tiled=True)]
    pallas_call x0 -> x14, Pallas kernels: none -> 481 us  [the longest x1 229 us: gather_weights(): pl.pallas_call(weights_kernel, out_shape=[jax.ShapeDtypeStruct((4 * r, n)...]
    unnamed x33 -> x0, waiting for transfers between devices: 436 us -> none
    psum x1 -> x0, blocking collectives: 329 us -> none  [shards(): lax.psum(small_terms(caches, records, model_width), ('shard', 'replica'))]
    reduce_scatter x4 -> x0, waiting for transfers between devices: 263 us -> none  [shards(): lax.psum_scatter(as_sent(weight_terms(caches, records)), 'shard', scatter...]
    dot_general x33 -> x7, matrix products: 108 us -> 43.6 us  [times(): return jnp.dot(left, right, preferred_element_type=jnp.float32)]
    all_gather x12 -> x0, local copies, waits for them, and re-layouts: 48.4 us -> none  [the longest x3 12.8 us: layer_backward(): lax.all_gather(as_sent(kept['key_local']), 'replica', axis=0, tiled=True)]
    reshape x0 -> x19, local copies, waits for them, and re-layouts: none -> 47.6 us  [the longest x8 26.6 us: heads_first(): matrix.reshape(2, TQ, n, HD).transpose(2, 1, 0, 3).reshape(n, TQ, 2 * HD)]
  transfers between devices with their start and end apart: 31 -> 20, of which waited for: 26 -> 3; matrix products, arithmetic and copies ran while one was open for 15% -> 10% of each run, Pallas kernels for 0% -> 0%
where the time goes in v1:
time: 869 us; the launch traced here: 861 us
  Pallas kernels  481 us (55%)
  local copies, waits for them, and re-layouts  154 us (18%)
  matrix products  99.1 us (11%)
  other arithmetic  51.9 us (6%)
  waiting for transfers between devices  25.2 us (3%)
  blocking collectives  24.7 us (3%)
  starting transfers between devices  23 us (3%)
    pallas_call x1, Pallas kernels, gather_weights(): pl.pallas_call(weights_kernel, out_shape=[jax.ShapeDtypeStruct((4 * r, n)...  229 us
    pallas_call x1, Pallas kernels, total_over_replicas(): pl.pallas_call(total_kernel, out_shape=jax.ShapeDtypeStruct(g.shape, g.dt...  124 us
    pallas_call x8, Pallas kernels, swap(): pl.pallas_call(swap_kernel, out_shape=jax.ShapeDtypeStruct(x.shape, x.dty...  103 us
    dot_general x7, matrix products, times(): return jnp.dot(left, right, preferred_element_type=jnp.float32)  43.6 us
    dot_general x7, matrix products, times_transposed(): lax.dot_general(left, right, (((1,), (1,)), ((), ())), preferred_element_...  41.4 us
    reshape x8, local copies, waits for them, and re-layouts, heads_first(): matrix.reshape(2, TQ, n, HD).transpose(2, 1, 0, 3).reshape(n, TQ, 2 * HD)  26.6 us
    all_gather x1, blocking collectives, shards(): docs = lax.all_gather(doc_ids[:, 0], 'replica', axis=1, tiled=True)  24.7 us
    ppermute x4, waiting for transfers between devices, everyone(): pair = jnp.stack([value, lax.ppermute(value, 'shard', X_ROUTE)])  19.5 us
  transfers between devices with their start and end apart: 20, of which 3 were waited for; matrix products, arithmetic and copies ran while one was open for 10% of the time, Pallas kernels for 0%

profile of v1, /device:TPU:0, one launch (start us, length us, event | category | flops | bytes accessed | tf_op | source)
XLA Modules:
  0.0 860.5 jit_solution(14263369635985362495)
XLA Ops:
  6.1 228.7 %gather_weights.1 = (bf16[1088,3264]{1,0:T(8,128)(2,1)}, bf16[1088,1088]{1,0:T(8,128)(2,1)}, bf16[1088,4352]{1,0:T(8,128)(2,1)}, bf16[4352,1088]{1,0:T(8,128)(2,1)}) custom-call(bf16[272,3264]{1,0:T(8,128)(2,1)} %bitcast.242, bf16[272,1088]{1,0:T(8,128)(2,1)} %bitcast.246, bf16[272,4352]{1,0:T(8,128)(2,1)} %bitcast.237, bf16[1088,1088]{1,0:T(8,128)(2,1)} %bitcast.235), custom_call_target="tpu_custom_call" | custom-call | tf_op jit(solution)/shard_map/gather_weights/pallas_call | solution.py:201
  249.2 24.7 %all-gather = s32[2,1,1024]{0,1,2:T(1,128)S(1)} all-gather(s32[2,1,64]{0,1,2:T(1,128)S(1)} %copy.76), channel_id=2, replica_groups=mesh['section'=2,'shard'=4,'replica'=16] {'replica'}, dimensions={2}, use_global_device_ids=true | all-gather | bytes 8704 | tf_op jit(solution)/shard_map/all_gather | solution.py:625
  276.7 16.4 %swap.8 = bf16[16,320,128]{2,1,0:T(8,128)(2,1)} custom-call(bf16[16,320,128]{2,1,0:T(8,128)(2,1)} %bitcast.228), custom_call_target="tpu_custom_call" | custom-call | tf_op jit(solution)/shard_map/swap/pallas_call | solution.py:104
  300.5 10.0 %swap.9 = bf16[16,64,128]{2,1,0:T(8,128)(2,1)} custom-call(bf16[16,64,128]{2,1,0:T(8,128)(2,1)} %copy-done.7), custom_call_target="tpu_custom_call" | custom-call | tf_op jit(solution)/shard_map/swap/pallas_call | solution.py:104
  320.9 11.8 %fusion.20 = bf16[128,1088]{0,1:T(8,128)(2,1)S(1)} fusion(f32[128,1088]{0,1:T(8,128)} %copy-done.25, bf16[4352,1088]{1,0:T(8,128)(2,1)} %get-tuple-element.28, bf16[1088,4352]{1,0:T(8,128)(2,1)} %get-tuple-element.27, f32[4352]{0:T(1024)S(1)} %reduce.14, f32[1088]{0:T(1024)S(1)} %get-tuple-element.83, f32[1088]{0:T(1024)S(1)} %get-tuple-element.80, ...), kind=kOutput, calls=%fused_computation.43 | convolution fusion | flops 2430992384 | bytes 19806976 | tf_op jit(solution)/shard_map/dot_general | solution.py:42
  340.5 7.0 fusion.4
  361.4 15.8 %swap.10 = bf16[16,320,128]{2,1,0:T(8,128)(2,1)} custom-call(bf16[16,320,128]{2,1,0:T(8,128)(2,1)} %bitcast.229), custom_call_target="tpu_custom_call" | custom-call | tf_op jit(solution)/shard_map/swap/pallas_call | solution.py:104
  383.8 9.8 %swap.11 = bf16[16,64,128]{2,1,0:T(8,128)(2,1)} custom-call(bf16[16,64,128]{2,1,0:T(8,128)(2,1)} %copy-done.8), custom_call_target="tpu_custom_call" | custom-call | tf_op jit(solution)/shard_map/swap/pallas_call | solution.py:104
  409.5 13.1 %fusion.128 = (f32[128]{0:T(128)S(1)}, f32[128]{0:T(128)S(1)}, f32[128,1088]{0,1:T(8,128)S(1)}) fusion(f32[128]{0:T(128)S(1)} %add_rsqrt_fusion.1, f32[128,1088]{0,1:T(8,128)S(1)} %get-tuple-element.116, f32[128]{0:T(128)S(1)} %broadcast_multiply_fusion.9, f32[1088]{0:T(1024)S(1)} %get-tuple-element.84, bf16[1088,4352]{1,0:T(8,128)(2,1)} %get-tuple-element.27, ...), kind=kOutput, calls=%fused_computation.260 | convolution fusion | flops 2436284416 | bytes 22567168 | tf_op jit(solution)/shard_map/dot_general | solution.py:46
  437.2 9.5 %swap.12.do = bf16[16,64,128]{2,1,0:T(8,128)(2,1)} custom-call(bf16[16,64,128]{2,1,0:T(8,128)(2,1)} %slice.197.x), custom_call_target="tpu_custom_call" | custom-call | tf_op jit(solution)/shard_map/swap/pallas_call | solution.py:104
  447.7 7.7 attention_backward.2
  456.5 15.7 %swap.13 = bf16[16,320,128]{2,1,0:T(8,128)(2,1)} custom-call(bf16[16,320,128]{2,1,0:T(8,128)(2,1)} %bitcast.211), custom_call_target="tpu_custom_call" | custom-call | tf_op jit(solution)/shard_map/swap/pallas_call | solution.py:104
  514.2 8.2 convert_reduce_fusion
  540.0 10.0 %swap.14.do = bf16[16,64,128]{2,1,0:T(8,128)(2,1)} custom-call(bf16[16,64,128]{2,1,0:T(8,128)(2,1)} %slice.202.x), custom_call_target="tpu_custom_call" | custom-call | tf_op jit(solution)/shard_map/swap/pallas_call | solution.py:104
  551.0 7.7 attention_backward.3
  559.7 15.7 %swap.15 = bf16[16,320,128]{2,1,0:T(8,128)(2,1)} custom-call(bf16[16,320,128]{2,1,0:T(8,128)(2,1)} %bitcast.210), custom_call_target="tpu_custom_call" | custom-call | tf_op jit(solution)/shard_map/swap/pallas_call | solution.py:104
  583.1 7.0 copy.95
  600.9 7.6 fusion.21
  634.4 19.5 %collective-permute-done.12 = bf16[128,4352]{1,0:T(8,128)(2,1)S(1)} collective-permute-done((bf16[128,4352]{1,0:T(8,128)(2,1)S(1)}, bf16[128,4352]{1,0:T(8,128)(2,1)S(1)}, u32[]{:S(2)}, u32[]{:S(2)}) %collective-permute-start.12) | collective-permute-done | bytes 1114144 | tf_op jit(solution)/shard_map/ppermute | solution.py:579
  675.2 11.8 %concatenate.100 = bf16[272,13056]{1,0:T(8,128)(2,1)} concatenate(bf16[272,3264]{1,0:T(8,128)(2,1)} %fusion.2, bf16[272,1088]{1,0:T(8,128)(2,1)S(1)} %copy-done.30, bf16[272,4352]{1,0:T(8,128)(2,1)} %fusion.1, bf16[272,4352]{1,0:T(8,128)(2,1)S(1)} %copy-done.11), dimensions={1} | concatenate | bytes 14204928 | tf_op jit(solution)/shard_map/concatenate | solution.py:646
  695.6 123.9 %total_over_replicas.1 = bf16[288,14336]{1,0:T(8,128)(2,1)} custom-call(bf16[288,14336]{1,0:T(8,128)(2,1)} %pad.4.g), custom_call_target="tpu_custom_call" | custom-call | tf_op jit(solution)/shard_map/total_over_replicas/pallas_call | solution.py:312
  821.3 10.6 %slice_convert_fusion = f32[272,14336]{1,0:T(8,128)} fusion(bf16[288,14336]{1,0:T(8,128)(2,1)} %total_over_replicas.1), kind=kLoop, calls=%fused_computation.1 | loop fusion | flops 3899392 | bytes 23396352 | tf_op jit(solution)/shard_map/convert_element_type | solution.py:652
  838.7 8.1 fusion.130
  848.2 6.9 reshape.314
  (285 shorter events, 251.2 us)
Async XLA Ops:
  5.9 228.9 %copy-start.16 = (bf16[128,1088]{0,1:T(8,128)(2,1)}, bf16[128,1088]{0,1:T(8,128)(2,1)S(1)}, u32[]{:S(2)}) copy-start(bf16[128,1088]{0,1:T(8,128)(2,1)S(1)} %copy.81) | copy-start | bytes 835588
  300.4 18.3 %copy-start.9 = (bf16[1088,1088]{1,0:T(8,128)(2,1)S(1)}, bf16[1088,1088]{1,0:T(8,128)(2,1)}, u32[]{:S(2)}) copy-start(bf16[1088,1088]{1,0:T(8,128)(2,1)} %get-tuple-element.26) | copy-start | bytes 7102468
  300.4 18.3 %copy-start.17 = (bf16[128,1088]{0,1:T(8,128)(2,1)S(1)}, bf16[128,1088]{0,1:T(8,128)(2,1)}, u32[]{:S(2)}) copy-start(bf16[128,1088]{0,1:T(8,128)(2,1)} %copy-done.16) | copy-start | bytes 835588
  332.7 6.4 collective-permute-start
  426.7 20.0 %copy-start.1 = (bf16[16,320,128]{2,1,0:T(8,128)(2,1)S(1)}, bf16[16,320,128]{2,1,0:T(8,128)(2,1)}, u32[]{:S(2)}) copy-start(bf16[16,320,128]{2,1,0:T(8,128)(2,1)} %swap.10) | copy-start | bytes 3932164
  475.3 32.3 %collective-permute-start.2 = (bf16[2,128,272]{1,2,0:T(8,128)(2,1)}, bf16[2,128,272]{1,2,0:T(8,128)(2,1)}, u32[]{:S(2)}, u32[]{:S(2)}) collective-permute-start(bf16[2,128,272]{1,2,0:T(8,128)(2,1)} %get-tuple-element.110), channel_id=1, source_target_pairs={{0,32},{16,48},{32,0},{48,16},{1,33},{17,49},{33,1},{49,17},{2,34}... | collective-permute-start | bytes 417800 | tf_op jit(solution)/shard_map/ppermute | solution.py:590
  478.6 31.1 %collective-permute-start.6 = (bf16[2,128,272]{1,2,0:T(8,128)(2,1)}, bf16[2,128,272]{1,2,0:T(8,128)(2,1)}, u32[]{:S(2)}, u32[]{:S(2)}) collective-permute-start(bf16[2,128,272]{1,2,0:T(8,128)(2,1)} %get-tuple-element.106), channel_id=1, source_target_pairs={{0,32},{16,48},{32,0},{48,16},{1,33},{17,49},{33,1},{49,17},{2,34}... | collective-permute-start | bytes 417800 | tf_op jit(solution)/shard_map/ppermute | solution.py:590
  480.3 26.0 %collective-permute-start.10 = (bf16[2,128,272]{1,2,0:T(8,128)(2,1)}, bf16[2,128,272]{1,2,0:T(8,128)(2,1)S(1)}, u32[]{:S(2)}, u32[]{:S(2)}) collective-permute-start(bf16[2,128,272]{1,2,0:T(8,128)(2,1)} %get-tuple-element.102), channel_id=1, source_target_pairs={{0,32},{16,48},{32,0},{48,16},{1,33},{17,49},{33,1},{49,17},{2,34}... | collective-permute-start | bytes 417800 | tf_op jit(solution)/shard_map/ppermute | solution.py:590
  504.8 8.6 collective-permute-start.1
  577.7 50.8 %collective-permute-start.8 = (bf16[128,1088]{0,1:T(8,128)(2,1)}, bf16[128,1088]{0,1:T(8,128)(2,1)}, u32[]{:S(2)}, u32[]{:S(2)}) collective-permute-start(bf16[128,1088]{0,1:T(8,128)(2,1)} %get-tuple-element.91), channel_id=1, source_target_pairs={{0,32},{16,48},{32,0},{48,16},{1,33},{17,49},{33,1},{49,17},{2,34}... | collective-permute-start | bytes 835592 | tf_op jit(solution)/shard_map/ppermute | solution.py:579
  579.4 45.9 %collective-permute-start.16 = (bf16[128,1088]{0,1:T(8,128)(2,1)}, bf16[128,1088]{0,1:T(8,128)(2,1)}, u32[]{:S(2)}, u32[]{:S(2)}) collective-permute-start(bf16[128,1088]{0,1:T(8,128)(2,1)} %get-tuple-element.89), channel_id=1, source_target_pairs={{0,32},{16,48},{32,0},{48,16},{1,33},{17,49},{33,1},{49,17},{2,34}... | collective-permute-start | bytes 835592 | tf_op jit(solution)/shard_map/ppermute | solution.py:579
  599.0 32.5 %collective-permute-start.4 = (bf16[128,3264]{0,1:T(8,128)(2,1)}, bf16[128,3264]{0,1:T(8,128)(2,1)}, u32[]{:S(2)}, u32[]{:S(2)}) collective-permute-start(bf16[128,3264]{0,1:T(8,128)(2,1)} %reshape.305), channel_id=1, source_target_pairs={{0,32},{16,48},{32,0},{48,16},{1,33},{17,49},{33,1},{49,17},{2,34}... | collective-permute-start | bytes 2506760 | tf_op jit(solution)/shard_map/ppermute | solution.py:579
  611.2 13.2 %collective-permute-start.18 = (f32[1,13056]{1,0:T(1,128)S(1)}, f32[1,13056]{1,0:T(1,128)}, u32[]{:S(2)}, u32[]{:S(2)}) collective-permute-start(f32[1,13056]{1,0:T(1,128)S(1)} %concatenate.101), channel_id=1, source_target_pairs={{0,32},{16,48},{32,0},{48,16},{1,33},{17,49},{33,1},{49,17},{2,34}... | collective-permute-start | bytes 156680 | tf_op jit(solution)/shard_map/ppermute | solution.py:617
  615.5 14.5 %collective-permute-start.14 = (bf16[2,128,1088]{1,2,0:T(8,128)(2,1)}, bf16[2,128,1088]{1,2,0:T(8,128)(2,1)}, u32[]{:S(2)}, u32[]{:S(2)}) collective-permute-start(bf16[2,128,1088]{1,2,0:T(8,128)(2,1)} %get-tuple-element.100), channel_id=1, source_target_pairs={{0,32},{16,48},{32,0},{48,16},{1,33},{17,49},{33,1},{49,17},{2,34}... | collective-permute-start | bytes 1671176 | tf_op jit(solution)/shard_map/ppermute | solution.py:590
  624.4 31.2 %collective-permute-start.7 = (bf16[2,128,272]{1,2,0:T(8,128)(2,1)S(1)}, bf16[2,128,272]{1,2,0:T(8,128)(2,1)S(1)}, u32[]{:S(2)}, u32[]{:S(2)}) collective-permute-start(bf16[2,128,272]{1,2,0:T(8,128)(2,1)S(1)} %copy-done.38), channel_id=1, source_target_pairs={{0,16},{16,0},{32,48},{48,32},{1,17},{17,1},{33,49},{49,33},{2,18}... | collective-permute-start | bytes 417800 | tf_op jit(solution)/shard_map/ppermute | solution.py:594
  625.3 28.6 %collective-permute-start.12 = (bf16[128,4352]{1,0:T(8,128)(2,1)S(1)}, bf16[128,4352]{1,0:T(8,128)(2,1)S(1)}, u32[]{:S(2)}, u32[]{:S(2)}) collective-permute-start(bf16[128,4352]{1,0:T(8,128)(2,1)S(1)} %copy-done.13), channel_id=1, source_target_pairs={{0,32},{16,48},{32,0},{48,16},{1,33},{17,49},{33,1},{49,17},{2,34}... | collective-permute-start | bytes 3342344 | tf_op jit(solution)/shard_map/ppermute | solution.py:579
  628.5 27.4 %collective-permute-start.19 = (f32[1,13056]{1,0:T(1,128)S(1)}, f32[1,13056]{1,0:T(1,128)S(1)}, u32[]{:S(2)}, u32[]{:S(2)}) collective-permute-start(f32[1,13056]{1,0:T(1,128)S(1)} %add.219), channel_id=1, source_target_pairs={{0,16},{16,0},{32,48},{48,32},{1,17},{17,1},{33,49},{49,33},{2,18}... | collective-permute-start | bytes 156680 | tf_op jit(solution)/shard_map/ppermute | solution.py:618
  629.9 26.2 %collective-permute-start.9 = (bf16[2,128,1088]{1,2,0:T(8,128)(2,1)S(1)}, bf16[2,128,1088]{1,2,0:T(8,128)(2,1)S(1)}, u32[]{:S(2)}, u32[]{:S(2)}) collective-permute-start(bf16[2,128,1088]{1,2,0:T(8,128)(2,1)S(1)} %pad_maximum_fusion.7), channel_id=1, source_target_pairs={{0,16},{16,0},{32,48},{48,32},{1,17},{17,1},{33,49},{49,33},{2,18}... | collective-permute-start | bytes 1671176 | tf_op jit(solution)/shard_map/ppermute | solution.py:580
  631.6 27.5 %collective-permute-start.17 = (bf16[2,128,1088]{1,2,0:T(8,128)(2,1)S(1)}, bf16[2,128,1088]{1,2,0:T(8,128)(2,1)S(1)}, u32[]{:S(2)}, u32[]{:S(2)}) collective-permute-start(bf16[2,128,1088]{1,2,0:T(8,128)(2,1)S(1)} %pad_maximum_fusion.8), channel_id=1, source_target_pairs={{0,16},{16,0},{32,48},{48,32},{1,17},{17,1},{33,49},{49,33},{2,18}... | collective-permute-start | bytes 1671176 | tf_op jit(solution)/shard_map/ppermute | solution.py:580
  653.9 5.4 collective-permute-start.15
  655.6 10.6 %collective-permute-start.5 = (bf16[2,128,3264]{1,2,0:T(8,128)(2,1)}, bf16[2,128,3264]{1,2,0:T(8,128)(2,1)}, u32[]{:S(2)}, u32[]{:S(2)}) collective-permute-start(bf16[2,128,3264]{1,2,0:T(8,128)(2,1)} %pad_maximum_fusion.1), channel_id=1, source_target_pairs={{0,16},{16,0},{32,48},{48,32},{1,17},{17,1},{33,49},{49,33},{2,18}... | collective-permute-start | bytes 5013512 | tf_op jit(solution)/shard_map/ppermute | solution.py:580
  655.9 14.6 %collective-permute-start.13 = (bf16[2,128,4352]{2,1,0:T(8,128)(2,1)}, bf16[2,128,4352]{2,1,0:T(8,128)(2,1)}, u32[]{:S(2)}, u32[]{:S(2)}) collective-permute-start(bf16[2,128,4352]{2,1,0:T(8,128)(2,1)} %pad_maximum_fusion), channel_id=1, source_target_pairs={{0,16},{16,0},{32,48},{48,32},{1,17},{17,1},{33,49},{49,33},{2,18}... | collective-permute-start | bytes 6684680 | tf_op jit(solution)/shard_map/ppermute | solution.py:580
  656.2 10.0 %collective-permute-start.3 = (bf16[2,128,272]{1,2,0:T(8,128)(2,1)}, bf16[2,128,272]{1,2,0:T(8,128)(2,1)}, u32[]{:S(2)}, u32[]{:S(2)}) collective-permute-start(bf16[2,128,272]{1,2,0:T(8,128)(2,1)} %get-tuple-element.108), channel_id=1, source_target_pairs={{0,16},{16,0},{32,48},{48,32},{1,17},{17,1},{33,49},{49,33},{2,18}... | collective-permute-start | bytes 417800 | tf_op jit(solution)/shard_map/ppermute | solution.py:594
  659.1 11.4 %collective-permute-start.11 = (bf16[2,128,272]{1,2,0:T(8,128)(2,1)S(1)}, bf16[2,128,272]{1,2,0:T(8,128)(2,1)}, u32[]{:S(2)}, u32[]{:S(2)}) collective-permute-start(bf16[2,128,272]{1,2,0:T(8,128)(2,1)S(1)} %copy-done.36), channel_id=1, source_target_pairs={{0,16},{16,0},{32,48},{48,32},{1,17},{17,1},{33,49},{49,33},{2,18}... | collective-permute-start | bytes 417800 | tf_op jit(solution)/shard_map/ppermute | solution.py:594
  (40 other events, 171.2 us)

commit v2 on v1

v2 whole, which is shorter than its diff:
```python
import functools

import jax
import jax.numpy as jnp
from jax import lax
from jax.experimental import pallas as pl
from jax.experimental.pallas import tpu as pltpu
from jax.sharding import PartitionSpec as P

MESH = pl.DeviceIdType.MESH
H = 17
HD = 64
TQ = 64
SEQ = 1024
NR = 16
D = 1088
FF = 4352
SCALE = HD ** (-0.5)
epsilon = 1e-05
masked_score = -1e30
BQ = 256
PIECE = 896
VMEM_BYTES = 58 * 1024 * 1024
RED_ROWS = 288
HALF = 144


def layer_norm(values, gain_row, shift_row):
    centre = values - jnp.mean(values, axis=-1, keepdims=True)
    inverse = lax.rsqrt(jnp.mean(centre * centre, axis=-1, keepdims=True) + epsilon)
    normed = centre * inverse
    return (normed * gain_row + shift_row, normed, inverse)


def norm_back(grad_normed_out, normed, inverse, gain_row):
    scaled = grad_normed_out * gain_row
    middle = jnp.mean(scaled, axis=-1, keepdims=True)
    slope = jnp.mean(scaled * normed, axis=-1, keepdims=True)
    return inverse * (scaled - middle - normed * slope)


def times(left, right):
    return jnp.dot(left, right, preferred_element_type=jnp.float32)


def times_transposed(left, right):
    return lax.dot_general(
        left, right, (((1,), (1,)), ((), ())), preferred_element_type=jnp.float32
    )


def outer_sum(left, right):
    return lax.dot_general(
        left, right, (((0,), (0,)), ((), ())), preferred_element_type=jnp.float32
    )


def y_peer(me, d):
    return (me // 4) * 4 + lax.rem(lax.rem(me, 4) + d, 4)


def z_peer(me, d):
    return lax.rem(me + 4 * d, NR)


def any_peer(me, d):
    return lax.rem(me // 4 + d // 4, 4) * 4 + lax.rem(lax.rem(me, 4) + d % 4, 4)


def remote(src, dst, send, recv, where):
    return pltpu.make_async_remote_copy(
        src_ref=src,
        dst_ref=dst,
        send_sem=send,
        recv_sem=recv,
        device_id=where,
        device_id_type=MESH,
    )


def cost(microseconds):
    return pl.CostEstimate(flops=0, bytes_accessed=int(microseconds * 3.5e6), transcendentals=0)


def greet(places):
    barrier = pltpu.get_barrier_semaphore()
    for where in places:
        pl.semaphore_signal(barrier, inc=1, device_id=where, device_id_type=MESH)
    pl.semaphore_wait(barrier, len(places))


def swap_kernel(x, o, send, recv, local):
    me = lax.axis_index("replica")
    greet([{"replica": any_peer(me, d)} for d in range(1, NR)])
    copies = []
    for d in range(1, NR):
        to = any_peer(me, d)
        copy = remote(x.at[to], o.at[me], send.at[d], recv.at[d], {"replica": to})
        copy.start()
        copies.append(copy)
    own = pltpu.make_async_copy(x.at[me], o.at[me], local)
    own.start()
    own.wait()
    for copy in copies:
        copy.wait()


def swap(x, collective_id):
    return pl.pallas_call(
        swap_kernel,
        out_shape=jax.ShapeDtypeStruct(x.shape, x.dtype),
        in_specs=[pl.BlockSpec(memory_space=pl.ANY)],
        out_specs=pl.BlockSpec(memory_space=pl.ANY),
        scratch_shapes=[
            pltpu.SemaphoreType.DMA((NR,)),
            pltpu.SemaphoreType.DMA((NR,)),
            pltpu.SemaphoreType.DMA,
        ],
        compiler_params=pltpu.CompilerParams(
            collective_id=collective_id, has_side_effects=True, vmem_limit_bytes=VMEM_BYTES
        ),
        cost_estimate=cost(16 if x.shape[1] > TQ else 9),
        name="swap",
    )(x)


W_SHAPES = ((272, 3264), (272, 1088), (272, 4352), (1088, 1088))
W_CUTS = (1664, 512, 2176, 512)


def weights_kernel(*refs):
    ins, docs, outs, all_docs, held = refs[:4], refs[4], refs[5:9], refs[9], refs[10:14]
    (own_s, own_r, local, back, xp_s, xp_r, xd_s, xd_r, f_s, f_r) = refs[14:24]
    (a1_s, a1_r, b1_s, b1_r, a2_s, a2_r, b2_s, b2_r, a3_s, a3_r, b3_s, b3_r, doc1_s, doc1_r, doc2_s, doc2_r) = refs[24:]
    j = lax.axis_index("shard")
    me = lax.axis_index("replica")
    z, y = me // 4, lax.rem(me, 4)
    xj = lax.rem(j + 2, 4)
    cj = j + 1 - 2 * lax.rem(j, 2)
    x_place, c_place = {"shard": xj}, {"shard": cj}
    y_places = [{"replica": y_peer(me, d)} for d in (1, 2, 3)]
    z_places = [{"replica": z_peer(me, d)} for d in (1, 2, 3)]
    greet([x_place, c_place] + y_places + z_places)

    def rows(start, count):
        return pl.ds(pl.multiple_of(start, 16), count)

    waits = []
    x_pieces, x_directs = [], []
    for a, (r, n) in enumerate(W_SHAPES):
        u = r // 17
        piece = remote(ins[a].at[rows(me * u, u)], outs[a].at[rows(j * r + me * u, u)], xp_s.at[a], xp_r.at[a], x_place)
        piece.start()
        x_pieces.append(piece)
    for a, (r, n) in enumerate(W_SHAPES):
        u = r // 17
        direct = remote(ins[a].at[rows(16 * u, u)], outs[a].at[rows(j * r + 16 * u, u)], xd_s.at[a], xd_r.at[a], x_place)
        direct.start()
        x_directs.append(direct)
    for a, (r, n) in enumerate(W_SHAPES):
        copy = remote(ins[a], outs[a].at[rows(j * r, r)], own_s.at[a], own_r.at[a], c_place)
        copy.start()
        waits.append(copy)
    all_docs[pl.ds(me, 1)] = docs[...][None]
    ours = all_docs.at[me]
    doc_firsts = [remote(ours, ours, doc1_s.at[i], doc1_r.at[i], y_places[i]) for i in range(3)]
    for copy in doc_firsts:
        copy.start()
    loads = [pltpu.make_async_copy(ins[a], held[a], local.at[a]) for a in range(4)]
    for copy in loads:
        copy.start()
    for a, (r, n) in enumerate(W_SHAPES):
        loads[a].wait()
        copy = pltpu.make_async_copy(held[a], outs[a].at[rows(j * r, r)], back.at[a])
        copy.start()
        waits.append(copy)
    for copy in doc_firsts:
        copy.wait()
    ours = all_docs.at[pl.ds(z * 4, 4)]
    for i in range(3):
        copy = remote(ours, ours, doc2_s.at[i], doc2_r.at[i], z_places[i])
        copy.start()
        waits.append(copy)
    firsts = []
    for a, (r, n) in enumerate(W_SHAPES):
        u, cut = r // 17, W_CUTS[a]
        x_pieces[a].wait()
        here = rows(xj * r + me * u, u)
        part_a = outs[a].at[here, pl.ds(0, cut)]
        part_b = outs[a].at[here, pl.ds(cut, n - cut)]
        group = []
        for i in range(3):
            group.append(remote(part_a, part_a, a1_s.at[a, i], a1_r.at[a, i], y_places[i]))
            group.append(remote(part_b, part_b, b1_s.at[a, i], b1_r.at[a, i], z_places[i]))
        for copy in group:
            copy.start()
        firsts.append(group)
    def row_part(a, first, half):
        r, u = W_SHAPES[a][0], W_SHAPES[a][0] // 17
        start = xj * r + lax.rem(first + 4, 4) * (4 * u) + half * (2 * u)
        return outs[a].at[rows(start, 2 * u), pl.ds(0, W_CUTS[a])]

    def column_part(a, first, k):
        (r, n), u = W_SHAPES[a], W_SHAPES[a][0] // 17
        start = xj * r + (4 * k + lax.rem(first + 4, 4)) * u
        return outs[a].at[rows(start, u), pl.ds(W_CUTS[a], n - W_CUTS[a])]

    heres = []
    for a in range(4):
        for copy in firsts[a]:
            copy.wait()
        rights, lefts = [], []
        for k in range(2):
            ref = row_part(a, z, k)
            rights.append(remote(ref, ref, a2_s.at[a, k], a2_r.at[a, k], z_places[0]))
            ref = row_part(a, z, 1 - k)
            lefts.append(remote(ref, ref, a2_s.at[a, 2 + k], a2_r.at[a, 2 + k], z_places[2]))
        for k in range(4):
            ref = column_part(a, y, k)
            rights.append(remote(ref, ref, b2_s.at[a, k], b2_r.at[a, k], y_places[0]))
            ref = column_part(a, y, 3 - k)
            lefts.append(remote(ref, ref, b2_s.at[a, 4 + k], b2_r.at[a, 4 + k], y_places[2]))
        for copy in rights + lefts:
            copy.start()
        heres.append((rights, lefts))
    for a, (r, n) in enumerate(W_SHAPES):
        rights, lefts = heres[a]
        passed = []
        rights[0].wait()
        ref = row_part(a, z - 1, 0)
        passed.append(remote(ref, ref, a3_s.at[a, 0], a3_r.at[a, 0], z_places[0]))
        lefts[0].wait()
        ref = row_part(a, z + 1, 1)
        passed.append(remote(ref, ref, a3_s.at[a, 1], a3_r.at[a, 1], z_places[2]))
        for k in range(2):
            rights[2 + k].wait()
            ref = column_part(a, y - 1, k)
            passed.append(remote(ref, ref, b3_s.at[a, k], b3_r.at[a, k], y_places[0]))
            lefts[2 + k].wait()
            ref = column_part(a, y + 1, 3 - k)
            passed.append(remote(ref, ref, b3_s.at[a, 2 + k], b3_r.at[a, 2 + k], y_places[2]))
        for copy in passed:
            copy.start()
        for copy in rights[1:2] + rights[4:] + lefts[1:2] + lefts[4:] + passed:
            copy.wait()
        x_directs[a].wait()
        whole = outs[a].at[rows(xj * r, r)]
        copy = remote(whole, whole, f_s.at[a], f_r.at[a], c_place)
        copy.start()
        waits.append(copy)
    for copy in waits:
        copy.wait()


def gather_weights(weights, docs):
    dma = pltpu.SemaphoreType.DMA
    outs = [jax.ShapeDtypeStruct((4 * r, n), jnp.bfloat16) for r, n in W_SHAPES]
    return pl.pallas_call(
        weights_kernel,
        out_shape=outs + [jax.ShapeDtypeStruct((NR, 8, 128), jnp.int32)],
        in_specs=[pl.BlockSpec(memory_space=pl.ANY)] * 4 + vmem_specs(1),
        out_specs=[pl.BlockSpec(memory_space=pl.ANY)] * 4 + vmem_specs(1),
        scratch_shapes=[pltpu.VMEM(shape, jnp.bfloat16) for shape in W_SHAPES]
        + [dma((4,))] * 10
        + [dma((4, 3))] * 4
        + [dma((4, 4))] * 2
        + [dma((4, 8))] * 2
        + [dma((4, 2))] * 2
        + [dma((4, 4))] * 2
        + [dma((3,))] * 4,
        compiler_params=pltpu.CompilerParams(
            collective_id=1, has_side_effects=True, vmem_limit_bytes=VMEM_BYTES
        ),
        name="gather_weights",
    )(*weights, docs)


def total_kernel(g, out, tr, ins, ad, part, mid, fin, p_s, p_r, q_s, q_r, m_s, m_r, n_s, n_r, e_s, e_r, w_s, w_r, loc):
    me = lax.axis_index("replica")
    z, y = me // 4, lax.rem(me, 4)
    y_places = [{"replica": y_peer(me, d)} for d in (1, 2, 3)]
    z_places = [{"replica": z_peer(me, d)} for d in (1, 2, 3)]
    greet(y_places + z_places)
    f32, bf16 = jnp.float32, jnp.bfloat16
    firsts, seconds = (y_places, z_places), (z_places, y_places)
    here, there = (y, z), (z, y)

    def at(side, first, second):
        first = lax.rem(first + 4, 4)
        piece = 4 * second + first if side == 0 else 4 * first + second
        return (pl.ds(side * HALF, HALF), pl.ds(pl.multiple_of(piece * PIECE, 128), PIECE))

    def piece_of(ref, side, first, second):
        return ref.at[at(side, first, second)]

    def value_of(side, first, second):
        return g[at(side, first, second)].astype(f32)

    opened, direct, added = [], [], []
    for s in range(2):
        t, right, left = here[s], firsts[s][0], firsts[s][2]
        group = []
        for k in range(2):
            group.append(remote(piece_of(g, s, t + 2, k), tr.at[s, 0, k], p_s.at[s, k], p_r.at[s, k], right))
            group.append(remote(piece_of(g, s, t + 2, k + 2), tr.at[s, 1, k], p_s.at[s, 2 + k], p_r.at[s, 2 + k], left))
        for copy in group:
            copy.start()
        opened.append(group)
    for s in range(2):
        t, right, left = here[s], firsts[s][0], firsts[s][2]
        group = []
        for k in range(2):
            group.append(remote(piece_of(g, s, t + 1, k + 2), ins.at[s, 0, k + 2], p_s.at[s, 4 + k], p_r.at[s, 4 + k], right))
            group.append(remote(piece_of(g, s, t - 1, k), ins.at[s, 1, k], p_s.at[s, 6 + k], p_r.at[s, 6 + k], left))
        for copy in group:
            copy.start()
        direct.append(group)
    for s in range(2):
        t, right, left = here[s], firsts[s][0], firsts[s][2]
        group = []
        for k in range(2):
            opened[s][2 * k].wait()
            ad[s, 0, k] = (tr[s, 0, k].astype(f32) + value_of(s, t + 1, k)).astype(bf16)
            copy = remote(ad.at[s, 0, k], ins.at[s, 0, k], q_s.at[s, k], q_r.at[s, k], right)
            copy.start()
            group.append(copy)
            opened[s][2 * k + 1].wait()
            ad[s, 1, k] = (tr[s, 1, k].astype(f32) + value_of(s, t - 1, k + 2)).astype(bf16)
            copy = remote(ad.at[s, 1, k], ins.at[s, 1, k + 2], q_s.at[s, 2 + k], q_r.at[s, 2 + k], left)
            copy.start()
            group.append(copy)
        added.append(group)
    middles = []
    for s in range(2):
        for copy in direct[s] + added[s]:
            copy.wait()
        for k in range(4):
            part[s, k] = (value_of(s, here[s], k) + ins[s, 0, k].astype(f32) + ins[s, 1, k].astype(f32)).astype(bf16)
        group = []
        for i in range(3):
            to = lax.rem(there[s] + 1 + i, 4)
            group.append(remote(part.at[s, to], mid.at[s, i], m_s.at[s, i], m_r.at[s, i], seconds[s][i]))
        for copy in group:
            copy.start()
        middles.append(group)
    backs = []
    for s in range(2):
        for copy in middles[s]:
            copy.wait()
        total = part[s, there[s]].astype(f32)
        for i in range(3):
            total = total + mid[s, i].astype(f32)
        fin[s] = total.astype(bf16)
        where = piece_of(out, s, here[s], there[s])
        group = [remote(fin.at[s], where, n_s.at[s, i], n_r.at[s, i], seconds[s][i]) for i in range(3)]
        group.append(pltpu.make_async_copy(fin.at[s], where, loc.at[s]))
        for copy in group:
            copy.start()
        backs.append(group)
    rights, lefts = [], []
    for s in range(2):
        t, right, left = here[s], firsts[s][0], firsts[s][2]
        for copy in backs[s]:
            copy.wait()
        to_right, to_left = [], []
        for k in range(4):
            ref = piece_of(out, s, t, k)
            to_right.append(remote(ref, ref, e_s.at[s, k], e_r.at[s, k], right))
            ref = piece_of(out, s, t, 3 - k)
            to_left.append(remote(ref, ref, e_s.at[s, 4 + k], e_r.at[s, 4 + k], left))
        for k in range(4):
            to_right[k].start()
            to_left[k].start()
        rights.append(to_right)
        lefts.append(to_left)
    passed = []
    for k in range(2):
        for s in range(2):
            t, right, left = here[s], firsts[s][0], firsts[s][2]
            rights[s][k].wait()
            ref = piece_of(out, s, t - 1, k)
            copy = remote(ref, ref, w_s.at[s, k], w_r.at[s, k], right)
            copy.start()
            passed.append(copy)
            lefts[s][k].wait()
            ref = piece_of(out, s, t + 1, 3 - k)
            copy = remote(ref, ref, w_s.at[s, 2 + k], w_r.at[s, 2 + k], left)
            copy.start()
            passed.append(copy)
    for s in range(2):
        for copy in rights[s][2:] + lefts[s][2:]:
            copy.wait()
    for copy in passed:
        copy.wait()


def total_over_replicas(g):
    dma = pltpu.SemaphoreType.DMA
    bf16 = jnp.bfloat16
    piece = (HALF, PIECE)
    return pl.pallas_call(
        total_kernel,
        out_shape=jax.ShapeDtypeStruct(g.shape, g.dtype),
        in_specs=vmem_specs(1),
        out_specs=pl.BlockSpec(memory_space=pl.ANY),
        scratch_shapes=[
            pltpu.VMEM((2, 2, 2) + piece, bf16),
            pltpu.VMEM((2, 2, 4) + piece, bf16),
            pltpu.VMEM((2, 2, 2) + piece, bf16),
            pltpu.VMEM((2, 4) + piece, bf16),
            pltpu.VMEM((2, 3) + piece, bf16),
            pltpu.VMEM((2,) + piece, bf16),
        ]
        + [dma((2, 8))] * 2
        + [dma((2, 4))] * 2
        + [dma((2, 3))] * 4
        + [dma((2, 8))] * 2
        + [dma((2, 4))] * 2
        + [dma((2,))],
        compiler_params=pltpu.CompilerParams(
            collective_id=2, has_side_effects=True, vmem_limit_bytes=VMEM_BYTES
        ),
        name="total_over_replicas",
    )(g)


def lane_mask(shape, micro):
    lane = lax.broadcasted_iota(jnp.int32, shape, len(shape) - 1)
    return (lane >= HD) if micro else (lane < HD)


def allowed_block(n0, n2, first_query, queries, keys):
    i = lax.broadcasted_iota(jnp.int32, (queries, keys), 0) + first_query
    j = lax.broadcasted_iota(jnp.int32, (queries, keys), 1)
    row = lax.broadcasted_iota(jnp.int32, (queries, 1), 0) + first_query
    start = jnp.where(row >= n2, n2, jnp.where(row >= n0, n0, 0))
    return (j <= i) & (j >= start)


def scores_of(q, k, micro, allowed):
    zero = jnp.zeros((), jnp.bfloat16)
    q = jnp.where(lane_mask(q.shape, micro), q, zero)
    s = lax.dot_general(q, k, (((1,), (1,)), ((), ())), preferred_element_type=jnp.float32)
    return jnp.where(allowed, s * SCALE, masked_score)


def take(x, entry, start, count):
    return x[pl.ds(start, count), entry].reshape(count * TQ, 2 * HD)


def forward_kernel(bounds, x, q16, o, o16, lse, lse16):
    zero = jnp.zeros((), jnp.bfloat16)
    me = lax.axis_index("replica")

    def attend(q, k, v, micro, first_query):
        allowed = allowed_block(bounds[micro], bounds[2 + micro], first_query, q.shape[0], k.shape[0])
        s = scores_of(q, k, micro, allowed)
        largest = jnp.max(s, axis=-1, keepdims=True)
        e = jnp.exp(s - largest)
        summed = jnp.sum(e, axis=-1, keepdims=True)
        p = (e * (1.0 / summed)).astype(jnp.bfloat16)
        v = jnp.where(lane_mask(v.shape, micro), v, zero)
        return times(p, v), largest + jnp.log(summed)

    per = BQ // TQ
    for b in range(SEQ // BQ):
        count = (b + 1) * per
        q = take(x, 0, b * per, per)
        k = take(x, 1, 0, count)
        v = take(x, 2, 0, count)
        o0, l0 = attend(q, k, v, 0, b * BQ)
        o1, l1 = attend(q, k, v, 1, b * BQ)
        o[pl.ds(b * per, per)] = (o0 + o1).astype(jnp.bfloat16).reshape(per, TQ, 2 * HD)
        lse[pl.ds(b * BQ, BQ)] = jnp.where(lane_mask((BQ, 2 * HD), 0), l0, l1)
    q = q16[...]
    k = take(x, 3, 0, NR)
    v = take(x, 4, 0, NR)
    o0, l0 = attend(q, k, v, 0, me * TQ)
    o1, l1 = attend(q, k, v, 1, me * TQ)
    o16[...] = (o0 + o1).astype(jnp.bfloat16)
    lse16[...] = jnp.where(lane_mask((TQ, 2 * HD), 0), l0, l1)


def vmem_specs(count):
    return [pl.BlockSpec(memory_space=pltpu.VMEM)] * count


def attention_forward(bounds, x, q16):
    f32, bf16 = jnp.float32, jnp.bfloat16
    return pl.pallas_call(
        forward_kernel,
        out_shape=[
            jax.ShapeDtypeStruct((NR, TQ, 2 * HD), bf16),
            jax.ShapeDtypeStruct((TQ, 2 * HD), bf16),
            jax.ShapeDtypeStruct((SEQ, 2 * HD), f32),
            jax.ShapeDtypeStruct((TQ, 2 * HD), f32),
        ],
        in_specs=[pl.BlockSpec(memory_space=pltpu.SMEM)] + vmem_specs(2),
        out_specs=vmem_specs(4),
        compiler_params=pltpu.CompilerParams(vmem_limit_bytes=VMEM_BYTES),
        cost_estimate=cost(5),
        name="attention_forward",
    )(bounds, x, q16)


def backward_kernel(bounds, x, q16, lse, lse16, do, do16, dx, dq16, dk, dv):
    zero = jnp.zeros((), jnp.bfloat16)
    me = lax.axis_index("replica")
    bf16 = jnp.bfloat16

    def pull(q, k, v, grad, logs, micro, first_query):
        allowed = allowed_block(bounds[micro], bounds[2 + micro], first_query, q.shape[0], k.shape[0])
        s = scores_of(q, k, micro, allowed)
        soft = jnp.exp(s - logs[:, micro * HD : micro * HD + 1])
        grad = jnp.where(lane_mask(grad.shape, micro), grad, zero)
        dp = times_transposed(grad, v)
        along = jnp.sum(soft * dp, axis=-1, keepdims=True)
        ds = (soft * (dp - along)).astype(bf16)
        q = jnp.where(lane_mask(q.shape, micro), q, zero)
        k = jnp.where(lane_mask(k.shape, micro), k, zero)
        return times(ds, k), outer_sum(ds, q), outer_sum(soft.astype(bf16), grad)

    per = BQ // TQ
    for b in reversed(range(SEQ // BQ)):
        count = (b + 1) * per
        q = take(x, 0, b * per, per)
        k = take(x, 1, 0, count)
        v = take(x, 2, 0, count)
        grad = do[pl.ds(b * per, per)].reshape(BQ, 2 * HD)
        logs = lse[pl.ds(b * BQ, BQ)]
        q0, k0, v0 = pull(q, k, v, grad, logs, 0, b * BQ)
        q1, k1, v1 = pull(q, k, v, grad, logs, 1, b * BQ)
        dx[pl.ds(b * per, per), 0] = ((q0 + q1) * SCALE).astype(bf16).reshape(per, TQ, 2 * HD)
        keys = pl.ds(0, (b + 1) * BQ)
        if b == SEQ // BQ - 1:
            dk[keys] = k0 + k1
            dv[keys] = v0 + v1
        else:
            dk[keys] += k0 + k1
            dv[keys] += v0 + v1
    dx[:, 1] = (dk[...] * SCALE).astype(bf16).reshape(NR, TQ, 2 * HD)
    dx[:, 2] = dv[...].astype(bf16).reshape(NR, TQ, 2 * HD)
    q = q16[...]
    k = take(x, 3, 0, NR)
    v = take(x, 4, 0, NR)
    q0, k0, v0 = pull(q, k, v, do16[...], lse16[...], 0, me * TQ)
    q1, k1, v1 = pull(q, k, v, do16[...], lse16[...], 1, me * TQ)
    dq16[...] = ((q0 + q1) * SCALE).astype(bf16)
    dx[:, 3] = ((k0 + k1) * SCALE).astype(bf16).reshape(NR, TQ, 2 * HD)
    dx[:, 4] = (v0 + v1).astype(bf16).reshape(NR, TQ, 2 * HD)


def attention_backward(bounds, x, q16, lse, lse16, do, do16):
    f32, bf16 = jnp.float32, jnp.bfloat16
    return pl.pallas_call(
        backward_kernel,
        out_shape=[
            jax.ShapeDtypeStruct((NR, 5, TQ, 2 * HD), bf16),
            jax.ShapeDtypeStruct((TQ, 2 * HD), bf16),
        ],
        in_specs=[pl.BlockSpec(memory_space=pltpu.SMEM)] + vmem_specs(6),
        out_specs=vmem_specs(2),
        scratch_shapes=[pltpu.VMEM((SEQ, 2 * HD), f32), pltpu.VMEM((SEQ, 2 * HD), f32)],
        compiler_params=pltpu.CompilerParams(vmem_limit_bytes=VMEM_BYTES),
        cost_estimate=cost(8),
        name="attention_backward",
    )(bounds, x, q16, lse, lse16, do, do16)


QKV = 3 * D
ENTER_BLOCK, LEAVE_BLOCK, BACK_ENTER_BLOCK = 1664, 2176, 640
LEFT_AT, LEFT_WIDTH = (0, 384, 768, 1152), 2304
EARLY_AT, EARLY_WIDTH = (0, 4352, 5504), 6656
LATE_WIDTH = 3328
SMALL = 1152


def low_lanes(shape):
    return lane_mask(shape, 0)


def to_blocks(upper, lower, odd):
    half = low_lanes(upper.shape)
    if odd:
        return jnp.where(half, pltpu.roll(upper, HD, 1), lower)
    return jnp.where(half, upper, pltpu.roll(lower, HD, 1))


def from_blocks(first, second):
    half = low_lanes(first.shape)
    upper = jnp.where(half, first, pltpu.roll(second, HD, 1))
    return upper, jnp.where(half, pltpu.roll(first, HD, 1), second)


def lines(start, count):
    return pl.ds(start, count)


def enter_kernel(x, gains, biases, w, message, q16, act, mixed):
    i = pl.program_id(0)

    @pl.when(i == 0)
    def _():
        normed, _, _ = layer_norm(x[...].astype(jnp.float32), gains[0:1], biases[0:1])
        act[...] = normed.astype(jnp.bfloat16)

    mixed[i] = times(act[...], w[...])

    @pl.when(i == pl.num_programs(0) - 1)
    def _():
        for b in range(3 * H):
            kind, head = divmod(b, H)
            i, t = divmod(b // 2, ENTER_BLOCK // 128)
            part = pl.ds(t * 128, 128)
            block = to_blocks(mixed[i, 0:TQ, part], mixed[i, TQ : 2 * TQ, part], b % 2)
            if kind != 1:
                row = 1 if kind == 0 else 2
                shift = biases[row : row + 1, head * HD : (head + 1) * HD]
                block = block + jnp.concatenate([shift, shift], axis=1)
            block = block.astype(jnp.bfloat16)
            if head < H - 1:
                message[head, kind * TQ : (kind + 1) * TQ] = block
            elif kind == 0:
                q16[...] = block
            else:
                for p in range(NR):
                    message[p, (kind + 2) * TQ : (kind + 3) * TQ] = block


def fixed(shape):
    return pl.BlockSpec(shape, lambda i: (0,) * len(shape))


def enter(x, gains, biases, w_qkv):
    bf16 = jnp.bfloat16
    steps = -(-QKV // ENTER_BLOCK)
    shapes = [(NR, 5 * TQ, 2 * HD), (TQ, 2 * HD), (2 * TQ, D)]
    return pl.pallas_call(
        enter_kernel,
        grid=(steps,),
        out_shape=[jax.ShapeDtypeStruct(shape, bf16) for shape in shapes],
        in_specs=[
            fixed(x.shape),
            fixed(gains.shape),
            fixed(biases.shape),
            pl.BlockSpec((D, ENTER_BLOCK), lambda i: (0, i)),
        ],
        out_specs=[fixed(shape) for shape in shapes],
        scratch_shapes=[pltpu.VMEM((steps, 2 * TQ, ENTER_BLOCK), jnp.float32)],
        compiler_params=pltpu.CompilerParams(vmem_limit_bytes=VMEM_BYTES),
        cost_estimate=cost(5),
        name="enter",
    )(x, gains, biases, w_qkv)


CURVE = 0.044715
ROOT = 0.7978845608028654


def leave_kernel(
    x, o, o16, act1, gains, biases, up_shift, w_out, w_up, w_down, result, resid, pre, lefts, act2, total
):
    i = pl.program_id(0)
    bf16 = jnp.bfloat16

    @pl.when(i == 0)
    def _():
        tiles = []
        for t in range(H // 2 + 1):
            first = o[2 * t] if 2 * t < H - 1 else o16[...]
            second = o[2 * t + 1] if 2 * t + 1 < H - 1 else o16[...]
            upper, lower = from_blocks(first.astype(jnp.float32), second.astype(jnp.float32))
            tiles.append(jnp.concatenate([upper, lower], axis=0))
        attended = jnp.concatenate(tiles, axis=1)[:, :D].astype(bf16)
        r = x[...].astype(jnp.float32) + times(attended, w_out[...]) + biases[3:4]
        resid[...] = r
        normed, _, _ = layer_norm(r, gains[1:2], biases[4:5])
        act2[...] = normed.astype(bf16)
        for s in range(4):
            part = slice(s * 272, (s + 1) * 272)
            for at, value in zip(LEFT_AT, (act1, attended, act2)):
                lefts[s, :, at : at + 272] = value[:, part]
        total[...] = r + biases[5:6]

    u = times(act2[...], w_up[...]) + up_shift[...]
    pre[...] = u
    g = (0.5 * u * (1.0 + jnp.tanh(ROOT * (u + CURVE * u * u * u)))).astype(bf16)
    for s in range(2):
        lefts[2 * i + s, :, LEFT_AT[3] : LEFT_AT[3] + D] = g[:, s * D : (s + 1) * D]
    total[...] += times(g, w_down[...])

    @pl.when(i == pl.num_programs(0) - 1)
    def _():
        result[...] = total[...].astype(bf16)


def leave(x, o, o16, act1, gains, biases, up_shift, weights):
    _, w_out, w_up, w_down = weights
    f32, bf16 = jnp.float32, jnp.bfloat16
    rows = 2 * TQ
    return pl.pallas_call(
        leave_kernel,
        grid=(FF // LEAVE_BLOCK,),
        out_shape=[
            jax.ShapeDtypeStruct((rows, D), bf16),
            jax.ShapeDtypeStruct((rows, D), f32),
            jax.ShapeDtypeStruct((rows, FF), f32),
            jax.ShapeDtypeStruct((4, rows, LEFT_WIDTH), bf16),
        ],
        in_specs=[
            fixed(x.shape),
            fixed(o.shape),
            fixed(o16.shape),
            fixed(act1.shape),
            fixed(gains.shape),
            fixed(biases.shape),
            pl.BlockSpec((1, LEAVE_BLOCK), lambda i: (0, i)),
            fixed(w_out.shape),
            pl.BlockSpec((D, LEAVE_BLOCK), lambda i: (0, i)),
            pl.BlockSpec((LEAVE_BLOCK, D), lambda i: (i, 0)),
        ],
        out_specs=[
            fixed((rows, D)),
            fixed((rows, D)),
            pl.BlockSpec((rows, LEAVE_BLOCK), lambda i: (0, i)),
            fixed((4, rows, LEFT_WIDTH)),
        ],
        scratch_shapes=[pltpu.VMEM((rows, D), bf16), pltpu.VMEM((rows, D), f32)],
        compiler_params=pltpu.CompilerParams(vmem_limit_bytes=VMEM_BYTES),
        cost_estimate=cost(12),
        name="leave",
    )(x, o, o16, act1, gains, biases, up_shift, w_out, w_up, w_down)


def column_sum(value):
    return jnp.sum(value, axis=0, keepdims=True)


def back_leave_kernel(
    dy, resid, pre, gains, w_out, w_up, w_down, early, grad_resid, do, do16, sums, total
):
    i = pl.program_id(0)
    f32, bf16 = jnp.float32, jnp.bfloat16

    @pl.when(i == 0)
    def _():
        total[...] = jnp.zeros_like(total)

    u = pre[...]
    grad_hidden = times_transposed(dy[...], w_down[...])
    t = jnp.tanh(ROOT * (u + CURVE * u * u * u))
    slope = 0.5 * (1.0 + t) + 0.5 * u * (1.0 - t * t) * (ROOT * (1.0 + 3.0 * CURVE * u * u))
    du = (grad_hidden * slope).astype(bf16)
    early[:, pl.ds(pl.multiple_of(i * LEAVE_BLOCK, 128), LEAVE_BLOCK)] = du
    du_sum = column_sum(du.astype(f32))
    for s in range(2):
        sums[pl.ds(4 + 2 * i + s, 1), 0:D] = du_sum[:, s * D : (s + 1) * D]
    total[...] += times_transposed(du, w_up[...])

    @pl.when(i == pl.num_programs(0) - 1)
    def _():
        da2 = total[...]
        _, normed, inverse = layer_norm(resid[...], gains[1:2], 0.0)
        dr = dy[...].astype(f32) + norm_back(da2, normed, inverse, gains[1:2])
        grad_resid[...] = dr
        db = dr.astype(bf16)
        for at in EARLY_AT[1:]:
            early[:, at + 1024 : at + 1152] = jnp.zeros((2 * TQ, 128), bf16)
        early[:, EARLY_AT[1] : EARLY_AT[1] + D] = db
        early[:, EARLY_AT[2] : EARLY_AT[2] + D] = dy[...]
        sums[0:1, 0:D] = column_sum(da2 * normed)
        sums[1:2, 0:D] = column_sum(da2)
        sums[2:3, 0:D] = column_sum(db.astype(f32))
        sums[3:4, 0:D] = column_sum(dy[...].astype(f32))
        heads = times_transposed(db, w_out[...])
        heads = jnp.concatenate([heads, jnp.zeros((2 * TQ, HD), f32)], axis=1)
        for b in range(H):
            tile = heads[:, (b // 2) * 128 : (b // 2 + 1) * 128]
            block = to_blocks(tile[0:TQ], tile[TQ : 2 * TQ], b % 2).astype(bf16)
            if b < H - 1:
                do[b] = block
            else:
                do16[...] = block


def back_leave(dy, resid, pre, gains, weights):
    _, w_out, w_up, w_down = weights
    f32, bf16 = jnp.float32, jnp.bfloat16
    rows = 2 * TQ
    shapes = [(rows, EARLY_WIDTH), (rows, D), (NR, TQ, 2 * HD), (TQ, 2 * HD), (8, SMALL)]
    types = [bf16, f32, bf16, bf16, f32]
    return pl.pallas_call(
        back_leave_kernel,
        grid=(FF // LEAVE_BLOCK,),
        out_shape=[jax.ShapeDtypeStruct(shape, t) for shape, t in zip(shapes, types)],
        in_specs=[
            fixed((rows, D)),
            fixed((rows, D)),
            pl.BlockSpec((rows, LEAVE_BLOCK), lambda i: (0, i)),
            fixed(gains.shape),
            fixed(w_out.shape),
            pl.BlockSpec((D, LEAVE_BLOCK), lambda i: (0, i)),
            pl.BlockSpec((LEAVE_BLOCK, D), lambda i: (i, 0)),
        ],
        out_specs=[fixed(shape) for shape in shapes],
        scratch_shapes=[pltpu.VMEM((rows, D), f32)],
        compiler_params=pltpu.CompilerParams(vmem_limit_bytes=VMEM_BYTES),
        cost_estimate=cost(14),
        name="back_leave",
    )(dy, resid, pre, gains, w_out, w_up, w_down)


def back_enter_kernel(x, back, dq16, grad_resid, before, gains, w, late, grad_in, sums, parts):
    i = pl.program_id(0)
    f32, bf16 = jnp.float32, jnp.bfloat16

    @pl.when(i == 0)
    def _():
        def last(kind):
            total = back[0, (kind + 2) * TQ : (kind + 3) * TQ].astype(f32)
            for p in range(1, NR):
                total = total + back[p, (kind + 2) * TQ : (kind + 3) * TQ].astype(f32)
            return total

        def block(b):
            kind, head = divmod(b, H)
            if head < H - 1:
                return back[head, kind * TQ : (kind + 1) * TQ].astype(f32)
            return dq16[...].astype(f32) if kind == 0 else last(kind)

        for t in range(3 * H // 2 + 1):
            first = block(2 * t)
            second = block(2 * t + 1) if 2 * t + 1 < 3 * H else jnp.zeros_like(first)
            upper, lower = from_blocks(first, second)
            late[0:TQ, t * 128 : (t + 1) * 128] = upper.astype(bf16)
            late[TQ : 2 * TQ, t * 128 : (t + 1) * 128] = lower.astype(bf16)

    parts[i] = times_transposed(late[:, 0:QKV], w[...])

    @pl.when(i == pl.num_programs(0) - 1)
    def _():
        da1 = jnp.concatenate([parts[k] for k in range(parts.shape[0])], axis=1)[:, :D]
        _, normed, inverse = layer_norm(x[...].astype(f32), gains[0:1], 0.0)
        dx = grad_resid[...] + norm_back(da1, normed, inverse, gains[0:1])
        grad_in[...] = dx.astype(bf16)
        sums[...] = jnp.zeros_like(sums)
        sums[0:1, 0:D] = column_sum(da1 * normed)
        sums[1:2, 0:D] = column_sum(da1)
        sums[2:3, 0:D] = column_sum(late[:, 0:D].astype(f32))
        sums[3:4, 0:D] = column_sum(late[:, 2 * D : QKV].astype(f32))
        sums[4:12, 0:D] = before[:, 0:D]


def back_enter(x, back, dq16, grad_resid, before, gains, w_qkv):
    f32, bf16 = jnp.float32, jnp.bfloat16
    rows = 2 * TQ
    steps = -(-D // BACK_ENTER_BLOCK)
    return pl.pallas_call(
        back_enter_kernel,
        grid=(steps,),
        out_shape=[
            jax.ShapeDtypeStruct((rows, LATE_WIDTH), bf16),
            jax.ShapeDtypeStruct((rows, D), bf16),
            jax.ShapeDtypeStruct((16, SMALL), f32),
        ],
        in_specs=[
            fixed(x.shape),
            fixed(back.shape),
            fixed(dq16.shape),
            fixed(grad_resid.shape),
            fixed(before.shape),
            fixed(gains.shape),
            pl.BlockSpec((BACK_ENTER_BLOCK, QKV), lambda i: (i, 0)),
        ],
        out_specs=[fixed((rows, LATE_WIDTH)), fixed((rows, D)), fixed((16, SMALL))],
        scratch_shapes=[pltpu.VMEM((steps, rows, BACK_ENTER_BLOCK), f32)],
        compiler_params=pltpu.CompilerParams(vmem_limit_bytes=VMEM_BYTES),
        cost_estimate=cost(5),
        name="back_enter",
    )(x, back, dq16, grad_resid, before, gains, w_qkv)


AT_OUT, AT_UP, AT_DOWN, DOWN_STEP = 3328, 4480, 8832, 1152


def products_kernel(
    l0, l1, l2, l3, e0, e1, e2, late, small, out, lefts, early, mixed, got, loc, late_s, late_r, small_s, small_r
):
    bf16 = jnp.bfloat16
    rows = 2 * TQ
    j = lax.axis_index("shard")
    xj = lax.rem(j + 2, 4)
    cj = j + 1 - 2 * lax.rem(j, 2)
    places = [{"shard": xj}, {"shard": cj}, {"shard": lax.rem(cj + 2, 4)}]
    greet(places)

    def slot(ref, k):
        return ref.at[pl.ds(k * rows, rows)]

    across = remote(late, slot(mixed, 1), late_s.at[0], late_r.at[0], places[0])
    across.start()
    beside = remote(late, slot(mixed, 2), late_s.at[1], late_r.at[1], places[1])
    beside.start()
    early_relay = remote(e1, slot(early, 3), late_s.at[3], late_r.at[3], places[1])
    early_relay.start()
    smalls = [remote(small, got.at[k], small_s.at[k], small_r.at[k], places[k]) for k in range(3)]
    for copy in smalls:
        copy.start()
    loads = [pltpu.make_async_copy(late, slot(mixed, 0), loc.at[0])]
    loads.append(pltpu.make_async_copy(l0.at[j], slot(lefts, 0), loc.at[1]))
    for k, ref in enumerate((l1, l2, l3)):
        loads.append(pltpu.make_async_copy(ref, slot(lefts, k + 1), loc.at[2 + k]))
    for k, ref in enumerate((e0, e1, e2)):
        loads.append(pltpu.make_async_copy(ref, slot(early, k), loc.at[5 + k]))
    for copy in loads:
        copy.start()
    for copy in loads:
        copy.wait()
    early_relay.wait()

    def stripe(left_at, right, right_at, at, columns, width):
        @pl.loop(0, columns // width)
        def _(i):
            take_at = pl.ds(pl.multiple_of(right_at + i * width, 128), width)
            put_at = pl.ds(pl.multiple_of(at + i * width, 128), width)
            product = outer_sum(lefts[:, left_at : left_at + 272], right[:, take_at])
            out[0:272, put_at] = product.astype(bf16)

    stripe(LEFT_AT[2], early, EARLY_AT[0], AT_UP, FF, 2176)
    across.wait()
    relay = remote(slot(mixed, 1), slot(mixed, 3), late_s.at[2], late_r.at[2], places[1])
    relay.start()
    out[0:272, AT_OUT:AT_UP] = outer_sum(
        lefts[:, LEFT_AT[1] : LEFT_AT[1] + 272], early[:, EARLY_AT[1] : EARLY_AT[2]]
    ).astype(bf16)
    for s in range(4):
        at = AT_DOWN + s * DOWN_STEP
        first = LEFT_AT[3] + s * 272
        out[0:272, at : at + DOWN_STEP] = outer_sum(
            lefts[:, first : first + 272], early[:, EARLY_AT[2] : EARLY_WIDTH]
        ).astype(bf16)
    beside.wait()
    relay.wait()
    stripe(LEFT_AT[0], mixed, 0, 0, LATE_WIDTH, 1664)
    for copy in smalls:
        copy.wait()
    filled = AT_DOWN + 4 * DOWN_STEP
    out[0:272, filled:] = jnp.zeros((272, NR * PIECE - filled), bf16)
    out[272:RED_ROWS] = jnp.zeros((RED_ROWS - 272, NR * PIECE), bf16)
    out[272:RED_ROWS, 0:SMALL] = (small[...] + got[0] + got[1] + got[2]).astype(bf16)


def products(lefts, early, late, small):
    dma = pltpu.SemaphoreType.DMA
    f32, bf16 = jnp.float32, jnp.bfloat16
    anywhere = pl.BlockSpec(memory_space=pl.ANY)
    return pl.pallas_call(
        products_kernel,
        out_shape=jax.ShapeDtypeStruct((RED_ROWS, NR * PIECE), bf16),
        in_specs=[anywhere] * 8 + vmem_specs(1),
        out_specs=pl.BlockSpec(memory_space=pltpu.VMEM),
        scratch_shapes=[
            pltpu.VMEM((8 * TQ, LEFT_WIDTH), bf16),
            pltpu.VMEM((8 * TQ, EARLY_WIDTH), bf16),
            pltpu.VMEM((8 * TQ, LATE_WIDTH), bf16),
            pltpu.VMEM((3, 16, SMALL), f32),
            dma((8,)),
            dma((4,)), dma((4,)), dma((3,)), dma((3,)),
        ],
        compiler_params=pltpu.CompilerParams(
            collective_id=5, has_side_effects=True, vmem_limit_bytes=VMEM_BYTES
        ),
        name="products",
    )(*lefts, *early, late, small)


def widen_kernel(g, qkv, out, up, down):
    f32 = jnp.float32
    qkv[...] = g[:, 0:QKV].astype(f32)
    out[...] = g[:, AT_OUT : AT_OUT + D].astype(f32)
    up[...] = g[:, AT_UP : AT_UP + FF].astype(f32)
    for s in range(4):
        at = AT_DOWN + s * DOWN_STEP
        down[s] = g[:, at : at + D].astype(f32)


def widen(g):
    f32 = jnp.float32
    return pl.pallas_call(
        widen_kernel,
        grid=(6,),
        out_shape=[
            jax.ShapeDtypeStruct((272, QKV), f32),
            jax.ShapeDtypeStruct((272, D), f32),
            jax.ShapeDtypeStruct((272, FF), f32),
            jax.ShapeDtypeStruct((4, 272, D), f32),
        ],
        in_specs=[pl.BlockSpec((48, NR * PIECE), lambda i: (i, 0))],
        out_specs=[
            pl.BlockSpec((48, QKV), lambda i: (i, 0)),
            pl.BlockSpec((48, D), lambda i: (i, 0)),
            pl.BlockSpec((48, FF), lambda i: (i, 0)),
            pl.BlockSpec((4, 48, D), lambda i: (0, i, 0)),
        ],
        compiler_params=pltpu.CompilerParams(vmem_limit_bytes=VMEM_BYTES),
        name="widen",
    )(g)


def layer_forward(x, bounds, gains, biases, up_shift, weights):
    message, q16, act1 = enter(x, gains, biases, weights[0])
    whole = swap(message, 3).reshape(NR, 5, TQ, 2 * HD)
    o, o16, lse, lse16 = attention_forward(bounds, whole, q16)
    result, resid, pre, lefts = leave(x, swap(o, 4), o16, act1, gains, biases, up_shift, weights)
    return result, (whole, q16, lse, lse16, resid, pre), lefts


def layer_backward(dy, x, kept, bounds, gains, weights, early_tie=None, late_tie=None):
    whole, q16, lse, lse16, resid, pre = kept
    early, grad_resid, do, do16, sums = back_leave(dy, resid, pre, gains, weights)
    dx, dq16 = attention_backward(bounds, whole, q16, lse, lse16, swap(do, 4), do16)
    dx, early_tie = lax.optimization_barrier((dx, early_tie))
    back = swap(dx.reshape(NR, 5 * TQ, 2 * HD), 3)
    late, grad_in, small = back_enter(x, back, dq16, grad_resid, sums, gains, weights[0])
    grad_in, late_tie = lax.optimization_barrier((grad_in, late_tie))
    return grad_in, early, late, small, early_tie, late_tie


X_ROUTE = [(j, j ^ 2) for j in range(4)]
C_ROUTE = [(j, j ^ 1) for j in range(4)]


CX_ROUTE = [(j, j ^ 3) for j in range(4)]


def everyone(value):
    return value, lax.ppermute(value, "shard", X_ROUTE), lax.ppermute(value, "shard", C_ROUTE)


def own_columns(cut):
    j = lax.axis_index("shard")

    def of(shard):
        return lax.dynamic_index_in_dim(cut, shard, 0, keepdims=False)

    across, beside = lax.rem(j + 2, 4), j + 1 - 2 * lax.rem(j, 2)
    return (
        cut,
        lax.ppermute(of(across), "shard", X_ROUTE),
        lax.ppermute(of(beside), "shard", C_ROUTE),
        lax.ppermute(of(lax.rem(beside + 2, 4)), "shard", CX_ROUTE),
    )


def shards(tokens, cotangent, doc_ids, gains, biases, up_bias, w_qkv, w_out, w_up, w_down):
    is_first = lax.axis_index("section") == 0
    ids = doc_ids[:, 0]
    counts = jnp.stack([jnp.sum((ids == n).astype(jnp.int32), axis=1) for n in (0, 2)])
    counts = jnp.pad(counts, ((0, 6), (0, 126)))
    *weights, counts = gather_weights((w_qkv[0], w_out[0], w_up[0], w_down[0]), counts)
    counts = jnp.sum(counts[:, :2, :2], axis=0)
    bounds = jnp.concatenate([counts[0], SEQ - counts[1]])
    gains, biases = gains[0], biases[0]
    own_in = tokens.reshape(2 * TQ, D)
    own_cot = cotangent.reshape(2 * TQ, D)
    result, _, _ = layer_forward(own_in, bounds, gains, biases, up_bias, weights)
    inbox = lax.ppermute(result, "section", [(0, 1)])
    inputs = jnp.where(is_first, own_in, inbox)
    layer_out, kept, lefts = layer_forward(inputs, bounds, gains, biases, up_bias, weights)
    lefts = own_columns(lefts)
    grad_in, _, _, _, sooner, later = layer_backward(
        own_cot, inputs, kept, bounds, gains, weights, lefts[1:3], lefts[3]
    )
    lefts = (lefts[0], *sooner, later)
    inbox = lax.ppermute(grad_in, "section", [(1, 0)])
    dy = jnp.where(is_first, inbox, own_cot)
    grad_in, early, late, small, _, _ = layer_backward(dy, inputs, kept, bounds, gains, weights)
    summed = total_over_replicas(products(lefts, everyone(early), late, small))
    qkv, out, up, down = widen(summed)
    small = summed[272:RED_ROWS, :D].astype(jnp.float32)
    return (
        layer_out.reshape(1, 2, 1, TQ, D),
        grad_in.reshape(1, 2, 1, TQ, D),
        jnp.stack([small[0], small[4]])[None],
        jnp.stack([small[k] for k in (1, 2, 3, 6, 5, 7)])[None],
        small[8:12].reshape(1, FF),
        qkv[None],
        out[None],
        up[None],
        down.reshape(1, 1088, D),
    )


def solution(mesh):
    placed = (
        P(None, "shard", "replica", None),
        P(None, "shard", "replica", None),
        P(None, "shard", "replica"),
        P("section", None, None),
        P("section", None, None),
        P("section", None),
        P("section", "shard", None),
        P("section", "shard", None),
        P("section", "shard", None),
        P("section", "shard", None),
    )
    return jax.shard_map(
        shards,
        mesh=mesh,
        in_specs=placed,
        out_specs=(
            P("section", None, "shard", "replica", None),
            P("section", None, "shard", "replica", None),
            P("section", None, None),
            P("section", None, None),
            P("section", None),
            P("section", "shard", None),
            P("section", "shard", None),
            P("section", "shard", None),
            P("section", "shard", None),
        ),
        check_vma=False,
    )
```

time: 869 us -> 501 us (0.58)
  local copies, waits for them, and re-layouts: 154 us -> 6.63 us
  matrix products: 99.1 us -> 0 us
  other arithmetic: 51.9 us -> 5.26 us
  blocking collectives: 24.7 us -> 0 us
  Pallas kernels: 481 us -> 457 us
  starting transfers between devices: 23 us -> 9.82 us
  waiting for transfers between devices: 25.2 us -> 12.5 us
    dot_general x18 -> x0, matrix products: 99.1 us -> none  [the longest x7 43.6 us: times(): return jnp.dot(left, right, preferred_element_type=jnp.float32)]
    reshape x19 -> x1, local copies, waits for them, and re-layouts: 47.6 us -> 0.7 us  [shards(): small[8:12].reshape(1, FF)]
    pallas_call x1 -> x11, Pallas kernels: 229 us -> 193 us  [the longest x1 67.9 us: gather_weights(): pl.pallas_call(weights_kernel, out_shape=outs + [jax.ShapeDtypeStruct((NR...]
    pallas_call x8, Pallas kernels: 103 us -> 128 us  [swap(): pl.pallas_call(swap_kernel, out_shape=jax.ShapeDtypeStruct(x.shape, x.dty...]
    all_gather x1 -> x0, blocking collectives: 24.7 us -> none  [shards(): docs = lax.all_gather(doc_ids[:, 0], 'replica', axis=1, tiled=True)]
    concatenate x14 -> x0, local copies, waits for them, and re-layouts: 23.2 us -> none  [the longest x1 11.8 us: shards(): block = jnp.concatenate([terms[0], terms[1], terms[2], down], axis=1)]
    transpose x7 -> x0, local copies, waits for them, and re-layouts: 21.2 us -> none  [the longest x2 13.7 us: heads_last(): blocks.reshape(n, TQ, 2, HD).transpose(2, 1, 0, 3).reshape(2 * TQ, n * HD)]
    slice x12 -> x3, local copies, waits for them, and re-layouts: 20.6 us -> 0.03 us  [the longest x2 0.03 us: shards(): small[k]]
  transfers between devices with their start and end apart: 20 -> 7, of which waited for: 3 -> 2; matrix products, arithmetic and copies ran while one was open for 10% -> 0% of each run, Pallas kernels for 0% -> 24%
where the time goes in v2:
time: 501 us; the launch traced here: 492 us
  Pallas kernels  457 us (91%)
  waiting for transfers between devices  12.5 us (2%)
  starting transfers between devices  9.82 us (2%)
  local copies, waits for them, and re-layouts  6.63 us (1%)
  other arithmetic  5.26 us (1%)
    pallas_call x8, Pallas kernels, swap(): pl.pallas_call(swap_kernel, out_shape=jax.ShapeDtypeStruct(x.shape, x.dty...  128 us
    pallas_call x1, Pallas kernels, total_over_replicas(): pl.pallas_call(total_kernel, out_shape=jax.ShapeDtypeStruct(g.shape, g.dt...  104 us
    pallas_call x1, Pallas kernels, gather_weights(): pl.pallas_call(weights_kernel, out_shape=outs + [jax.ShapeDtypeStruct((NR...  67.9 us
    pallas_call x2, Pallas kernels, back_leave(): pl.pallas_call(back_leave_kernel, grid=(FF // LEAVE_BLOCK,), out_shape=[j...  31.4 us
    pallas_call x1, Pallas kernels, products(): pl.pallas_call(products_kernel, out_shape=jax.ShapeDtypeStruct((RED_ROWS,...  31.2 us
    pallas_call x2, Pallas kernels, leave(): pl.pallas_call(leave_kernel, grid=(FF // LEAVE_BLOCK,), out_shape=[jax.Sh...  25.5 us
    pallas_call x2, Pallas kernels, attention_backward(): pl.pallas_call(backward_kernel, out_shape=[jax.ShapeDtypeStruct((NR, 5, T...  19.4 us
    pallas_call x2, Pallas kernels, back_enter(): pl.pallas_call(back_enter_kernel, grid=(steps,), out_shape=[jax.ShapeDtyp...  16.1 us
  transfers between devices with their start and end apart: 7, of which 2 were waited for; matrix products, arithmetic and copies ran while one was open for 0% of the time, Pallas kernels for 24%

profile of v2, /device:TPU:0, one launch (start us, length us, event | category | flops | bytes accessed | tf_op | source)
XLA Modules:
  0.0 492.4 jit_solution(7355471776516000858)
XLA Ops:
  3.5 67.9 %gather_weights.1 = (bf16[1088,3264]{1,0:T(8,128)(2,1)}, bf16[1088,1088]{1,0:T(8,128)(2,1)}, bf16[1088,4352]{1,0:T(8,128)(2,1)}, bf16[4352,1088]{1,0:T(8,128)(2,1)}, s32[16,8,128]{2,1,0:T(8,128)}) custom-call(bf16[272,3264]{1,0:T(8,128)(2,1)} %bitcast.50, bf16[272,1088]{1,0:T(8,128)(2,1)} %bitcast.58, bf16[272,4352]{1,0:T(8,128)(2,1)} %bitcast.49, ...), custom_call_target="tpu_custom_call" | custom-call | tf_op jit(solution)/shard_map/gather_weights/pallas_call | solution.py:258
  72.3 5.7 %enter.2 = (bf16[16,320,128]{2,1,0:T(8,128)(2,1)}, bf16[64,128]{1,0:T(8,128)(2,1)}, bf16[128,1088]{1,0:T(8,128)(2,1)}) custom-call(bf16[128,1088]{1,0:T(8,128)(2,1)} %bitcast.46, f32[2,1088]{1,0:T(2,128)} %bitcast.59, f32[6,1088]{1,0:T(8,128)} %bitcast.54, bf16[1088,3264]{1,0:T(8,128)(2,1)} %get-tuple-element.58.w), custom_call_target="tpu_custom_call" | custom-call | bytes 17500000 | tf_op jit(solution)/shard_map/enter/pallas_call | solution.py:638
  77.9 24.3 %swap.8 = bf16[16,320,128]{2,1,0:T(8,128)(2,1)} custom-call(bf16[16,320,128]{2,1,0:T(8,128)(2,1)} %get-tuple-element.59.x), custom_call_target="tpu_custom_call" | custom-call | bytes 56000000 | tf_op jit(solution)/shard_map/swap/pallas_call | solution.py:109
  102.8 6.2 %attention_forward.2 = (bf16[16,64,128]{2,1,0:T(8,128)(2,1)}, bf16[64,128]{1,0:T(8,128)(2,1)}, f32[1024,128]{1,0:T(8,128)}, f32[64,128]{1,0:T(8,128)}) custom-call(s32[4]{0:T(128)} %pad_add_fusion.1.bounds, bf16[16,5,64,128]{3,2,1,0:T(8,128)(2,1)} %bitcast.45, bf16[64,128]{1,0:T(8,128)(2,1)} %get-tuple-element.60.q16), custom_call_target="tpu_custom_call" | custom-call | bytes 17500000 | tf_op jit(solution)/shard_map/attention_forward/pallas_call | solution.py:490
  109.0 10.4 %swap.9.o = bf16[16,64,128]{2,1,0:T(8,128)(2,1)} custom-call(bf16[16,64,128]{2,1,0:T(8,128)(2,1)} %get-tuple-element.61.x), custom_call_target="tpu_custom_call" | custom-call | bytes 31500000 | tf_op jit(solution)/shard_map/swap/pallas_call | solution.py:109
  119.4 12.8 %leave.2 = (bf16[128,1088]{1,0:T(8,128)(2,1)}, f32[128,1088]{1,0:T(8,128)}, f32[128,4352]{1,0:T(8,128)}, bf16[4,128,2304]{2,1,0:T(8,128)(2,1)}) custom-call(bf16[128,1088]{1,0:T(8,128)(2,1)} %bitcast.47, bf16[16,64,128]{2,1,0:T(8,128)(2,1)} %swap.9.o, bf16[64,128]{1,0:T(8,128)(2,1)} %get-tuple-element.62.o16, bf16[128,1088]{1,0:T(8,128)(2,1)} %get-tuple-element.63.act1, ...), custom_call_target="tpu_custom_call" | custom-call | bytes 42000000 | tf_op jit(solution)/shard_map/leave/pallas_call | solution.py:701
  145.8 18.7 %swap.10 = bf16[16,320,128]{2,1,0:T(8,128)(2,1)} custom-call(bf16[16,320,128]{2,1,0:T(8,128)(2,1)} %get-tuple-element.68.x), custom_call_target="tpu_custom_call" | custom-call | bytes 56000000 | tf_op jit(solution)/shard_map/swap/pallas_call | solution.py:109
  164.4 6.2 %attention_forward.3 = (bf16[16,64,128]{2,1,0:T(8,128)(2,1)}, bf16[64,128]{1,0:T(8,128)(2,1)}, f32[1024,128]{1,0:T(8,128)}, f32[64,128]{1,0:T(8,128)}) custom-call(s32[4]{0:T(128)} %pad_add_fusion.1.bounds, bf16[16,5,64,128]{3,2,1,0:T(8,128)(2,1)} %bitcast.42, bf16[64,128]{1,0:T(8,128)(2,1)} %get-tuple-element.69.q16), custom_call_target="tpu_custom_call" | custom-call | bytes 17500000 | tf_op jit(solution)/shard_map/attention_forward/pallas_call | solution.py:490
  170.6 9.8 %swap.11.o = bf16[16,64,128]{2,1,0:T(8,128)(2,1)} custom-call(bf16[16,64,128]{2,1,0:T(8,128)(2,1)} %get-tuple-element.70.x), custom_call_target="tpu_custom_call" | custom-call | bytes 31500000 | tf_op jit(solution)/shard_map/swap/pallas_call | solution.py:109
  180.5 12.7 %leave.3 = (bf16[128,1088]{1,0:T(8,128)(2,1)}, f32[128,1088]{1,0:T(8,128)}, f32[128,4352]{1,0:T(8,128)}, bf16[4,128,2304]{2,1,0:T(8,128)(2,1)}) custom-call(bf16[128,1088]{1,0:T(8,128)(2,1)} %broadcast_select_fusion.1.x, bf16[16,64,128]{2,1,0:T(8,128)(2,1)} %swap.11.o, bf16[64,128]{1,0:T(8,128)(2,1)} %get-tuple-element.71.o16, ...), custom_call_target="tpu_custom_call" | custom-call | bytes 42000000 | tf_op jit(solution)/shard_map/leave/pallas_call | solution.py:701
  198.3 15.7 %back_leave.2 = (bf16[128,6656]{1,0:T(8,128)(2,1)}, f32[128,1088]{1,0:T(8,128)}, bf16[16,64,128]{2,1,0:T(8,128)(2,1)}, bf16[64,128]{1,0:T(8,128)(2,1)}, f32[8,1152]{1,0:T(8,128)}) custom-call(bf16[128,1088]{1,0:T(8,128)(2,1)} %bitcast.53, f32[128,1088]{1,0:T(8,128)} %get-tuple-element.76.resid, f32[128,4352]{1,0:T(8,128)} %get-tuple-element.77.pre, ...), custom_call_target="tpu_custom_call" | custom-call | bytes 49000000 | tf_op jit(solution)/shard_map/back_leave/pallas_call | solution.py:792
  214.0 10.3 %swap.12.do = bf16[16,64,128]{2,1,0:T(8,128)(2,1)} custom-call(bf16[16,64,128]{2,1,0:T(8,128)(2,1)} %get-tuple-element.78.x), custom_call_target="tpu_custom_call" | custom-call | bytes 31500000 | tf_op jit(solution)/shard_map/swap/pallas_call | solution.py:109
  224.3 9.7 %attention_backward.2 = (bf16[16,5,64,128]{3,2,1,0:T(8,128)(2,1)}, bf16[64,128]{1,0:T(8,128)(2,1)}) custom-call(s32[4]{0:T(128)} %pad_add_fusion.1.bounds, bf16[16,5,64,128]{3,2,1,0:T(8,128)(2,1)} %bitcast.43, bf16[64,128]{1,0:T(8,128)(2,1)} %get-tuple-element.69.q16, f32[1024,128]{1,0:T(8,128)} %get-tuple-element.74.lse, ...), custom_call_target="tpu_custom_call" | custom-call | bytes 28000000 | tf_op jit(solution)/shard_map/attention_backward/pallas_call | solution.py:555
  234.1 22.6 %swap.13.back = bf16[16,320,128]{2,1,0:T(8,128)(2,1)} custom-call(bf16[16,320,128]{2,1,0:T(8,128)(2,1)} %bitcast.51), custom_call_target="tpu_custom_call" | custom-call | bytes 56000000 | tf_op jit(solution)/shard_map/swap/pallas_call | solution.py:109
  256.6 8.0 %back_enter.2 = (bf16[128,3328]{1,0:T(8,128)(2,1)}, bf16[128,1088]{1,0:T(8,128)(2,1)}, f32[16,1152]{1,0:T(8,128)}) custom-call(bf16[128,1088]{1,0:T(8,128)(2,1)} %broadcast_select_fusion.1.x, bf16[16,320,128]{2,1,0:T(8,128)(2,1)} %swap.13.back, bf16[64,128]{1,0:T(8,128)(2,1)} %get-tuple-element.83.dq16, f32[128,1088]{1,0:T(8,128)} %get-tuple-element.84.grad_resid, ...), custom_call_target="tpu_custom_call" | custom-call | bytes 17500000 | tf_op jit(solution)/shard_map/back_enter/pallas_call | solution.py:858
  266.0 8.1 %collective-permute-done.4 = bf16[128,1088]{1,0:T(8,128)(2,1)S(1)} collective-permute-done((bf16[128,1088]{1,0:T(8,128)(2,1)}, bf16[128,1088]{1,0:T(8,128)(2,1)S(1)}, u32[]{:S(2)}, u32[]{:S(2)}) %collective-permute-start.4) | collective-permute-done | bytes 278560 | tf_op jit(solution)/shard_map/ppermute | solution.py:1075
  274.8 15.7 %back_leave.3 = (bf16[128,6656]{1,0:T(8,128)(2,1)}, f32[128,1088]{1,0:T(8,128)}, bf16[16,64,128]{2,1,0:T(8,128)(2,1)}, bf16[64,128]{1,0:T(8,128)(2,1)}, f32[8,1152]{1,0:T(8,128)}) custom-call(bf16[128,1088]{1,0:T(8,128)(2,1)} %broadcast_select_fusion.dy, f32[128,1088]{1,0:T(8,128)} %get-tuple-element.76.resid, f32[128,4352]{1,0:T(8,128)} %get-tuple-element.77.pre, ...), custom_call_target="tpu_custom_call" | custom-call | bytes 49000000 | tf_op jit(solution)/shard_map/back_leave/pallas_call | solution.py:792
  292.7 10.5 %swap.14.do = bf16[16,64,128]{2,1,0:T(8,128)(2,1)} custom-call(bf16[16,64,128]{2,1,0:T(8,128)(2,1)} %get-tuple-element.88.x), custom_call_target="tpu_custom_call" | custom-call | bytes 31500000 | tf_op jit(solution)/shard_map/swap/pallas_call | solution.py:109
  303.2 9.7 %attention_backward.3 = (bf16[16,5,64,128]{3,2,1,0:T(8,128)(2,1)}, bf16[64,128]{1,0:T(8,128)(2,1)}) custom-call(s32[4]{0:T(128)} %pad_add_fusion.1.bounds, bf16[16,5,64,128]{3,2,1,0:T(8,128)(2,1)} %bitcast.44, bf16[64,128]{1,0:T(8,128)(2,1)} %get-tuple-element.69.q16, f32[1024,128]{1,0:T(8,128)} %get-tuple-element.74.lse, ...), custom_call_target="tpu_custom_call" | custom-call | bytes 28000000 | tf_op jit(solution)/shard_map/attention_backward/pallas_call | solution.py:555
  312.9 22.0 %swap.15.back = bf16[16,320,128]{2,1,0:T(8,128)(2,1)} custom-call(bf16[16,320,128]{2,1,0:T(8,128)(2,1)} %bitcast.52), custom_call_target="tpu_custom_call" | custom-call | bytes 56000000 | tf_op jit(solution)/shard_map/swap/pallas_call | solution.py:109
  334.9 8.1 %back_enter.3 = (bf16[128,3328]{1,0:T(8,128)(2,1)}, bf16[128,1088]{1,0:T(8,128)(2,1)}, f32[16,1152]{1,0:T(8,128)}) custom-call(bf16[128,1088]{1,0:T(8,128)(2,1)} %broadcast_select_fusion.1.x, bf16[16,320,128]{2,1,0:T(8,128)(2,1)} %swap.15.back, bf16[64,128]{1,0:T(8,128)(2,1)} %get-tuple-element.91.dq16, f32[128,1088]{1,0:T(8,128)} %get-tuple-element.92.grad_resid, ...), custom_call_target="tpu_custom_call" | custom-call | bytes 17500000 | tf_op jit(solution)/shard_map/back_enter/pallas_call | solution.py:858
  344.8 31.2 %products.1.g = bf16[288,14336]{1,0:T(8,128)(2,1)} custom-call(bf16[4,128,2304]{2,1,0:T(8,128)(2,1)} %get-tuple-element.81.l0, bf16[128,2304]{1,0:T(8,128)(2,1)} %copy-done.5, bf16[128,2304]{1,0:T(8,128)(2,1)} %copy-done.4, bf16[128,2304]{1,0:T(8,128)(2,1)} %copy-done.6, bf16[128,6656]{1,0:T(8,128)(2,1)} %get-tuple-element.98.e0, ...), custom_call_target="tpu_custom_call" | custom-call | tf_op jit(solution)/shard_map/products/pallas_call | solution.py:957
  376.0 103.9 %total_over_replicas.1.g = bf16[288,14336]{1,0:T(8,128)(2,1)} custom-call(bf16[288,14336]{1,0:T(8,128)(2,1)} %products.1.g), custom_call_target="tpu_custom_call" | custom-call | tf_op jit(solution)/shard_map/total_over_replicas/pallas_call | solution.py:401
  480.8 9.2 %widen.1 = (f32[272,3264]{1,0:T(8,128)}, f32[272,1088]{1,0:T(8,128)}, f32[272,4352]{1,0:T(8,128)}, f32[4,272,1088]{2,1,0:T(8,128)}) custom-call(bf16[288,14336]{1,0:T(8,128)(2,1)} %total_over_replicas.1.g), custom_call_target="tpu_custom_call" | custom-call | tf_op jit(solution)/shard_map/widen/pallas_call | solution.py:989
  (46 shorter events, 31.7 us)
Async XLA Ops:
  119.4 19.9 %copy-start = (bf16[2,1,64,1088]{3,2,1,0:T(8,128)(2,1)S(1)}, bf16[2,1,64,1088]{3,2,1,0:T(8,128)(2,1)}, u32[]{:S(2)}) copy-start(bf16[2,1,64,1088]{3,2,1,0:T(8,128)(2,1)} %param.10) | copy-start | bytes 835588
  132.2 7.2 %collective-permute-start = (bf16[128,1088]{1,0:T(8,128)(2,1)}, bf16[128,1088]{1,0:T(8,128)(2,1)S(1)}, u32[]{:S(2)}, u32[]{:S(2)}) collective-permute-start(bf16[128,1088]{1,0:T(8,128)(2,1)} %get-tuple-element.67), channel_id=1, source_target_pairs={{0,64},{1,65},{2,66},{3,67},{4,68},{5,69},{6,70},{7,71},{8,72},{9,... | collective-permute-start | bytes 835592 | tf_op jit(solution)/shard_map/ppermute | solution.py:1067
  194.7 39.3 %collective-permute-start.2 = (bf16[128,2304]{1,0:T(8,128)(2,1)S(1)}, bf16[128,2304]{1,0:T(8,128)(2,1)S(1)}, u32[]{:S(2)}, u32[]{:S(2)}) collective-permute-start(bf16[128,2304]{1,0:T(8,128)(2,1)S(1)} %get-tuple-element.117), channel_id=1, source_target_pairs={{0,16},{16,0},{32,48},{48,32},{1,17},{17,1},{33,49},{49,33},{2,18}... | collective-permute-start | bytes 1769480 | tf_op jit(solution)/shard_map/ppermute | solution.py:1050
  194.8 39.2 %collective-permute-start.1 = (bf16[128,2304]{1,0:T(8,128)(2,1)S(1)}, bf16[128,2304]{1,0:T(8,128)(2,1)S(1)}, u32[]{:S(2)}, u32[]{:S(2)}) collective-permute-start(bf16[128,2304]{1,0:T(8,128)(2,1)S(1)} %get-tuple-element.118), channel_id=1, source_target_pairs={{0,32},{16,48},{32,0},{48,16},{1,33},{17,49},{33,1},{49,17},{2,34}... | collective-permute-start | bytes 1769480 | tf_op jit(solution)/shard_map/ppermute | solution.py:1049
  197.0 67.6 %collective-permute-start.3 = (bf16[128,2304]{1,0:T(8,128)(2,1)S(1)}, bf16[128,2304]{1,0:T(8,128)(2,1)S(1)}, u32[]{:S(2)}, u32[]{:S(2)}) collective-permute-start(bf16[128,2304]{1,0:T(8,128)(2,1)S(1)} %get-tuple-element.116), channel_id=1, source_target_pairs={{0,48},{16,32},{32,16},{48,0},{1,49},{17,33},{33,17},{49,1},{2,50}... | collective-permute-start | bytes 1769480 | tf_op jit(solution)/shard_map/ppermute | solution.py:1051
  234.0 30.6 %copy-start.4 = (bf16[128,2304]{1,0:T(8,128)(2,1)}, bf16[128,2304]{1,0:T(8,128)(2,1)S(1)}, u32[]{:S(2)}) copy-start(bf16[128,2304]{1,0:T(8,128)(2,1)S(1)} %collective-permute-done.2.l2) | copy-start | bytes 1769476
  234.0 30.6 %copy-start.5 = (bf16[128,2304]{1,0:T(8,128)(2,1)}, bf16[128,2304]{1,0:T(8,128)(2,1)S(1)}, u32[]{:S(2)}) copy-start(bf16[128,2304]{1,0:T(8,128)(2,1)S(1)} %collective-permute-done.1.l1) | copy-start | bytes 1769476
  256.6 17.4 %copy-start.3 = (bf16[2,1,64,1088]{3,2,1,0:T(8,128)(2,1)S(1)}, bf16[2,1,64,1088]{3,2,1,0:T(8,128)(2,1)}, u32[]{:S(2)}) copy-start(bf16[2,1,64,1088]{3,2,1,0:T(8,128)(2,1)} %param.11) | copy-start | bytes 835588
  264.6 25.9 %copy-start.6 = (bf16[128,2304]{1,0:T(8,128)(2,1)}, bf16[128,2304]{1,0:T(8,128)(2,1)S(1)}, u32[]{:S(2)}) copy-start(bf16[128,2304]{1,0:T(8,128)(2,1)S(1)} %collective-permute-done.3.l3) | copy-start | bytes 1769476
  264.7 9.4 %collective-permute-start.4 = (bf16[128,1088]{1,0:T(8,128)(2,1)}, bf16[128,1088]{1,0:T(8,128)(2,1)S(1)}, u32[]{:S(2)}, u32[]{:S(2)}) collective-permute-start(bf16[128,1088]{1,0:T(8,128)(2,1)} %get-tuple-element.87), channel_id=1, source_target_pairs={{64,0},{65,1},{66,2},{67,3},{68,4},{69,5},{70,6},{71,7},{72,8},{73... | collective-permute-start | bytes 835592 | tf_op jit(solution)/shard_map/ppermute | solution.py:1075
  290.5 52.5 %collective-permute-start.6 = (bf16[128,6656]{1,0:T(8,128)(2,1)}, bf16[128,6656]{1,0:T(8,128)(2,1)S(1)}, u32[]{:S(2)}, u32[]{:S(2)}) collective-permute-start(bf16[128,6656]{1,0:T(8,128)(2,1)} %get-tuple-element.98.e0), channel_id=1, source_target_pairs={{0,16},{16,0},{32,48},{48,32},{1,17},{17,1},{33,49},{49,33},{2,18}... | collective-permute-start | bytes 5111816 | tf_op jit(solution)/shard_map/ppermute | solution.py:1037
  290.6 52.4 %collective-permute-start.5 = (bf16[128,6656]{1,0:T(8,128)(2,1)}, bf16[128,6656]{1,0:T(8,128)(2,1)S(1)}, u32[]{:S(2)}, u32[]{:S(2)}) collective-permute-start(bf16[128,6656]{1,0:T(8,128)(2,1)} %get-tuple-element.98.e0), channel_id=1, source_target_pairs={{0,32},{16,48},{32,0},{48,16},{1,33},{17,49},{33,1},{49,17},{2,34}... | collective-permute-start | bytes 5111816 | tf_op jit(solution)/shard_map/ppermute | solution.py:1037
  343.0 1.2 copy-start.1
  343.0 1.7 copy-start.2

commit v3 on v2

--- a/solution.py
+++ b/solution.py
@@ -125,13 +125,14 @@
 
 
 W_SHAPES = ((272, 3264), (272, 1088), (272, 4352), (1088, 1088))
-W_CUTS = (1664, 512, 2176, 512)
+W_CUTS = (1408, 512, 1920, 512)
+W_ENDS = (2816, 896, 3712, 896)
 
 
 def weights_kernel(*refs):
     ins, docs, outs, all_docs, held = refs[:4], refs[4], refs[5:9], refs[9], refs[10:14]
-    (own_s, own_r, local, back, xp_s, xp_r, xd_s, xd_r, f_s, f_r) = refs[14:24]
-    (a1_s, a1_r, b1_s, b1_r, a2_s, a2_r, b2_s, b2_r, a3_s, a3_r, b3_s, b3_r, doc1_s, doc1_r, doc2_s, doc2_r) = refs[24:]
+    (own_s, own_r, local, back, xp_s, xp_r, xd_s, xd_r, xe_s, xe_r, f_s, f_r) = refs[14:26]
+    (a1_s, a1_r, b1_s, b1_r, a2_s, a2_r, b2_s, b2_r, a3_s, a3_r, b3_s, b3_r, doc1_s, doc1_r, doc2_s, doc2_r) = refs[26:]
     j = lax.axis_index("shard")
     me = lax.axis_index("replica")
     z, y = me // 4, lax.rem(me, 4)
@@ -149,12 +150,17 @@
     x_pieces, x_directs = [], []
     for a, (r, n) in enumerate(W_SHAPES):
         u = r // 17
-        piece = remote(ins[a].at[rows(me * u, u)], outs[a].at[rows(j * r + me * u, u)], xp_s.at[a], xp_r.at[a], x_place)
+        most = pl.ds(0, W_ENDS[a])
+        piece = remote(ins[a].at[rows(me * u, u), most], outs[a].at[rows(j * r + me * u, u), most], xp_s.at[a], xp_r.at[a], x_place)
         piece.start()
         x_pieces.append(piece)
     for a, (r, n) in enumerate(W_SHAPES):
         u = r // 17
-        direct = remote(ins[a].at[rows(16 * u, u)], outs[a].at[rows(j * r + 16 * u, u)], xd_s.at[a], xd_r.at[a], x_place)
+        most, rest = pl.ds(0, W_ENDS[a]), pl.ds(W_ENDS[a], n - W_ENDS[a])
+        direct = remote(ins[a].at[rows(16 * u, u), most], outs[a].at[rows(j * r + 16 * u, u), most], xd_s.at[a], xd_r.at[a], x_place)
+        direct.start()
+        x_directs.append(direct)
+        direct = remote(ins[a].at[:, rest], outs[a].at[rows(j * r, r), rest], xe_s.at[a], xe_r.at[a], x_place)
         direct.start()
         x_directs.append(direct)
     for a, (r, n) in enumerate(W_SHAPES):
@@ -187,7 +193,7 @@
         x_pieces[a].wait()
         here = rows(xj * r + me * u, u)
         part_a = outs[a].at[here, pl.ds(0, cut)]
-        part_b = outs[a].at[here, pl.ds(cut, n - cut)]
+        part_b = outs[a].at[here, pl.ds(cut, W_ENDS[a] - cut)]
         group = []
         for i in range(3):
             group.append(remote(part_a, part_a, a1_s.at[a, i], a1_r.at[a, i], y_places[i]))
@@ -201,9 +207,9 @@
         return outs[a].at[rows(start, 2 * u), pl.ds(0, W_CUTS[a])]
 
     def column_part(a, first, k):
-        (r, n), u = W_SHAPES[a], W_SHAPES[a][0] // 17
+        r, u = W_SHAPES[a][0], W_SHAPES[a][0] // 17
         start = xj * r + (4 * k + lax.rem(first + 4, 4)) * u
-        return outs[a].at[rows(start, u), pl.ds(W_CUTS[a], n - W_CUTS[a])]
+        return outs[a].at[rows(start, u), pl.ds(W_CUTS[a], W_ENDS[a] - W_CUTS[a])]
 
     heres = []
     for a in range(4):
@@ -243,7 +249,8 @@
             copy.start()
         for copy in rights[1:2] + rights[4:] + lefts[1:2] + lefts[4:] + passed:
             copy.wait()
-        x_directs[a].wait()
+        x_directs[2 * a].wait()
+        x_directs[2 * a + 1].wait()
         whole = outs[a].at[rows(xj * r, r)]
         copy = remote(whole, whole, f_s.at[a], f_r.at[a], c_place)
         copy.start()
@@ -261,7 +268,7 @@
         in_specs=[pl.BlockSpec(memory_space=pl.ANY)] * 4 + vmem_specs(1),
         out_specs=[pl.BlockSpec(memory_space=pl.ANY)] * 4 + vmem_specs(1),
         scratch_shapes=[pltpu.VMEM(shape, jnp.bfloat16) for shape in W_SHAPES]
-        + [dma((4,))] * 10
+        + [dma((4,))] * 12
         + [dma((4, 3))] * 4
         + [dma((4, 4))] * 2
         + [dma((4, 8))] * 2
@@ -273,155 +280,6 @@
         ),
         name="gather_weights",
     )(*weights, docs)
-
-
-def total_kernel(g, out, tr, ins, ad, part, mid, fin, p_s, p_r, q_s, q_r, m_s, m_r, n_s, n_r, e_s, e_r, w_s, w_r, loc):
-    me = lax.axis_index("replica")
-    z, y = me // 4, lax.rem(me, 4)
-    y_places = [{"replica": y_peer(me, d)} for d in (1, 2, 3)]
-    z_places = [{"replica": z_peer(me, d)} for d in (1, 2, 3)]
-    greet(y_places + z_places)
-    f32, bf16 = jnp.float32, jnp.bfloat16
-    firsts, seconds = (y_places, z_places), (z_places, y_places)
-    here, there = (y, z), (z, y)
-
-    def at(side, first, second):
-        first = lax.rem(first + 4, 4)
-        piece = 4 * second + first if side == 0 else 4 * first + second
-        return (pl.ds(side * HALF, HALF), pl.ds(pl.multiple_of(piece * PIECE, 128), PIECE))
-
-    def piece_of(ref, side, first, second):
-        return ref.at[at(side, first, second)]
-
-    def value_of(side, first, second):
-        return g[at(side, first, second)].astype(f32)
-
-    opened, direct, added = [], [], []
-    for s in range(2):
-        t, right, left = here[s], firsts[s][0], firsts[s][2]
-        group = []
-        for k in range(2):
-            group.append(remote(piece_of(g, s, t + 2, k), tr.at[s, 0, k], p_s.at[s, k], p_r.at[s, k], right))
-            group.append(remote(piece_of(g, s, t + 2, k + 2), tr.at[s, 1, k], p_s.at[s, 2 + k], p_r.at[s, 2 + k], left))
-        for copy in group:
-            copy.start()
-        opened.append(group)
-    for s in range(2):
-        t, right, left = here[s], firsts[s][0], firsts[s][2]
-        group = []
-        for k in range(2):
-            group.append(remote(piece_of(g, s, t + 1, k + 2), ins.at[s, 0, k + 2], p_s.at[s, 4 + k], p_r.at[s, 4 + k], right))
-            group.append(remote(piece_of(g, s, t - 1, k), ins.at[s, 1, k], p_s.at[s, 6 + k], p_r.at[s, 6 + k], left))
-        for copy in group:
-            copy.start()
-        direct.append(group)
-    for s in range(2):
-        t, right, left = here[s], firsts[s][0], firsts[s][2]
-        group = []
-        for k in range(2):
-            opened[s][2 * k].wait()
-            ad[s, 0, k] = (tr[s, 0, k].astype(f32) + value_of(s, t + 1, k)).astype(bf16)
-            copy = remote(ad.at[s, 0, k], ins.at[s, 0, k], q_s.at[s, k], q_r.at[s, k], right)
-            copy.start()
-            group.append(copy)
-            opened[s][2 * k + 1].wait()
-            ad[s, 1, k] = (tr[s, 1, k].astype(f32) + value_of(s, t - 1, k + 2)).astype(bf16)
-            copy = remote(ad.at[s, 1, k], ins.at[s, 1, k + 2], q_s.at[s, 2 + k], q_r.at[s, 2 + k], left)
-            copy.start()
-            group.append(copy)
-        added.append(group)
-    middles = []
-    for s in range(2):
-        for copy in direct[s] + added[s]:
-            copy.wait()
-        for k in range(4):
-            part[s, k] = (value_of(s, here[s], k) + ins[s, 0, k].astype(f32) + ins[s, 1, k].astype(f32)).astype(bf16)
-        group = []
-        for i in range(3):
-            to = lax.rem(there[s] + 1 + i, 4)
-            group.append(remote(part.at[s, to], mid.at[s, i], m_s.at[s, i], m_r.at[s, i], seconds[s][i]))
-        for copy in group:
-            copy.start()
-        middles.append(group)
-    backs = []
-    for s in range(2):
-        for copy in middles[s]:
-            copy.wait()
-        total = part[s, there[s]].astype(f32)
-        for i in range(3):
-            total = total + mid[s, i].astype(f32)
-        fin[s] = total.astype(bf16)
-        where = piece_of(out, s, here[s], there[s])
-        group = [remote(fin.at[s], where, n_s.at[s, i], n_r.at[s, i], seconds[s][i]) for i in range(3)]
-        group.append(pltpu.make_async_copy(fin.at[s], where, loc.at[s]))
-        for copy in group:
-            copy.start()
-        backs.append(group)
-    rights, lefts = [], []
-    for s in range(2):
-        t, right, left = here[s], firsts[s][0], firsts[s][2]
-        for copy in backs[s]:
-            copy.wait()
-        to_right, to_left = [], []
-        for k in range(4):
-            ref = piece_of(out, s, t, k)
-            to_right.append(remote(ref, ref, e_s.at[s, k], e_r.at[s, k], right))
-            ref = piece_of(out, s, t, 3 - k)
-            to_left.append(remote(ref, ref, e_s.at[s, 4 + k], e_r.at[s, 4 + k], left))
-        for k in range(4):
-            to_right[k].start()
-            to_left[k].start()
-        rights.append(to_right)
-        lefts.append(to_left)
-    passed = []
-    for k in range(2):
-        for s in range(2):
-            t, right, left = here[s], firsts[s][0], firsts[s][2]
-            rights[s][k].wait()
-            ref = piece_of(out, s, t - 1, k)
-            copy = remote(ref, ref, w_s.at[s, k], w_r.at[s, k], right)
-            copy.start()
-            passed.append(copy)
-            lefts[s][k].wait()
-            ref = piece_of(out, s, t + 1, 3 - k)
-            copy = remote(ref, ref, w_s.at[s, 2 + k], w_r.at[s, 2 + k], left)
-            copy.start()
-            passed.append(copy)
-    for s in range(2):
-        for copy in rights[s][2:] + lefts[s][2:]:
-            copy.wait()
-    for copy in passed:
-        copy.wait()
-
-
-def total_over_replicas(g):
-    dma = pltpu.SemaphoreType.DMA
-    bf16 = jnp.bfloat16
-    piece = (HALF, PIECE)
-    return pl.pallas_call(
-        total_kernel,
-        out_shape=jax.ShapeDtypeStruct(g.shape, g.dtype),
-        in_specs=vmem_specs(1),
-        out_specs=pl.BlockSpec(memory_space=pl.ANY),
-        scratch_shapes=[
-            pltpu.VMEM((2, 2, 2) + piece, bf16),
-            pltpu.VMEM((2, 2, 4) + piece, bf16),
-            pltpu.VMEM((2, 2, 2) + piece, bf16),
-            pltpu.VMEM((2, 4) + piece, bf16),
-            pltpu.VMEM((2, 3) + piece, bf16),
-            pltpu.VMEM((2,) + piece, bf16),
-        ]
-        + [dma((2, 8))] * 2
-        + [dma((2, 4))] * 2
-        + [dma((2, 3))] * 4
-        + [dma((2, 8))] * 2
-        + [dma((2, 4))] * 2
-        + [dma((2,))],
-        compiler_params=pltpu.CompilerParams(
-            collective_id=2, has_side_effects=True, vmem_limit_bytes=VMEM_BYTES
-        ),
-        name="total_over_replicas",
-    )(g)
 
 
 def lane_mask(shape, micro):
@@ -883,16 +741,23 @@
 AT_OUT, AT_UP, AT_DOWN, DOWN_STEP = 3328, 4480, 8832, 1152
 
 
-def products_kernel(
-    l0, l1, l2, l3, e0, e1, e2, late, small, out, lefts, early, mixed, got, loc, late_s, late_r, small_s, small_r
+def weight_sums_kernel(
+    l0, l1, l2, l3, e0, e1, e2, late, small, out,
+    lefts, early, mixed, got, g, tr, ins, ad, part, mid, fin,
+    loc, late_s, late_r, small_s, small_r,
+    p_s, p_r, q_s, q_r, m_s, m_r, n_s, n_r, e_s, e_r, w_s, w_r, last,
 ):
-    bf16 = jnp.bfloat16
+    f32, bf16 = jnp.float32, jnp.bfloat16
     rows = 2 * TQ
     j = lax.axis_index("shard")
+    me = lax.axis_index("replica")
+    z, y = me // 4, lax.rem(me, 4)
     xj = lax.rem(j + 2, 4)
     cj = j + 1 - 2 * lax.rem(j, 2)
     places = [{"shard": xj}, {"shard": cj}, {"shard": lax.rem(cj + 2, 4)}]
-    greet(places)
+    y_places = [{"replica": y_peer(me, d)} for d in (1, 2, 3)]
+    z_places = [{"replica": z_peer(me, d)} for d in (1, 2, 3)]
+    greet(places + y_places + z_places)
 
     def slot(ref, k):
         return ref.at[pl.ds(k * rows, rows)]
@@ -924,53 +789,187 @@
             take_at = pl.ds(pl.multiple_of(right_at + i * width, 128), width)
             put_at = pl.ds(pl.multiple_of(at + i * width, 128), width)
             product = outer_sum(lefts[:, left_at : left_at + 272], right[:, take_at])
-            out[0:272, put_at] = product.astype(bf16)
+            g[0:272, put_at] = product.astype(bf16)
 
     stripe(LEFT_AT[2], early, EARLY_AT[0], AT_UP, FF, 2176)
-    across.wait()
-    relay = remote(slot(mixed, 1), slot(mixed, 3), late_s.at[2], late_r.at[2], places[1])
-    relay.start()
-    out[0:272, AT_OUT:AT_UP] = outer_sum(
+    g[0:272, AT_OUT:AT_UP] = outer_sum(
         lefts[:, LEFT_AT[1] : LEFT_AT[1] + 272], early[:, EARLY_AT[1] : EARLY_AT[2]]
     ).astype(bf16)
     for s in range(4):
         at = AT_DOWN + s * DOWN_STEP
         first = LEFT_AT[3] + s * 272
-        out[0:272, at : at + DOWN_STEP] = outer_sum(
+        g[0:272, at : at + DOWN_STEP] = outer_sum(
             lefts[:, first : first + 272], early[:, EARLY_AT[2] : EARLY_WIDTH]
         ).astype(bf16)
+    filled = AT_DOWN + 4 * DOWN_STEP
+    g[0:272, filled:] = jnp.zeros((272, NR * PIECE - filled), bf16)
+    g[272:RED_ROWS] = jnp.zeros((RED_ROWS - 272, NR * PIECE), bf16)
+
+    firsts, seconds = (y_places, z_places), (z_places, y_places)
+    here, there = (y, z), (z, y)
+
+    def at(side, first, second):
+        piece = 4 * second + lax.rem(first + 4, 4)
+        return (pl.ds(side * HALF, HALF), pl.ds(pl.multiple_of(piece * PIECE, 128), PIECE))
+
+    def piece_of(ref, side, first, second):
+        return ref.at[at(side, first, second)]
+
+    def value_of(side, first, second):
+        return g[at(side, first, second)].astype(f32)
+
+    opened, direct, added = {}, {}, {}
+
+    def open_piece(s, k):
+        t, right, left = here[s], firsts[s][0], firsts[s][2]
+        copy = remote(piece_of(g, s, t + 2, k), tr.at[s, k], p_s.at[s, k], p_r.at[s, k], right if k < 2 else left)
+        copy.start()
+        opened[s, k] = copy
+
+    def direct_piece(s, k):
+        t, right, left = here[s], firsts[s][0], firsts[s][2]
+        if k < 2:
+            copy = remote(piece_of(g, s, t - 1, k), ins.at[s, 1, k], p_s.at[s, 4 + k], p_r.at[s, 4 + k], left)
+        else:
+            copy = remote(piece_of(g, s, t + 1, k), ins.at[s, 0, k], p_s.at[s, 4 + k], p_r.at[s, 4 + k], right)
+        copy.start()
+        direct[s, k] = copy
+
+    def add_piece(s, k):
+        t, right, left = here[s], firsts[s][0], firsts[s][2]
+        opened[s, k].wait()
+        mine = value_of(s, t + 1 if k < 2 else t - 1, k)
+        ad[s, k] = (tr[s, k].astype(f32) + mine).astype(bf16)
+        to, side = (right, 0) if k < 2 else (left, 1)
+        copy = remote(ad.at[s, k], ins.at[s, side, k], q_s.at[s, k], q_r.at[s, k], to)
+        copy.start()
+        added[s, k] = copy
+
+    for k in (1, 2, 3):
+        for s in range(2):
+            open_piece(s, k)
+    for k in (1, 2, 3):
+        for s in range(2):
+            direct_piece(s, k)
+    for k in (1, 2):
+        for s in range(2):
+            add_piece(s, k)
+    across.wait()
+    relay = remote(slot(mixed, 1), slot(mixed, 3), late_s.at[2], late_r.at[2], places[1])
+    relay.start()
     beside.wait()
+    for s in range(2):
+        add_piece(s, 3)
     relay.wait()
     stripe(LEFT_AT[0], mixed, 0, 0, LATE_WIDTH, 1664)
     for copy in smalls:
         copy.wait()
-    filled = AT_DOWN + 4 * DOWN_STEP
-    out[0:272, filled:] = jnp.zeros((272, NR * PIECE - filled), bf16)
-    out[272:RED_ROWS] = jnp.zeros((RED_ROWS - 272, NR * PIECE), bf16)
-    out[272:RED_ROWS, 0:SMALL] = (small[...] + got[0] + got[1] + got[2]).astype(bf16)
-
-
-def products(lefts, early, late, small):
+    g[272:RED_ROWS, 0:SMALL] = (small[...] + got[0] + got[1] + got[2]).astype(bf16)
+    for s in range(2):
+        open_piece(s, 0)
+        direct_piece(s, 0)
+    for s in range(2):
+        add_piece(s, 0)
+
+    middles = []
+    for s in range(2):
+        for k in range(4):
+            direct[s, k].wait()
+            added[s, k].wait()
+            part[s, k] = (value_of(s, here[s], k) + ins[s, 0, k].astype(f32) + ins[s, 1, k].astype(f32)).astype(bf16)
+        group = []
+        for i in range(3):
+            to = lax.rem(there[s] + 1 + i, 4)
+            group.append(remote(part.at[s, to], mid.at[s, i], m_s.at[s, i], m_r.at[s, i], seconds[s][i]))
+        for copy in group:
+            copy.start()
+        middles.append(group)
+    backs = []
+    for s in range(2):
+        for copy in middles[s]:
+            copy.wait()
+        total = part[s, there[s]].astype(f32)
+        for i in range(3):
+            total = total + mid[s, i].astype(f32)
+        fin[s] = total.astype(bf16)
+        where = piece_of(out, s, here[s], there[s])
+        group = [remote(fin.at[s], where, n_s.at[s, i], n_r.at[s, i], seconds[s][i]) for i in range(3)]
+        group.append(pltpu.make_async_copy(fin.at[s], where, last.at[s]))
+        for copy in group:
+            copy.start()
+        backs.append(group)
+    to_rights, to_lefts = [], []
+    for s in range(2):
+        t, right, left = here[s], firsts[s][0], firsts[s][2]
+        for copy in backs[s]:
+            copy.wait()
+        to_right, to_left = [], []
+        for k in range(4):
+            ref = piece_of(out, s, t, k)
+            to_right.append(remote(ref, ref, e_s.at[s, k], e_r.at[s, k], right))
+            ref = piece_of(out, s, t, 3 - k)
+            to_left.append(remote(ref, ref, e_s.at[s, 4 + k], e_r.at[s, 4 + k], left))
+        for k in range(4):
+            to_right[k].start()
+            to_left[k].start()
+        to_rights.append(to_right)
+        to_lefts.append(to_left)
+    passed = []
+    for k in range(2):
+        for s in range(2):
+            t, right, left = here[s], firsts[s][0], firsts[s][2]
+            to_rights[s][k].wait()
+            ref = piece_of(out, s, t - 1, k)
+            copy = remote(ref, ref, w_s.at[s, k], w_r.at[s, k], right)
+            copy.start()
+            passed.append(copy)
+            to_lefts[s][k].wait()
+            ref = piece_of(out, s, t + 1, 3 - k)
+            copy = remote(ref, ref, w_s.at[s, 2 + k], w_r.at[s, 2 + k], left)
+            copy.start()
+            passed.append(copy)
+    for s in range(2):
+        for copy in to_rights[s][2:] + to_lefts[s][2:]:
+            copy.wait()
+    for copy in passed:
+        copy.wait()
+
+
+def weight_sums(lefts, early, late, small):
     dma = pltpu.SemaphoreType.DMA
     f32, bf16 = jnp.float32, jnp.bfloat16
     anywhere = pl.BlockSpec(memory_space=pl.ANY)
+    piece = (HALF, PIECE)
     return pl.pallas_call(
-        products_kernel,
+        weight_sums_kernel,
         out_shape=jax.ShapeDtypeStruct((RED_ROWS, NR * PIECE), bf16),
         in_specs=[anywhere] * 8 + vmem_specs(1),
-        out_specs=pl.BlockSpec(memory_space=pltpu.VMEM),
+        out_specs=anywhere,
         scratch_shapes=[
             pltpu.VMEM((8 * TQ, LEFT_WIDTH), bf16),
             pltpu.VMEM((8 * TQ, EARLY_WIDTH), bf16),
             pltpu.VMEM((8 * TQ, LATE_WIDTH), bf16),
             pltpu.VMEM((3, 16, SMALL), f32),
+            pltpu.VMEM((RED_ROWS, NR * PIECE), bf16),
+            pltpu.VMEM((2, 4) + piece, bf16),
+            pltpu.VMEM((2, 2, 4) + piece, bf16),
+            pltpu.VMEM((2, 4) + piece, bf16),
+            pltpu.VMEM((2, 4) + piece, bf16),
+            pltpu.VMEM((2, 3) + piece, bf16),
+            pltpu.VMEM((2,) + piece, bf16),
             dma((8,)),
             dma((4,)), dma((4,)), dma((3,)), dma((3,)),
-        ],
+        ]
+        + [dma((2, 8))] * 2
+        + [dma((2, 4))] * 2
+        + [dma((2, 3))] * 4
+        + [dma((2, 8))] * 2
+        + [dma((2, 4))] * 2
+        + [dma((2,))],
         compiler_params=pltpu.CompilerParams(
-            collective_id=5, has_side_effects=True, vmem_limit_bytes=VMEM_BYTES
+            collective_id=2, has_side_effects=True, vmem_limit_bytes=VMEM_BYTES
         ),
-        name="products",
+        name="weight_sums",
     )(*lefts, *early, late, small)
 
 
@@ -1075,7 +1074,7 @@
     inbox = lax.ppermute(grad_in, "section", [(1, 0)])
     dy = jnp.where(is_first, inbox, own_cot)
     grad_in, early, late, small, _, _ = layer_backward(dy, inputs, kept, bounds, gains, weights)
-    summed = total_over_replicas(products(lefts, everyone(early), late, small))
+    summed = weight_sums(lefts, everyone(early), late, small)
     qkv, out, up, down = widen(summed)
     small = summed[272:RED_ROWS, :D].astype(jnp.float32)
     return (

time: 501 us -> 472 us (0.942)
  Pallas kernels: 457 us -> 427 us
    pallas_call x2 -> x1, Pallas kernels: 135 us -> 112 us  [weight_sums(): pl.pallas_call(weight_sums_kernel, out_shape=jax.ShapeDtypeStruct((RED_RO...]
    pallas_call x1, Pallas kernels: 67.9 us -> 61.5 us  [gather_weights(): pl.pallas_call(weights_kernel, out_shape=outs + [jax.ShapeDtypeStruct((NR...]
  transfers between devices with their start and end apart: 7 -> 7, of which waited for: 2 -> 2; matrix products, arithmetic and copies ran while one was open for 0% -> 0% of each run, Pallas kernels for 24% -> 25%
where the time goes in v3:
time: 472 us; the launch traced here: 463 us
  Pallas kernels  427 us (90%)
  waiting for transfers between devices  12.5 us (3%)
  starting transfers between devices  10.5 us (2%)
  local copies, waits for them, and re-layouts  6.63 us (1%)
  other arithmetic  5.26 us (1%)
    pallas_call x8, Pallas kernels, swap(): pl.pallas_call(swap_kernel, out_shape=jax.ShapeDtypeStruct(x.shape, x.dty...  128 us
    pallas_call x1, Pallas kernels, weight_sums(): pl.pallas_call(weight_sums_kernel, out_shape=jax.ShapeDtypeStruct((RED_RO...  112 us
    pallas_call x1, Pallas kernels, gather_weights(): pl.pallas_call(weights_kernel, out_shape=outs + [jax.ShapeDtypeStruct((NR...  61.5 us
    pallas_call x2, Pallas kernels, back_leave(): pl.pallas_call(back_leave_kernel, grid=(FF // LEAVE_BLOCK,), out_shape=[j...  31.4 us
    pallas_call x2, Pallas kernels, leave(): pl.pallas_call(leave_kernel, grid=(FF // LEAVE_BLOCK,), out_shape=[jax.Sh...  25.5 us
    pallas_call x2, Pallas kernels, attention_backward(): pl.pallas_call(backward_kernel, out_shape=[jax.ShapeDtypeStruct((NR, 5, T...  19.4 us
    pallas_call x2, Pallas kernels, back_enter(): pl.pallas_call(back_enter_kernel, grid=(steps,), out_shape=[jax.ShapeDtyp...  16.1 us
    pallas_call x2, Pallas kernels, attention_forward(): pl.pallas_call(forward_kernel, out_shape=[jax.ShapeDtypeStruct((NR, TQ, 2...  12.4 us
  transfers between devices with their start and end apart: 7, of which 2 were waited for; matrix products, arithmetic and copies ran while one was open for 0% of the time, Pallas kernels for 25%

profile of v3, /device:TPU:0, one launch (start us, length us, event | category | flops | bytes accessed | tf_op | source)
XLA Modules:
  0.0 462.9 jit_solution(4218740766405028166)
XLA Ops:
  3.5 61.5 %gather_weights.1 = (bf16[1088,3264]{1,0:T(8,128)(2,1)}, bf16[1088,1088]{1,0:T(8,128)(2,1)}, bf16[1088,4352]{1,0:T(8,128)(2,1)}, bf16[4352,1088]{1,0:T(8,128)(2,1)}, s32[16,8,128]{2,1,0:T(8,128)}) custom-call(bf16[272,3264]{1,0:T(8,128)(2,1)} %bitcast.50, bf16[272,1088]{1,0:T(8,128)(2,1)} %bitcast.58, bf16[272,4352]{1,0:T(8,128)(2,1)} %bitcast.49, ...), custom_call_target="tpu_custom_call" | custom-call | tf_op jit(solution)/shard_map/gather_weights/pallas_call | solution.py:265
  65.8 5.6 %enter.2 = (bf16[16,320,128]{2,1,0:T(8,128)(2,1)}, bf16[64,128]{1,0:T(8,128)(2,1)}, bf16[128,1088]{1,0:T(8,128)(2,1)}) custom-call(bf16[128,1088]{1,0:T(8,128)(2,1)} %bitcast.46, f32[2,1088]{1,0:T(2,128)} %bitcast.59, f32[6,1088]{1,0:T(8,128)} %bitcast.54, bf16[1088,3264]{1,0:T(8,128)(2,1)} %get-tuple-element.58.w), custom_call_target="tpu_custom_call" | custom-call | bytes 17500000 | tf_op jit(solution)/shard_map/enter/pallas_call | solution.py:496
  71.5 23.9 %swap.8 = bf16[16,320,128]{2,1,0:T(8,128)(2,1)} custom-call(bf16[16,320,128]{2,1,0:T(8,128)(2,1)} %get-tuple-element.59.x), custom_call_target="tpu_custom_call" | custom-call | bytes 56000000 | tf_op jit(solution)/shard_map/swap/pallas_call | solution.py:109
  95.9 6.2 %attention_forward.2 = (bf16[16,64,128]{2,1,0:T(8,128)(2,1)}, bf16[64,128]{1,0:T(8,128)(2,1)}, f32[1024,128]{1,0:T(8,128)}, f32[64,128]{1,0:T(8,128)}) custom-call(s32[4]{0:T(128)} %pad_add_fusion.1.bounds, bf16[16,5,64,128]{3,2,1,0:T(8,128)(2,1)} %bitcast.45, bf16[64,128]{1,0:T(8,128)(2,1)} %get-tuple-element.60.q16), custom_call_target="tpu_custom_call" | custom-call | bytes 17500000 | tf_op jit(solution)/shard_map/attention_forward/pallas_call | solution.py:348
  102.1 10.4 %swap.9.o = bf16[16,64,128]{2,1,0:T(8,128)(2,1)} custom-call(bf16[16,64,128]{2,1,0:T(8,128)(2,1)} %get-tuple-element.61.x), custom_call_target="tpu_custom_call" | custom-call | bytes 31500000 | tf_op jit(solution)/shard_map/swap/pallas_call | solution.py:109
  112.6 12.8 %leave.2 = (bf16[128,1088]{1,0:T(8,128)(2,1)}, f32[128,1088]{1,0:T(8,128)}, f32[128,4352]{1,0:T(8,128)}, bf16[4,128,2304]{2,1,0:T(8,128)(2,1)}) custom-call(bf16[128,1088]{1,0:T(8,128)(2,1)} %bitcast.47, bf16[16,64,128]{2,1,0:T(8,128)(2,1)} %swap.9.o, bf16[64,128]{1,0:T(8,128)(2,1)} %get-tuple-element.62.o16, bf16[128,1088]{1,0:T(8,128)(2,1)} %get-tuple-element.63.act1, ...), custom_call_target="tpu_custom_call" | custom-call | bytes 42000000 | tf_op jit(solution)/shard_map/leave/pallas_call | solution.py:559
  133.5 5.6 %enter.3 = (bf16[16,320,128]{2,1,0:T(8,128)(2,1)}, bf16[64,128]{1,0:T(8,128)(2,1)}, bf16[128,1088]{1,0:T(8,128)(2,1)}) custom-call(bf16[128,1088]{1,0:T(8,128)(2,1)} %broadcast_select_fusion.1.x, f32[2,1088]{1,0:T(2,128)} %bitcast.61, f32[6,1088]{1,0:T(8,128)} %bitcast.56, bf16[1088,3264]{1,0:T(8,128)(2,1)} %get-tuple-element.58.w), custom_call_target="tpu_custom_call" | custom-call | bytes 17500000 | tf_op jit(solution)/shard_map/enter/pallas_call | solution.py:496
  139.1 18.7 %swap.10 = bf16[16,320,128]{2,1,0:T(8,128)(2,1)} custom-call(bf16[16,320,128]{2,1,0:T(8,128)(2,1)} %get-tuple-element.68.x), custom_call_target="tpu_custom_call" | custom-call | bytes 56000000 | tf_op jit(solution)/shard_map/swap/pallas_call | solution.py:109
  157.8 6.2 %attention_forward.3 = (bf16[16,64,128]{2,1,0:T(8,128)(2,1)}, bf16[64,128]{1,0:T(8,128)(2,1)}, f32[1024,128]{1,0:T(8,128)}, f32[64,128]{1,0:T(8,128)}) custom-call(s32[4]{0:T(128)} %pad_add_fusion.1.bounds, bf16[16,5,64,128]{3,2,1,0:T(8,128)(2,1)} %bitcast.42, bf16[64,128]{1,0:T(8,128)(2,1)} %get-tuple-element.69.q16), custom_call_target="tpu_custom_call" | custom-call | bytes 17500000 | tf_op jit(solution)/shard_map/attention_forward/pallas_call | solution.py:348
  164.0 9.8 %swap.11.o = bf16[16,64,128]{2,1,0:T(8,128)(2,1)} custom-call(bf16[16,64,128]{2,1,0:T(8,128)(2,1)} %get-tuple-element.70.x), custom_call_target="tpu_custom_call" | custom-call | bytes 31500000 | tf_op jit(solution)/shard_map/swap/pallas_call | solution.py:109
  173.9 12.7 %leave.3 = (bf16[128,1088]{1,0:T(8,128)(2,1)}, f32[128,1088]{1,0:T(8,128)}, f32[128,4352]{1,0:T(8,128)}, bf16[4,128,2304]{2,1,0:T(8,128)(2,1)}) custom-call(bf16[128,1088]{1,0:T(8,128)(2,1)} %broadcast_select_fusion.1.x, bf16[16,64,128]{2,1,0:T(8,128)(2,1)} %swap.11.o, bf16[64,128]{1,0:T(8,128)(2,1)} %get-tuple-element.71.o16, ...), custom_call_target="tpu_custom_call" | custom-call | bytes 42000000 | tf_op jit(solution)/shard_map/leave/pallas_call | solution.py:559
  191.8 15.7 %back_leave.2 = (bf16[128,6656]{1,0:T(8,128)(2,1)}, f32[128,1088]{1,0:T(8,128)}, bf16[16,64,128]{2,1,0:T(8,128)(2,1)}, bf16[64,128]{1,0:T(8,128)(2,1)}, f32[8,1152]{1,0:T(8,128)}) custom-call(bf16[128,1088]{1,0:T(8,128)(2,1)} %bitcast.53, f32[128,1088]{1,0:T(8,128)} %get-tuple-element.76.resid, f32[128,4352]{1,0:T(8,128)} %get-tuple-element.77.pre, ...), custom_call_target="tpu_custom_call" | custom-call | bytes 49000000 | tf_op jit(solution)/shard_map/back_leave/pallas_call | solution.py:650
  207.5 10.2 %swap.12.do = bf16[16,64,128]{2,1,0:T(8,128)(2,1)} custom-call(bf16[16,64,128]{2,1,0:T(8,128)(2,1)} %get-tuple-element.78.x), custom_call_target="tpu_custom_call" | custom-call | bytes 31500000 | tf_op jit(solution)/shard_map/swap/pallas_call | solution.py:109
  217.7 9.7 %attention_backward.2 = (bf16[16,5,64,128]{3,2,1,0:T(8,128)(2,1)}, bf16[64,128]{1,0:T(8,128)(2,1)}) custom-call(s32[4]{0:T(128)} %pad_add_fusion.1.bounds, bf16[16,5,64,128]{3,2,1,0:T(8,128)(2,1)} %bitcast.43, bf16[64,128]{1,0:T(8,128)(2,1)} %get-tuple-element.69.q16, f32[1024,128]{1,0:T(8,128)} %get-tuple-element.74.lse, ...), custom_call_target="tpu_custom_call" | custom-call | bytes 28000000 | tf_op jit(solution)/shard_map/attention_backward/pallas_call | solution.py:413
  227.4 22.6 %swap.13.back = bf16[16,320,128]{2,1,0:T(8,128)(2,1)} custom-call(bf16[16,320,128]{2,1,0:T(8,128)(2,1)} %bitcast.51), custom_call_target="tpu_custom_call" | custom-call | bytes 56000000 | tf_op jit(solution)/shard_map/swap/pallas_call | solution.py:109
  250.1 8.0 %back_enter.2 = (bf16[128,3328]{1,0:T(8,128)(2,1)}, bf16[128,1088]{1,0:T(8,128)(2,1)}, f32[16,1152]{1,0:T(8,128)}) custom-call(bf16[128,1088]{1,0:T(8,128)(2,1)} %broadcast_select_fusion.1.x, bf16[16,320,128]{2,1,0:T(8,128)(2,1)} %swap.13.back, bf16[64,128]{1,0:T(8,128)(2,1)} %get-tuple-element.83.dq16, f32[128,1088]{1,0:T(8,128)} %get-tuple-element.84.grad_resid, ...), custom_call_target="tpu_custom_call" | custom-call | bytes 17500000 | tf_op jit(solution)/shard_map/back_enter/pallas_call | solution.py:716
  259.4 8.1 %collective-permute-done.4 = bf16[128,1088]{1,0:T(8,128)(2,1)S(1)} collective-permute-done((bf16[128,1088]{1,0:T(8,128)(2,1)}, bf16[128,1088]{1,0:T(8,128)(2,1)S(1)}, u32[]{:S(2)}, u32[]{:S(2)}) %collective-permute-start.4) | collective-permute-done | bytes 278560 | tf_op jit(solution)/shard_map/ppermute | solution.py:1074
  268.3 15.7 %back_leave.3 = (bf16[128,6656]{1,0:T(8,128)(2,1)}, f32[128,1088]{1,0:T(8,128)}, bf16[16,64,128]{2,1,0:T(8,128)(2,1)}, bf16[64,128]{1,0:T(8,128)(2,1)}, f32[8,1152]{1,0:T(8,128)}) custom-call(bf16[128,1088]{1,0:T(8,128)(2,1)} %broadcast_select_fusion.dy, f32[128,1088]{1,0:T(8,128)} %get-tuple-element.76.resid, f32[128,4352]{1,0:T(8,128)} %get-tuple-element.77.pre, ...), custom_call_target="tpu_custom_call" | custom-call | bytes 49000000 | tf_op jit(solution)/shard_map/back_leave/pallas_call | solution.py:650
  286.6 10.4 %swap.14.do = bf16[16,64,128]{2,1,0:T(8,128)(2,1)} custom-call(bf16[16,64,128]{2,1,0:T(8,128)(2,1)} %get-tuple-element.88.x), custom_call_target="tpu_custom_call" | custom-call | bytes 31500000 | tf_op jit(solution)/shard_map/swap/pallas_call | solution.py:109
  297.0 9.7 %attention_backward.3 = (bf16[16,5,64,128]{3,2,1,0:T(8,128)(2,1)}, bf16[64,128]{1,0:T(8,128)(2,1)}) custom-call(s32[4]{0:T(128)} %pad_add_fusion.1.bounds, bf16[16,5,64,128]{3,2,1,0:T(8,128)(2,1)} %bitcast.44, bf16[64,128]{1,0:T(8,128)(2,1)} %get-tuple-element.69.q16, f32[1024,128]{1,0:T(8,128)} %get-tuple-element.74.lse, ...), custom_call_target="tpu_custom_call" | custom-call | bytes 28000000 | tf_op jit(solution)/shard_map/attention_backward/pallas_call | solution.py:413
  306.7 22.0 %swap.15.back = bf16[16,320,128]{2,1,0:T(8,128)(2,1)} custom-call(bf16[16,320,128]{2,1,0:T(8,128)(2,1)} %bitcast.52), custom_call_target="tpu_custom_call" | custom-call | bytes 56000000 | tf_op jit(solution)/shard_map/swap/pallas_call | solution.py:109
  328.7 8.1 %back_enter.3 = (bf16[128,3328]{1,0:T(8,128)(2,1)}, bf16[128,1088]{1,0:T(8,128)(2,1)}, f32[16,1152]{1,0:T(8,128)}) custom-call(bf16[128,1088]{1,0:T(8,128)(2,1)} %broadcast_select_fusion.1.x, bf16[16,320,128]{2,1,0:T(8,128)(2,1)} %swap.15.back, bf16[64,128]{1,0:T(8,128)(2,1)} %get-tuple-element.91.dq16, f32[128,1088]{1,0:T(8,128)} %get-tuple-element.92.grad_resid, ...), custom_call_target="tpu_custom_call" | custom-call | bytes 17500000 | tf_op jit(solution)/shard_map/back_enter/pallas_call | solution.py:716
  338.5 111.9 %weight_sums.1.g = bf16[288,14336]{1,0:T(8,128)(2,1)} custom-call(bf16[4,128,2304]{2,1,0:T(8,128)(2,1)} %get-tuple-element.81.l0, bf16[128,2304]{1,0:T(8,128)(2,1)} %copy-done.5, bf16[128,2304]{1,0:T(8,128)(2,1)} %copy-done.4, bf16[128,2304]{1,0:T(8,128)(2,1)} %copy-done.6, bf16[128,6656]{1,0:T(8,128)(2,1)} %get-tuple-element.98.e0, ...), custom_call_target="tpu_custom_call" | custom-call | tf_op jit(solution)/shard_map/weight_sums/pallas_call | solution.py:943
  451.2 9.2 %widen.1 = (f32[272,3264]{1,0:T(8,128)}, f32[272,1088]{1,0:T(8,128)}, f32[272,4352]{1,0:T(8,128)}, f32[4,272,1088]{2,1,0:T(8,128)}) custom-call(bf16[288,14336]{1,0:T(8,128)(2,1)} %weight_sums.1.g), custom_call_target="tpu_custom_call" | custom-call | tf_op jit(solution)/shard_map/widen/pallas_call | solution.py:988
  (45 shorter events, 26.7 us)
Async XLA Ops:
  112.5 20.2 %copy-start = (bf16[2,1,64,1088]{3,2,1,0:T(8,128)(2,1)S(1)}, bf16[2,1,64,1088]{3,2,1,0:T(8,128)(2,1)}, u32[]{:S(2)}) copy-start(bf16[2,1,64,1088]{3,2,1,0:T(8,128)(2,1)} %param.10) | copy-start | bytes 835588
  125.3 7.4 %collective-permute-start = (bf16[128,1088]{1,0:T(8,128)(2,1)}, bf16[128,1088]{1,0:T(8,128)(2,1)S(1)}, u32[]{:S(2)}, u32[]{:S(2)}) collective-permute-start(bf16[128,1088]{1,0:T(8,128)(2,1)} %get-tuple-element.67), channel_id=1, source_target_pairs={{0,64},{1,65},{2,66},{3,67},{4,68},{5,69},{6,70},{7,71},{8,72},{9,... | collective-permute-start | bytes 835592 | tf_op jit(solution)/shard_map/ppermute | solution.py:1066
  188.2 39.3 %collective-permute-start.2 = (bf16[128,2304]{1,0:T(8,128)(2,1)S(1)}, bf16[128,2304]{1,0:T(8,128)(2,1)S(1)}, u32[]{:S(2)}, u32[]{:S(2)}) collective-permute-start(bf16[128,2304]{1,0:T(8,128)(2,1)S(1)} %get-tuple-element.117), channel_id=1, source_target_pairs={{0,16},{16,0},{32,48},{48,32},{1,17},{17,1},{33,49},{49,33},{2,18}... | collective-permute-start | bytes 1769480 | tf_op jit(solution)/shard_map/ppermute | solution.py:1049
  188.2 39.2 %collective-permute-start.1 = (bf16[128,2304]{1,0:T(8,128)(2,1)S(1)}, bf16[128,2304]{1,0:T(8,128)(2,1)S(1)}, u32[]{:S(2)}, u32[]{:S(2)}) collective-permute-start(bf16[128,2304]{1,0:T(8,128)(2,1)S(1)} %get-tuple-element.118), channel_id=1, source_target_pairs={{0,32},{16,48},{32,0},{48,16},{1,33},{17,49},{33,1},{49,17},{2,34}... | collective-permute-start | bytes 1769480 | tf_op jit(solution)/shard_map/ppermute | solution.py:1048
  190.7 67.4 %collective-permute-start.3 = (bf16[128,2304]{1,0:T(8,128)(2,1)S(1)}, bf16[128,2304]{1,0:T(8,128)(2,1)S(1)}, u32[]{:S(2)}, u32[]{:S(2)}) collective-permute-start(bf16[128,2304]{1,0:T(8,128)(2,1)S(1)} %get-tuple-element.116), channel_id=1, source_target_pairs={{0,48},{16,32},{32,16},{48,0},{1,49},{17,33},{33,17},{49,1},{2,50}... | collective-permute-start | bytes 1769480 | tf_op jit(solution)/shard_map/ppermute | solution.py:1050
  227.4 30.6 %copy-start.4 = (bf16[128,2304]{1,0:T(8,128)(2,1)}, bf16[128,2304]{1,0:T(8,128)(2,1)S(1)}, u32[]{:S(2)}) copy-start(bf16[128,2304]{1,0:T(8,128)(2,1)S(1)} %collective-permute-done.2.l2) | copy-start | bytes 1769476
  227.4 30.6 %copy-start.5 = (bf16[128,2304]{1,0:T(8,128)(2,1)}, bf16[128,2304]{1,0:T(8,128)(2,1)S(1)}, u32[]{:S(2)}) copy-start(bf16[128,2304]{1,0:T(8,128)(2,1)S(1)} %collective-permute-done.1.l1) | copy-start | bytes 1769476
  250.1 17.5 %copy-start.3 = (bf16[2,1,64,1088]{3,2,1,0:T(8,128)(2,1)S(1)}, bf16[2,1,64,1088]{3,2,1,0:T(8,128)(2,1)}, u32[]{:S(2)}) copy-start(bf16[2,1,64,1088]{3,2,1,0:T(8,128)(2,1)} %param.11) | copy-start | bytes 835588
  258.1 25.9 %copy-start.6 = (bf16[128,2304]{1,0:T(8,128)(2,1)}, bf16[128,2304]{1,0:T(8,128)(2,1)S(1)}, u32[]{:S(2)}) copy-start(bf16[128,2304]{1,0:T(8,128)(2,1)S(1)} %collective-permute-done.3.l3) | copy-start | bytes 1769476
  258.1 9.4 %collective-permute-start.4 = (bf16[128,1088]{1,0:T(8,128)(2,1)}, bf16[128,1088]{1,0:T(8,128)(2,1)S(1)}, u32[]{:S(2)}, u32[]{:S(2)}) collective-permute-start(bf16[128,1088]{1,0:T(8,128)(2,1)} %get-tuple-element.87), channel_id=1, source_target_pairs={{64,0},{65,1},{66,2},{67,3},{68,4},{69,5},{70,6},{71,7},{72,8},{73... | collective-permute-start | bytes 835592 | tf_op jit(solution)/shard_map/ppermute | solution.py:1074
  284.0 52.7 %collective-permute-start.6 = (bf16[128,6656]{1,0:T(8,128)(2,1)}, bf16[128,6656]{1,0:T(8,128)(2,1)S(1)}, u32[]{:S(2)}, u32[]{:S(2)}) collective-permute-start(bf16[128,6656]{1,0:T(8,128)(2,1)} %get-tuple-element.98.e0), channel_id=1, source_target_pairs={{0,16},{16,0},{32,48},{48,32},{1,17},{17,1},{33,49},{49,33},{2,18}... | collective-permute-start | bytes 5111816 | tf_op jit(solution)/shard_map/ppermute | solution.py:1036
  284.1 52.6 %collective-permute-start.5 = (bf16[128,6656]{1,0:T(8,128)(2,1)}, bf16[128,6656]{1,0:T(8,128)(2,1)S(1)}, u32[]{:S(2)}, u32[]{:S(2)}) collective-permute-start(bf16[128,6656]{1,0:T(8,128)(2,1)} %get-tuple-element.98.e0), channel_id=1, source_target_pairs={{0,32},{16,48},{32,0},{48,16},{1,33},{17,49},{33,1},{49,17},{2,34}... | collective-permute-start | bytes 5111816 | tf_op jit(solution)/shard_map/ppermute | solution.py:1036
  336.8 1.2 copy-start.1
  336.8 1.7 copy-start.2
